TPU v7x, 32 devices: a whole 2x2x4 slice. The times are simulated.
32 devices in a mesh: groups: 2 (over y), seq: 4 (over z), mp: 2 (over x), rep: 2 (over core).
Axes of the slice: x: 2, y: 2, z: 4, core: 2. Of those that a mesh axis runs over, the one named last changes fastest.
Arguments:
- byte_states: bfloat16 [4096, 1024], P(('groups', 'seq', 'mp', 'rep')), parts along dimension 0, may hold values from -6 to 6
- cotangent: bfloat16 [4096, 1024], P(('groups', 'seq', 'mp', 'rep')), parts along dimension 0, may hold values from -6 to 6
- boundaries: int32 [1024], P('groups'), parts along dimension 0, may hold values from 0 to 2047, as said below
- enc_gain: float32 [1024], replicated, may hold values from 0.25 to 1.75
- w_qkv: bfloat16 [1024, 3072], replicated, may hold values from -1 to 1
- w_out: bfloat16 [1024, 1024], replicated, may hold values from -0.1875 to 0.1875
- pad_vector: float32 [3072], replicated, may hold values from -5 to 5
- main_gain: float32 [4096], replicated, may hold values from 0.25 to 1.75
- gate_w: bfloat16 [4096, 6144], P('seq', ('mp', 'rep')), may hold values from -0.09375 to 0.09375
- up_w: bfloat16 [4096, 6144], P('seq', ('mp', 'rep')), may hold values from -0.09375 to 0.09375
- down_t: bfloat16 [4096, 6144], P('seq', ('mp', 'rep')), may hold values from -0.078125 to 0.078125
Outputs:
- main_out: bfloat16 [1024, 4096], P(('groups', 'seq', 'mp', 'rep')), parts along dimension 0
- span_grad: bfloat16 [1024, 1024], P(('groups', 'seq', 'mp', 'rep')), parts along dimension 0
There are 2 independent parts, one for each index of `groups`. A program takes and returns all parts, laid end to end along the dimension named above; an argument that names none is the same for every part. Nothing has to cross between parts.
Inputs may be any that keep to these rules, and one draw needn't show every extreme that they name: `boundaries`: Sorted, strictly increasing, the first is 0. Every aligned block of 128 bytes holds 1 to 63 span starts, and some block holds exactly 63. The bytes of a seq index are the 4 consecutive blocks that its devices hold. The spans of the owner at seq index s (spans s * 128 to (s + 1) * 128 - 1) start only in the bytes of seq indices s - 1, s and s + 1, at most 23 of them in those of s - 1 and at most 23 in those of s + 1; in every draw some owner has exactly 23 starting in those of s - 1, and some owner exactly 23 in those of s + 1.
All inputs are finite; a program needn't handle non-finite values.
Results may differ from a plain program's by a relative error of at most 0.009.
Values may be sent and summed in bfloat16 or wider, within the bound.
No kernel may reach another device: no remote copies, remote signals or barrier semaphores. Data moves between devices by JAX's collectives and lax.ppermute only.
A program may use at most 128 MiB of HBM per device.

v0:
```python
import jax
import jax.numpy as jnp
from jax import lax
from jax.sharding import PartitionSpec as P

HEAD = 128
WINDOW = 128
SPAN_DEV = 32
CAP = 64
LANE = 24


def from_behind(value, axis, by):
    length = lax.axis_size(axis)
    pairs = [(i, i + by) for i in range(length) if 0 <= i + by < length]
    return lax.ppermute(value, axis, pairs)


def with_halo(value, sides, width):
    for axis, dim in sides:
        size, length = (lax.axis_size(axis), value.shape[dim])
        up = [(i, (i + 1) % size) for i in range(size - 1)]
        down = [(j, i) for i, j in up]
        last = lax.slice_in_dim(value, length - width, length, axis=dim)
        first = lax.slice_in_dim(value, 0, width, axis=dim)
        before = lax.ppermute(last, axis, up)
        after = lax.ppermute(first, axis, down)
        value = jnp.concatenate([before, value, after], axis=dim)
    return value


def rms_scale(values, gain):
    return values * lax.rsqrt(jnp.mean(values * values, axis=-1, keepdims=True) + 1e-05) * gain


def local(
    byte_states,
    cotangent,
    boundaries,
    enc_gain,
    w_qkv,
    w_out,
    pad_vector,
    main_gain,
    gate_w,
    up_w,
    down_t,
):
    n_member = lax.axis_size(("mp", "rep"))
    device = lax.axis_index(("seq", "mp", "rep"))
    owner_index = lax.axis_index("seq")
    member = lax.axis_index(("mp", "rep"))
    length = byte_states.shape[0]
    width = byte_states.shape[1]
    main_width = pad_vector.shape[0] + width
    head_count = width // HEAD
    begin = device * length
    x_float = byte_states.astype(jnp.float32)
    normed = rms_scale(x_float, enc_gain).astype(jnp.bfloat16)
    qkv = jnp.dot(normed, w_qkv, preferred_element_type=jnp.float32).astype(jnp.bfloat16)
    queries = qkv[:, :width]
    keyval = qkv[:, width:]
    rim_kv = from_behind(keyval, ("seq", "mp", "rep"), 1)
    all_kv = jnp.concatenate([rim_kv, keyval], axis=0)
    qpos = begin + jnp.arange(length, dtype=jnp.int32)
    kpos = begin - WINDOW + jnp.arange(WINDOW + length, dtype=jnp.int32)
    allowed = (
        (kpos[None, :] <= qpos[:, None])
        & (kpos[None, :] > qpos[:, None] - WINDOW)
        & (kpos[None, :] >= 0)
    )
    q_heads = queries.reshape(length, head_count, HEAD)
    k_heads = all_kv[:, :width].reshape(WINDOW + length, head_count, HEAD)
    v_heads = all_kv[:, width:].reshape(WINDOW + length, head_count, HEAD)
    scores = jnp.einsum(
        "qhd,khd->hqk", q_heads, k_heads, preferred_element_type=jnp.float32
    ) / jnp.sqrt(jnp.float32(HEAD))
    scores = jnp.where(allowed[None], scores, jnp.float32(-1e30))
    probs = jax.nn.softmax(scores, axis=-1).astype(jnp.bfloat16)
    mixed = jnp.einsum("hqk,khd->qhd", probs, v_heads, preferred_element_type=jnp.float32)
    attended = mixed.reshape(length, width).astype(jnp.bfloat16)
    encoded = (x_float + jnp.dot(attended, w_out, preferred_element_type=jnp.float32)).astype(
        jnp.bfloat16
    )
    span_own = SPAN_DEV * n_member
    right_side = jnp.searchsorted(boundaries, qpos, side="right")
    left_side = jnp.searchsorted(boundaries, qpos, side="left")
    span_index = right_side - 1
    starts_here = (right_side - left_side).astype(jnp.bfloat16)
    lowest = span_index[0]
    highest = span_index[length - 1]
    slot_ids = jnp.arange(CAP, dtype=jnp.int32)
    onehot = (span_index[None, :] - lowest == slot_ids[:, None]).astype(jnp.bfloat16)
    grad_piece = jnp.dot(onehot, cotangent, preferred_element_type=jnp.float32).astype(jnp.bfloat16)
    enc_piece = jnp.dot(
        onehot * starts_here[None, :], encoded, preferred_element_type=jnp.float32
    ).astype(jnp.bfloat16)
    pieces = jnp.concatenate([enc_piece, grad_piece], axis=1)
    span_ids = lowest + slot_ids
    valid = span_ids <= highest
    row_ids = jnp.arange(span_own, dtype=jnp.int32)
    lane_ids = jnp.arange(LANE, dtype=jnp.int32)
    lane_targets = jnp.concatenate(
        [owner_index * span_own - LANE + lane_ids, (owner_index + 1) * span_own + lane_ids]
    )
    choosing = ((lane_targets[:, None] == span_ids[None, :]) & valid[None, :]).astype(jnp.bfloat16)
    lanes = jnp.dot(choosing, pieces, preferred_element_type=jnp.float32).astype(jnp.bfloat16)
    bordered = with_halo(lanes, (("seq", 0),), LANE)
    own_rows = span_ids - owner_index * span_own
    keeping = ((row_ids[:, None] == own_rows[None, :]) & valid[None, :]).astype(jnp.bfloat16)
    block = jnp.dot(keeping, pieces, preferred_element_type=jnp.float32)
    block = block.at[:LANE].add(bordered[:LANE].astype(jnp.float32))
    block = block.at[span_own - LANE :].add(bordered[3 * LANE :].astype(jnp.float32))
    owner_block = lax.psum(block.astype(jnp.bfloat16), ("mp", "rep")).astype(jnp.float32)
    share = span_own // n_member
    span_grad = lax.dynamic_slice_in_dim(owner_block[:, width:], member * share, share, 0).astype(
        jnp.bfloat16
    )
    wide = jnp.concatenate(
        [owner_block[:, :width], jnp.broadcast_to(pad_vector, (span_own, main_width - width))],
        axis=1,
    )
    main_in = rms_scale(wide, main_gain).astype(jnp.bfloat16)
    gate_full, up_full, down_full = (
        lax.all_gather(gate_w, "seq", axis=0, tiled=True),
        lax.all_gather(up_w, "seq", axis=0, tiled=True),
        lax.all_gather(down_t, "seq", axis=0, tiled=True),
    )
    gate = jnp.dot(main_in, gate_full, preferred_element_type=jnp.float32)
    upward = jnp.dot(main_in, up_full, preferred_element_type=jnp.float32)
    hidden = (jax.nn.silu(gate) * upward).astype(jnp.bfloat16)
    partial_out = lax.dot_general(
        hidden, down_full, (((1,), (1,)), ((), ())), preferred_element_type=jnp.float32
    )
    totals = lax.psum(partial_out.astype(jnp.bfloat16), ("mp", "rep")).astype(jnp.float32)
    summed = lax.dynamic_slice_in_dim(totals, member * share, share, 0)
    residual = lax.dynamic_slice_in_dim(wide, member * share, share, 0)
    main_out = (residual + summed).astype(jnp.bfloat16)
    return (main_out, span_grad)


def solution(mesh):
    placed = (
        P(("groups", "seq", "mp", "rep"), None),
        P(("groups", "seq", "mp", "rep"), None),
        P("groups"),
        P(),
        P(),
        P(),
        P(),
        P(),
        P("seq", ("mp", "rep")),
        P("seq", ("mp", "rep")),
        P("seq", ("mp", "rep")),
    )
    return jax.shard_map(
        local,
        mesh=mesh,
        in_specs=placed,
        out_specs=(
            P(("groups", "seq", "mp", "rep"), None),
            P(("groups", "seq", "mp", "rep"), None),
        ),
        check_vma=False,
    )
```

profile of v0, /device:TPU:0, one launch (start us, length us, event | category | flops | bytes accessed | tf_op | source)
XLA Modules:
  0.0 787.1 jit_solution(869668647306406422)
XLA Ops:
  9.3 4.0 convolution_convert_fusion.1
  13.3 3.2 collective-permute-start
  16.5 13.4 %while.50 = (s32[]{:T(128)}, u32[128]{0:T(128)S(1)}, u32[128]{0:T(128)S(1)}, s32[512]{0:T(512)S(1)}, s32[]{:T(128)}, /*index=5*/s32[]{:T(128)}, s32[]{:T(128)}, s32[]{}) while((s32[]{:T(128)}, u32[128]{0:T(128)S(1)}, u32[128]{0:T(128)S(1)}, s32[512]{0:T(512)S(1)}, s32[]{:T(128)}, /*index=5*/s32[]{:T(128)}, s32[]{:T(128)}, s32[]{}) %tuple.95), condition=%wide.region_1.2_spmd.clone, body=%wide.region_0.0_spmd.clone.sunk | while | flops 2820 | bytes 10352 | solution.py:86
  16.6 1.3 gather_fusion
  17.9 1.3 gather_fusion
  20.6 1.3 gather_fusion
  21.9 1.3 gather_fusion
  23.3 1.3 gather_fusion
  25.9 1.3 gather_fusion
  27.3 1.3 gather_fusion
  28.6 1.3 gather_fusion
  30.5 13.3 %while.51 = (s32[]{:T(128)}, u32[128]{0:T(128)S(1)}, u32[128]{0:T(128)S(1)}, s32[512]{0:T(512)S(1)}, s32[]{:T(128)}, /*index=5*/s32[]{:T(128)}, s32[]{:T(128)}, s32[]{}) while((s32[]{:T(128)}, u32[128]{0:T(128)S(1)}, u32[128]{0:T(128)S(1)}, s32[512]{0:T(512)S(1)}, s32[]{:T(128)}, /*index=5*/s32[]{:T(128)}, s32[]{:T(128)}, s32[]{}) %tuple.96), condition=%wide.region_3.4_spmd.clone, body=%wide.region_2.3_spmd.clone.sunk | while | flops 2820 | bytes 10352 | solution.py:87
  30.5 1.3 gather_fusion.1
  31.9 1.3 gather_fusion.1
  33.2 1.3 gather_fusion.1
  34.5 1.3 gather_fusion.1
  49.1 2.1 fusion.23
  51.2 1.3 fusion.12
  52.5 2.0 fusion.66
  55.7 3.5 convolution_convert_fusion.3
  60.2 3.7 collective-permute-start.1
  64.2 1.3 collective-permute-start.2
  66.6 5.0 collective-permute-done.2
  74.3 31.1 %all-reduce.3.cloned.1.call-done = bf16[128,2048]{1,0:T(8,128)(2,1)} async-done(((bf16[128,2048]{1,0:T(8,128)(2,1)}), bf16[128,2048]{1,0:T(8,128)(2,1)}) %all-reduce.3.cloned.1.call-update) | async-done | bytes 524304 | tf_op jit(solution)/shard_map/psum | solution.py:114
  106.5 1.6 multiply_reduce_fusion
  108.0 184.1 %all-gather.4.cloned.1.call-done = bf16[4096,1536]{1,0:T(8,128)(2,1)} async-done(((bf16[1024,1536]{1,0:T(8,128)(2,1)}), bf16[4096,1536]{1,0:T(8,128)(2,1)}) %all-gather.4.cloned.1.call-update) | async-done | bytes 12582928 | tf_op jit(solution)/shard_map/all_gather | solution.py:125
  292.2 7.3 fusion.26
  299.5 210.4 %all-gather.6.cloned.1.call-done = bf16[4096,1536]{1,0:T(8,128)(2,1)} async-done(((bf16[1024,1536]{1,0:T(8,128)(2,1)}), bf16[4096,1536]{1,0:T(8,128)(2,1)}) %all-gather.6.cloned.1.call-update) | async-done | bytes 12582928 | tf_op jit(solution)/shard_map/all_gather | solution.py:126
  509.9 217.7 %all-gather.8.cloned.1.call-done = bf16[4096,1536]{1,0:T(8,128)(2,1)} async-done(((bf16[1024,1536]{1,0:T(8,128)(2,1)}), bf16[4096,1536]{1,0:T(8,128)(2,1)}) %all-gather.8.cloned.1.call-update) | async-done | bytes 12582928 | tf_op jit(solution)/shard_map/all_gather | solution.py:127
  727.6 15.6 %convolution_convert_fusion = bf16[128,4096]{1,0:T(8,128)(2,1)} fusion(bf16[4096,1536]{1,0:T(8,128)(2,1)} %all-gather.8.cloned.1.call-done, bf16[4096,1536]{1,0:T(8,128)(2,1)} %all-gather.6.cloned.1.call-done, f32[128,1536]{1,0:T(8,128)} %fusion.26, f32[128,1024]{1,0:T(8,128)S(1)} %slice.92, f32[4096]{0:T(1024)S(1)} %pad.5.clone, f32[4096]{0:T(1024)S(1)} %copy-done.9, ...), kind=kOutput, calls=%fused_computation.19 | convolution fusion | flops 3225026560 | bytes 27558400 | tf_op jit(solution)/shard_map/dot_general | solution.py:132
  743.9 33.7 %all-reduce.5.cloned.1.call-done = bf16[128,4096]{1,0:T(8,128)(2,1)} async-done(((bf16[128,4096]{1,0:T(8,128)(2,1)}), bf16[128,4096]{1,0:T(8,128)(2,1)}) %all-reduce.5.cloned.1.call-update) | async-done | bytes 1048592 | tf_op jit(solution)/shard_map/psum | solution.py:135
  777.6 1.9 add_convert_fusion
  (134 shorter events, 25.7 us)
Async XLA Ops:
  8.0 51.3 %copy-start = (bf16[1024,1024]{1,0:T(8,128)(2,1)S(1)}, bf16[1024,1024]{1,0:T(8,128)(2,1)}, u32[]{:S(2)}) copy-start(bf16[1024,1024]{1,0:T(8,128)(2,1)} %param.24) | copy-start | bytes 6291460
  8.0 97.5 %all-reduce.3.cloned.1.call-start = ((), (), s32[]{:S(2)}) async-start(), calls=%async_computation | async-start | bytes 1048576 | tf_op jit(solution)/shard_map/psum | solution.py:114
  9.3 7.2 copy-start.2
  13.3 17.2 %copy-start.4 = (bf16[128,2048]{1,0:T(8,128)(2,1)}, bf16[128,2048]{1,0:T(8,128)(2,1)S(1)}, u32[]{:S(2)}) copy-start(bf16[128,2048]{1,0:T(8,128)(2,1)S(1)} %slice.84) | copy-start | bytes 1572868
  13.3 35.8 %collective-permute-start = (bf16[128,2048]{1,0:T(8,128)(2,1)S(1)}, bf16[128,2048]{1,0:T(8,128)(2,1)}, u32[]{:S(2)}, u32[]{:S(2)}) collective-permute-start(bf16[128,2048]{1,0:T(8,128)(2,1)S(1)} %slice.84), channel_id=1, source_target_pairs={{0,1},{1,2},{2,3},{3,4},{4,5},{5,6},{6,7},{7,8},{8,9},{9,10},{10,1... | collective-permute-start | bytes 1572872 | tf_op jit(solution)/shard_map/ppermute | solution.py:16
  47.9 3.2 copy-start.5
  55.7 3.6 copy-start.3
  59.2 0.7 copy-start.7
  59.3 0.7 copy-start.8
  60.2 6.3 collective-permute-start.1
  64.2 7.3 collective-permute-start.2
  72.5 219.7 %all-gather.4.cloned.1.call-start = ((), (), s32[]{:S(2)}) async-start(), calls=%async_computation.1 | async-start | bytes 15728640 | tf_op jit(solution)/shard_map/all_gather | solution.py:125
  73.0 436.8 %all-gather.6.cloned.1.call-start = ((), (), s32[]{:S(2)}) async-start(), calls=%async_computation.2 | async-start | bytes 15728640 | tf_op jit(solution)/shard_map/all_gather | solution.py:126
  73.6 0.7 copy-start.6
  73.6 654.0 %all-gather.8.cloned.1.call-start = ((), (), s32[]{:S(2)}) async-start(), calls=%async_computation.3 | async-start | bytes 15728640 | tf_op jit(solution)/shard_map/all_gather | solution.py:127
  74.2 218.0 %copy-start.9 = (f32[4096]{0:T(1024)S(1)}, f32[4096]{0:T(1024)}, u32[]{:S(2)}) copy-start(f32[4096]{0:T(1024)} %param.26) | copy-start | bytes 49156
  74.2 703.4 %all-reduce.5.cloned.1.call-start = ((), (), s32[]{:S(2)}) async-start(), calls=%async_computation.4 | async-start | bytes 2097152 | tf_op jit(solution)/shard_map/psum | solution.py:135
  299.5 443.7 %slice-start = ((bf16[128,2048]{1,0:T(8,128)(2,1)}), bf16[128,1024]{1,0:T(8,128)(2,1)S(1)}, s32[]{:S(2)}) async-start(bf16[128,2048]{1,0:T(8,128)(2,1)} %all-reduce.3.cloned.1.call-done), calls=%async_computation.5 | async-start | bytes 524288 | tf_op jit(solution)/shard_map/slice | solution.py:116
  727.6 51.9 %copy-start.1 = (bf16[1024,1024]{1,0:T(8,128)(2,1)S(1)}, bf16[1024,1024]{1,0:T(8,128)(2,1)}, u32[]{:S(2)}) copy-start(bf16[1024,1024]{1,0:T(8,128)(2,1)} %param.24) | copy-start | bytes 6291460
Sparse Core Ops, SparseCore 0:
  72.6 32.8 all-reduce.2
  743.4 34.2 all-reduce.4
Sparse Core Ops, SparseCore 1:
  74.5 217.6 all-gather.3
  293.6 216.2 all-gather.5
  511.3 216.2 all-gather.7
where the time goes:
time: 788 us; the launch traced here: 787 us
  waiting for transfers between devices  685 us (87%)
  matrix products  36 us (5%)
  local copies, waits for them, and re-layouts  29 us (4%)
  between operations  16 us (2%)
  other arithmetic  12.3 us (2%)
  starting transfers between devices  8.39 us (1%)
    all_gather x1, waiting for transfers between devices, local(): lax.all_gather(down_t, 'seq', axis=0, tiled=True)  218 us
    all_gather x1, waiting for transfers between devices, local(): lax.all_gather(up_w, 'seq', axis=0, tiled=True)  210 us
    all_gather x1, waiting for transfers between devices, local(): lax.all_gather(gate_w, 'seq', axis=0, tiled=True)  184 us
    psum x1, waiting for transfers between devices, local(): lax.psum(partial_out.astype(jnp.bfloat16), ('mp', 'rep'))  33.7 us
    psum x1, waiting for transfers between devices, local(): lax.psum(block.astype(jnp.bfloat16), ('mp', 'rep')).astype(jnp.float32)  31.1 us
  transfers between devices with their start and end apart: 8, of which 7 were waited for; matrix products, arithmetic and copies ran while one was open for 5% of the time, Pallas kernels for 0%

commit v1 on v0

v1 whole, which is shorter than its diff:
```python
import jax
import jax.numpy as jnp
from jax import lax
from jax.sharding import PartitionSpec as P

HEAD = 128
WINDOW = 128
CAP = 64
LANE = 24
PART = ("seq", "mp", "rep")
MEMBER = ("mp", "rep")
F32 = jnp.float32
BF16 = jnp.bfloat16


def dot(a, b):
    return jnp.dot(a, b, preferred_element_type=F32)


def dot_t(a, b):
    return lax.dot_general(a, b, (((1,), (1,)), ((), ())), preferred_element_type=F32)


def rms_scale(values, gain):
    return values * lax.rsqrt(jnp.mean(values * values, axis=-1, keepdims=True) + 1e-05) * gain


def encode(x, halo, begin, sel, q_at, enc_gain, w_qkv, w_out):
    length, width = x.shape
    heads = width // HEAD
    both = jnp.concatenate([halo, x], axis=0)
    normed = rms_scale(both.astype(F32), enc_gain).astype(BF16)
    picked = dot(sel, normed[length:]).astype(BF16)
    queries = dot(picked, w_qkv[:, :width]).astype(BF16)
    keyval = dot(normed, w_qkv[:, width:]).astype(BF16)
    k_at = jnp.arange(2 * length, dtype=jnp.int32) - length
    allowed = (
        (k_at[None, :] <= q_at[:, None])
        & (k_at[None, :] > q_at[:, None] - WINDOW)
        & (k_at[None, :] + begin >= 0)
    )
    q_heads = queries.reshape(CAP, heads, HEAD)
    k_heads = keyval[:, :width].reshape(2 * length, heads, HEAD)
    v_heads = keyval[:, width:].reshape(2 * length, heads, HEAD)
    scores = jnp.einsum("qhd,khd->hqk", q_heads, k_heads, preferred_element_type=F32)
    scores = jnp.where(allowed[None], scores / jnp.sqrt(F32(HEAD)), F32(-1e30))
    probs = jax.nn.softmax(scores, axis=-1).astype(BF16)
    mixed = jnp.einsum("hqk,khd->qhd", probs, v_heads, preferred_element_type=F32)
    attended = mixed.reshape(CAP, width).astype(BF16)
    return (dot(sel, x) + dot(attended, w_out)).astype(BF16)


def sum_of_spans(cotangent, span_index):
    n_member = lax.axis_size(MEMBER)
    n_seq = lax.axis_size("seq")
    owner = lax.axis_index("seq")
    length, width = cotangent.shape
    span_own = 32 * n_member
    lowest, highest = span_index[0], span_index[length - 1]
    slot_ids = jnp.arange(CAP, dtype=jnp.int32)
    onehot = (span_index[None, :] - lowest == slot_ids[:, None]).astype(BF16)
    pieces = dot(onehot, cotangent).astype(BF16)
    span_ids = lowest + slot_ids
    valid = (span_ids <= highest)[None, :]
    lane_ids = jnp.arange(LANE, dtype=jnp.int32)
    row_ids = jnp.arange(span_own, dtype=jnp.int32)

    def choose(targets):
        return dot(((targets[:, None] == span_ids[None, :]) & valid).astype(BF16), pieces)

    to_before = choose(owner * span_own - LANE + lane_ids).astype(BF16)
    to_after = choose((owner + 1) * span_own + lane_ids).astype(BF16)
    up = [(i, i + 1) for i in range(n_seq - 1)]
    down = [(i + 1, i) for i in range(n_seq - 1)]
    from_before = lax.ppermute(to_after, "seq", up).astype(F32)
    from_after = lax.ppermute(to_before, "seq", down).astype(F32)
    block = choose(owner * span_own + row_ids)
    block = jnp.concatenate(
        [block[:LANE] + from_before, block[LANE:-LANE], block[-LANE:] + from_after], axis=0
    )
    sent = block.astype(BF16).reshape(n_member, span_own // n_member, width)
    got = lax.all_to_all(sent, MEMBER, 0, 0, tiled=True)
    return jnp.sum(got.astype(F32), axis=0).astype(BF16)


def split_high_low(values):
    high = values.astype(BF16)
    return high, (values - high.astype(F32)).astype(BF16)


def local(
    byte_states,
    cotangent,
    boundaries,
    enc_gain,
    w_qkv,
    w_out,
    pad_vector,
    main_gain,
    gate_w,
    up_w,
    down_t,
):
    n_member = lax.axis_size(MEMBER)
    n_seq = lax.axis_size("seq")
    n_dev = n_seq * n_member
    seq = lax.axis_index("seq")
    device = lax.axis_index(PART)
    length, width = byte_states.shape
    depth, columns = gate_w.shape
    main_width = depth * n_seq
    n_span = boundaries.shape[0]
    share = n_span // n_dev
    begin = device * length

    shift = [(i, i + 1) for i in range(n_dev - 1)]
    halo = lax.ppermute(byte_states, PART, shift)

    wide_gain = main_gain[width:]
    pad_in = jnp.concatenate([jnp.zeros((width,), F32), pad_vector * wide_gain])
    pad_here = lax.dynamic_slice_in_dim(pad_in, seq * depth, depth, 0)
    pad_rows = jnp.stack(split_high_low(pad_here) * 4)
    pad_terms = jnp.concatenate([dot(pad_rows, gate_w), dot(pad_rows, up_w)], axis=1)
    pad_terms = pad_terms[:1] + pad_terms[1:2]

    places = jnp.arange(length, dtype=jnp.int32)
    earlier = jnp.sum((boundaries[:, None] < begin + places[None, :]).astype(jnp.int32), axis=0)
    starts = jnp.sum((boundaries[:, None] == begin + places[None, :]).astype(jnp.int32), axis=0)
    slot_ids = jnp.arange(CAP, dtype=jnp.int32)
    picks = (earlier - earlier[0] == slot_ids[:, None]) & (starts > 0)
    q_at = jnp.sum(jnp.where(picks, places[None, :], 0), axis=1)
    sel = picks.astype(BF16)
    blocks = jnp.arange(n_dev, dtype=jnp.int32)
    block_first = jnp.sum((boundaries[:, None] < blocks[None, :] * length).astype(jnp.int32), axis=0)
    block_count = jnp.concatenate([block_first[1:], jnp.full((1,), n_span, jnp.int32)]) - block_first
    span_at = jnp.where(
        slot_ids[None, :] < block_count[:, None], block_first[:, None] + slot_ids[None, :], -1
    )

    span_grad = sum_of_spans(cotangent, earlier + starts - 1)
    rows = encode(byte_states, halo, begin, sel, q_at, enc_gain, w_qkv, w_out)

    gain_rows = main_gain[:width]
    order = jnp.arange(n_span, dtype=jnp.int32).reshape(n_seq, n_member, share)
    order = order.transpose(1, 0, 2).reshape(-1)
    direct = depth == width and n_seq == 4
    if direct:
        others = [lax.ppermute(rows, "seq", [(j, 0)]) for j in range(1, n_seq)]
        column = jnp.stack([rows] + others)
        gathered = lax.all_gather(column, MEMBER, axis=0)
        gathered = gathered.reshape(n_dev * CAP, width)
        row_span = span_at.reshape(n_seq, n_member, CAP).transpose(1, 0, 2).reshape(-1)
    else:
        gathered = lax.all_gather(rows, PART, axis=0, tiled=True)
        row_span = span_at.reshape(-1)
    compact = dot((order[:, None] == row_span[None, :]).astype(BF16), gathered)
    squares = jnp.sum(compact * compact, axis=1, keepdims=True) + jnp.sum(pad_vector * pad_vector)
    scale = lax.rsqrt(squares / main_width + 1e-05)
    main_in = (compact * scale * gain_rows).astype(BF16)

    if direct:
        pad_sum = pad_terms
        for j in range(1, n_seq):
            pad_sum = pad_sum + lax.ppermute(pad_terms, "seq", [(j, 0)])
        gate = dot(main_in, gate_w) + scale * pad_sum[:, :columns]
        upward = dot(main_in, up_w) + scale * pad_sum[:, columns:]
        hidden = (jax.nn.silu(gate) * upward).astype(BF16)
        at_two = lax.ppermute(hidden, "seq", [(0, 2)])
        at_one = lax.ppermute(at_two, "seq", [(2, 1)])
        at_three = lax.ppermute(at_two, "seq", [(2, 3)])
        hidden = jnp.where(
            seq == 0, hidden, jnp.where(seq == 2, at_two, jnp.where(seq == 1, at_one, at_three))
        )
    else:
        padded = jnp.pad(main_in, ((0, 0), (0, main_width - width)))
        here = lax.dynamic_slice_in_dim(padded, seq * depth, depth, 1)
        gate = dot(here, gate_w) + scale * pad_terms[:, :columns]
        upward = dot(here, up_w) + scale * pad_terms[:, columns:]
        gate, upward = lax.psum((gate, upward), "seq")
        hidden = (jax.nn.silu(gate) * upward).astype(BF16)

    partial = dot_t(hidden, down_t).astype(BF16).reshape(n_member, n_seq * share, depth)
    got = lax.all_to_all(partial, MEMBER, 0, 0, tiled=True)
    summed = jnp.sum(got.astype(F32), axis=0)
    member = lax.axis_index(MEMBER)
    mine = lax.dynamic_slice_in_dim(compact, member * n_seq * share, n_seq * share, 0)
    wide = jnp.concatenate(
        [mine, jnp.broadcast_to(pad_vector, (n_seq * share, main_width - width))], axis=1
    )
    residual = lax.dynamic_slice_in_dim(wide, seq * depth, depth, 1)
    done = (summed + residual).astype(BF16).reshape(n_seq, share, depth)
    spread = lax.all_to_all(done, "seq", 0, 0, tiled=True)
    main_out = spread.transpose(1, 0, 2).reshape(share, main_width)
    return (main_out, span_grad)


def solution(mesh):
    spread = P(("groups", "seq", "mp", "rep"), None)
    weight = P("seq", ("mp", "rep"))
    placed = (spread, spread, P("groups"), P(), P(), P(), P(), P(), weight, weight, weight)
    return jax.shard_map(
        local, mesh=mesh, in_specs=placed, out_specs=(spread, spread), check_vma=False
    )
```

time: 788 us -> 212 us (0.27)
  waiting for transfers between devices: 685 us -> 77.9 us
  starting transfers between devices: 8.39 us -> 62.4 us
  local copies, waits for them, and re-layouts: 29 us -> 9.62 us
    all_gather x3 -> x1, waiting for transfers between devices: 612 us -> 8.88 us  [local(): gathered = lax.all_gather(column, MEMBER, axis=0)]
    psum x2 -> x0, waiting for transfers between devices: 64.9 us -> none  [the longest x1 33.7 us: local(): lax.psum(partial_out.astype(jnp.bfloat16), ('mp', 'rep'))]
    ppermute x3 -> x12, waiting for transfers between devices: 5.97 us -> 49.3 us  [the longest x1 33.2 us: local(): at_two = lax.ppermute(hidden, 'seq', [(0, 2)])]
    all_to_all x0 -> x3, starting transfers between devices: none -> 40.2 us  [the longest x1 32.4 us: local(): spread = lax.all_to_all(done, 'seq', 0, 0, tiled=True)]
    gather x20 -> x0, local copies, waits for them, and re-layouts: 25.3 us -> none  [the longest x10 12.7 us: local(): right_side = jnp.searchsorted(boundaries, qpos, side='right')]
    all_to_all x0 -> x3, waiting for transfers between devices: none -> 19.7 us  [the longest x1 8.87 us: local(): got = lax.all_to_all(partial, MEMBER, 0, 0, tiled=True)]
    ppermute x3 -> x12, starting transfers between devices: 8.19 us -> 22.1 us  [the longest x1 5.49 us: local(): at_two = lax.ppermute(hidden, 'seq', [(0, 2)])]
    dot_general x9 -> x16, matrix products: 34 us -> 30.1 us  [the longest x13 21.6 us: dot(): return jnp.dot(a, b, preferred_element_type=F32)]
  transfers between devices with their start and end apart: 8 -> 16, of which waited for: 7 -> 11; matrix products, arithmetic and copies ran while one was open for 5% -> 13% of each run, Pallas kernels for 0% -> 0%
where the time goes in v1:
time: 212 us; the launch traced here: 211 us
  waiting for transfers between devices  77.9 us (37%)
  starting transfers between devices  62.4 us (29%)
  matrix products  30.1 us (14%)
  other arithmetic  16.5 us (8%)
  between operations  14.5 us (7%)
  local copies, waits for them, and re-layouts  9.62 us (5%)
    ppermute x1, waiting for transfers between devices, local(): at_two = lax.ppermute(hidden, 'seq', [(0, 2)])  33.2 us
    all_to_all x1, starting transfers between devices, local(): spread = lax.all_to_all(done, 'seq', 0, 0, tiled=True)  32.4 us
    dot_general x13, matrix products, dot(): return jnp.dot(a, b, preferred_element_type=F32)  21.6 us
    ppermute x3, waiting for transfers between devices, local(): others = [lax.ppermute(rows, 'seq', [(j, 0)]) for j in range(1, n_seq)]  13.5 us
    all_gather x1, waiting for transfers between devices, local(): gathered = lax.all_gather(column, MEMBER, axis=0)  8.88 us
    all_to_all x1, waiting for transfers between devices, local(): got = lax.all_to_all(partial, MEMBER, 0, 0, tiled=True)  8.87 us
    all_to_all x1, waiting for transfers between devices, local(): spread = lax.all_to_all(done, 'seq', 0, 0, tiled=True)  8.16 us
    dot_general x1, matrix products, dot_t(): lax.dot_general(a, b, (((1,), (1,)), ((), ())), preferred_element_type=F32)  5.81 us
  transfers between devices with their start and end apart: 16, of which 11 were waited for; matrix products, arithmetic and copies ran while one was open for 13% of the time, Pallas kernels for 0%

profile of v1, /device:TPU:0, one launch (start us, length us, event | category | flops | bytes accessed | tf_op | source)
XLA Modules:
  0.0 211.0 jit_solution(7289015316502573090)
XLA Ops:
  7.2 2.6 %collective-permute-start = (bf16[128,1024]{1,0:T(8,128)(2,1)}, bf16[128,1024]{1,0:T(8,128)(2,1)S(1)}, u32[]{:S(2)}, u32[]{:S(2)}) collective-permute-start(bf16[128,1024]{1,0:T(8,128)(2,1)} %param.11), channel_id=1, source_target_pairs={{0,1},{1,2},{2,3},{3,4},{4,5},{5,6},{6,7},{7,8},{8,9},{9,10},{10,1... | collective-permute-start | bytes 786440 | tf_op jit(solution)/shard_map/ppermute | solution.py:117
  11.5 1.8 fusion.60
  14.5 1.9 fusion.33
  16.5 2.3 %fusion.28 = bf16[8,8,8,128]{3,2,1,0:T(8,128)(2,1)S(1)} fusion(bf16[1024,3072]{1,0:T(8,128)(2,1)} %param.15, bf16[256,1024]{1,0:T(8,128)(2,1)} %fusion.33, s32[128]{0:T(128)} %copy-done.12, pred[128]{0:T(512)(128)(4,1)} %copy-done.13), kind=kOutput, calls=%fused_computation.34 | convolution fusion | flops 151142400 | bytes 2491392 | tf_op jit(solution)/shard_map/dot_general | solution.py:17
  18.8 3.6 %fusion.3 = bf16[256,2048]{1,0:T(8,128)(2,1)S(1)} fusion(bf16[256,1024]{1,0:T(8,128)(2,1)} %fusion.33, bf16[1024,3072]{1,0:T(8,128)(2,1)} %param.15), kind=kOutput, calls=%fused_computation.4 | convolution fusion | flops 1074266112 | bytes 5767168 | tf_op jit(solution)/shard_map/dot_general | solution.py:17
  24.6 2.3 %fusion.27 = bf16[8,8,8,128]{3,2,1,0:T(8,128)(2,1)S(1)} fusion(bf16[32,8,8,128]{3,2,1,0:T(8,128)(2,1)} %get-tuple-element.9, f32[8,64]{1,0:T(8,128)S(1)} %fusion.87, f32[8,64,256]{2,1,0:T(8,128)} %copy-done.3), kind=kOutput, calls=%fused_computation.33 | convolution fusion | flops 34013952 | bytes 1181696 | tf_op jit(solution)/shard_map/hqk,khd->qhd/dot_general | solution.py:48
  27.0 2.1 fusion.23
  32.9 8.4 %collective-permute-done.3 = bf16[64,1024]{1,0:T(8,128)(2,1)S(1)} collective-permute-done((bf16[64,1024]{1,0:T(8,128)(2,1)S(1)}, bf16[64,1024]{1,0:T(8,128)(2,1)S(1)}, u32[]{:S(2)}, u32[]{:S(2)}) %collective-permute-start.3) | collective-permute-done | bytes 131104 | tf_op jit(solution)/shard_map/ppermute | solution.py:148
  41.3 2.4 %collective-permute-done.2 = bf16[64,1024]{1,0:T(8,128)(2,1)S(1)} collective-permute-done((bf16[64,1024]{1,0:T(8,128)(2,1)S(1)}, bf16[64,1024]{1,0:T(8,128)(2,1)S(1)}, u32[]{:S(2)}, u32[]{:S(2)}) %collective-permute-start.2) | collective-permute-done | bytes 131104 | tf_op jit(solution)/shard_map/ppermute | solution.py:148
  43.7 2.7 %collective-permute-done.1 = bf16[64,1024]{1,0:T(8,128)(2,1)S(1)} collective-permute-done((bf16[64,1024]{1,0:T(8,128)(2,1)S(1)}, bf16[64,1024]{1,0:T(8,128)(2,1)S(1)}, u32[]{:S(2)}, u32[]{:S(2)}) %collective-permute-start.1) | collective-permute-done | bytes 131104 | tf_op jit(solution)/shard_map/ppermute | solution.py:148
  47.4 1.3 slice_multiply_fusion
  49.3 1.4 copy-done.1
  56.8 1.9 collective-permute-done.6
  59.5 8.9 %all-gather.3.cloned.1.call-done = bf16[16,64,1024]{2,1,0:T(8,128)(2,1)} async-done(((bf16[4,64,1024]{2,1,0:T(8,128)(2,1)}), bf16[16,64,1024]{2,1,0:T(8,128)(2,1)}) %all-gather.3.cloned.1.call-update) | async-done | bytes 2097168 | tf_op jit(solution)/shard_map/all_gather | solution.py:150
  68.3 3.0 %multiply_reduce_fusion = (f32[512]{0:T(512)S(1)}, f32[512,1024]{1,0:T(8,128)S(1)}) fusion(bf16[1024,1024]{1,0:T(8,128)(2,1)} %bitcast.67, s32[1024]{0:T(1024)S(1)} %select_n.47, s32[512]{0:T(512)S(1)} %reshape.269), kind=kOutput, calls=%fused_computation.8 | convolution fusion | flops 1075314176 | bytes 4202496 | tf_op jit(solution)/shard_map/dot_general | solution.py:17
  72.0 1.9 fusion.83
  73.9 3.6 %multiply_convert_fusion = bf16[512,1536]{1,0:T(8,128)(2,1)} fusion(f32[512,1536]{1,0:T(8,128)S(1)} %fusion.83, f32[1536]{0:T(1024)S(1)} %get-tuple-element.3, f32[1536]{0:T(1024)S(1)} %get-tuple-element.2, f32[512]{0:T(512)S(1)} %add_rsqrt_fusion, bf16[1024,1536]{1,0:T(8,128)(2,1)S(1)} %copy-done.2, f32[512,1024]{1,0:T(8,128)S(1)} %get-tuple-element.19, ...), kind=kOutput, calls=%fused_computation.3 | convolution fusion | flops 1620049920 | bytes 9979904 | tf_op jit(solution)/shard_map/dot_general | solution.py:17
  77.6 5.5 %collective-permute-start.7 = (bf16[512,1536]{1,0:T(8,128)(2,1)}, bf16[512,1536]{1,0:T(8,128)(2,1)}, u32[]{:S(2)}, u32[]{:S(2)}) collective-permute-start(bf16[512,1536]{1,0:T(8,128)(2,1)} %multiply_convert_fusion), channel_id=1, source_target_pairs={{0,8},{1,9},{2,10},{3,11},{16,24},{17,25},{18,26},{19,27}} | collective-permute-start | bytes 4718600 | tf_op jit(solution)/shard_map/ppermute | solution.py:168
  83.1 33.2 %collective-permute-done.7 = bf16[512,1536]{1,0:T(8,128)(2,1)} collective-permute-done((bf16[512,1536]{1,0:T(8,128)(2,1)}, bf16[512,1536]{1,0:T(8,128)(2,1)}, u32[]{:S(2)}, u32[]{:S(2)}) %collective-permute-start.7) | collective-permute-done | bytes 1572896 | tf_op jit(solution)/shard_map/ppermute | solution.py:168
  116.2 1.8 collective-permute-start.9
  118.0 1.9 collective-permute-start.8
  127.0 5.8 %fusion.17 = bf16[512,1024]{1,0:T(8,128)(2,1)} fusion(bf16[1024,1536]{1,0:T(8,128)(2,1)} %param.21, bf16[512,1536]{1,0:T(8,128)(2,1)} %multiply_convert_fusion, bf16[512,1536]{1,0:T(8,128)(2,1)} %collective-permute-done.7, bf16[512,1536]{1,0:T(8,128)(2,1)} %collective-permute-done.8, bf16[512,1536]{1,0:T(8,128)(2,1)} %collective-permute-done.9, ...), kind=kOutput, calls=%fused_computation.20 | convolution fusion | flops 1613496320 | bytes 10485763 | tf_op jit(solution)/shard_map/dot_general | solution.py:21
  132.9 4.4 %all-to-all-start = ((bf16[4,128,1024]{2,1,0:T(8,128)(2,1)}), bf16[4,128,1024]{2,1,0:T(8,128)(2,1)}, u32[]{:S(2)}, u32[]{:S(2)}) async-start(bf16[4,128,1024]{2,1,0:T(8,128)(2,1)} %bitcast.58), calls=%async_computation | async-start | bytes 2097152 | tf_op jit(solution)/shard_map/all_to_all | solution.py:183
  141.0 1.9 constant_dynamic-slice_fusion
  142.9 8.9 %all-to-all-done = bf16[4,128,1024]{2,1,0:T(8,128)(2,1)} async-done(((bf16[4,128,1024]{2,1,0:T(8,128)(2,1)}), bf16[4,128,1024]{2,1,0:T(8,128)(2,1)}, u32[]{:S(2)}, u32[]{:S(2)}) %all-to-all-start) | async-done | bytes 1048608 | tf_op jit(solution)/shard_map/all_to_all | solution.py:183
  151.8 3.4 %all-to-all-start.2 = ((bf16[4,32,1024]{2,1,0:T(8,128)(2,1)}), bf16[4,32,1024]{2,1,0:T(8,128)(2,1)S(1)}, u32[]{:S(2)}, u32[]{:S(2)}) async-start(bf16[4,32,1024]{2,1,0:T(8,128)(2,1)} %bitcast.59), calls=%async_computation.2 | async-start | bytes 524288 | tf_op jit(solution)/shard_map/all_to_all | solution.py:82
  155.2 1.5 convert_reduce_fusion
  156.7 1.8 fusion.38
  158.5 2.7 %all-to-all-done.2 = bf16[4,32,1024]{2,1,0:T(8,128)(2,1)S(1)} async-done(((bf16[4,32,1024]{2,1,0:T(8,128)(2,1)}), bf16[4,32,1024]{2,1,0:T(8,128)(2,1)S(1)}, u32[]{:S(2)}, u32[]{:S(2)}) %all-to-all-start.2) | async-done | bytes 262176 | tf_op jit(solution)/shard_map/all_to_all | solution.py:82
  161.2 32.4 %all-to-all-start.1 = ((bf16[4,32,1024]{2,1,0:T(8,128)(2,1)}), bf16[4,32,1024]{2,1,0:T(8,128)(2,1)}, u32[]{:S(2)}, u32[]{:S(2)}) async-start(bf16[4,32,1024]{2,1,0:T(8,128)(2,1)} %bitcast.11), calls=%async_computation.1 | async-start | bytes 524288 | tf_op jit(solution)/shard_map/all_to_all | solution.py:192
  194.3 8.2 %all-to-all-done.1 = bf16[4,32,1024]{2,1,0:T(8,128)(2,1)} async-done(((bf16[4,32,1024]{2,1,0:T(8,128)(2,1)}), bf16[4,32,1024]{2,1,0:T(8,128)(2,1)}, u32[]{:S(2)}, u32[]{:S(2)}) %all-to-all-start.1) | async-done | bytes 262176 | tf_op jit(solution)/shard_map/all_to_all | solution.py:192
  202.5 1.7 copy.49
  (99 shorter events, 29.4 us)
Async XLA Ops:
  7.2 41.6 %copy-start = (bf16[1024,1536]{1,0:T(8,128)(2,1)S(1)}, bf16[1024,1536]{1,0:T(8,128)(2,1)}, u32[]{:S(2)}) copy-start(bf16[1024,1536]{1,0:T(8,128)(2,1)} %param.20) | copy-start | bytes 9437188
  7.2 61.2 %all-gather.3.cloned.1.call-start = ((), (), s32[]{:S(2)}) async-start(), calls=%async_computation.3 | async-start | bytes 2621440 | tf_op jit(solution)/shard_map/all_gather | solution.py:150
  7.2 6.2 %collective-permute-start = (bf16[128,1024]{1,0:T(8,128)(2,1)}, bf16[128,1024]{1,0:T(8,128)(2,1)S(1)}, u32[]{:S(2)}, u32[]{:S(2)}) collective-permute-start(bf16[128,1024]{1,0:T(8,128)(2,1)} %param.11), channel_id=1, source_target_pairs={{0,1},{1,2},{2,3},{3,4},{4,5},{5,6},{6,7},{7,8},{8,9},{9,10},{10,1... | collective-permute-start | bytes 786440 | tf_op jit(solution)/shard_map/ppermute | solution.py:117
  10.8 3.8 %copy-start.13 = (pred[128]{0:T(512)(128)(4,1)}, pred[128]{0:T(512)(128)(4,1)S(1)}, u32[]{:S(2)}) copy-start(pred[128]{0:T(512)(128)(4,1)S(1)} %broadcast_compare_fusion.1) | copy-start | bytes 388
  11.3 2.1 copy-start.12
  23.2 3.7 %copy-start.4 = (f32[64,1024]{1,0:T(8,128)S(1)}, f32[64,1024]{1,0:T(8,128)}, u32[]{:S(2)}) copy-start(f32[64,1024]{1,0:T(8,128)} %fusion.60) | copy-start | bytes 786436
  23.6 0.8 copy-start.3
  26.9 20.4 %copy-start.7 = (f32[3072]{0:T(1024)S(1)}, f32[3072]{0:T(1024)}, u32[]{:S(2)}) copy-start(f32[3072]{0:T(1024)} %param.17) | copy-start | bytes 36868
  29.0 12.3 %collective-permute-start.3 = (bf16[64,1024]{1,0:T(8,128)(2,1)S(1)}, bf16[64,1024]{1,0:T(8,128)(2,1)S(1)}, u32[]{:S(2)}, u32[]{:S(2)}) collective-permute-start(bf16[64,1024]{1,0:T(8,128)(2,1)S(1)} %fusion.23), channel_id=1, source_target_pairs={{12,0},{13,1},{14,2},{15,3},{28,16},{29,17},{30,18},{31,19}} | collective-permute-start | bytes 393224 | tf_op jit(solution)/shard_map/ppermute | solution.py:148
  30.3 13.4 %collective-permute-start.2 = (bf16[64,1024]{1,0:T(8,128)(2,1)S(1)}, bf16[64,1024]{1,0:T(8,128)(2,1)S(1)}, u32[]{:S(2)}, u32[]{:S(2)}) collective-permute-start(bf16[64,1024]{1,0:T(8,128)(2,1)S(1)} %fusion.23), channel_id=1, source_target_pairs={{8,0},{9,1},{10,2},{11,3},{24,16},{25,17},{26,18},{27,19}} | collective-permute-start | bytes 393224 | tf_op jit(solution)/shard_map/ppermute | solution.py:148
  31.6 14.8 %collective-permute-start.1 = (bf16[64,1024]{1,0:T(8,128)(2,1)S(1)}, bf16[64,1024]{1,0:T(8,128)(2,1)S(1)}, u32[]{:S(2)}, u32[]{:S(2)}) collective-permute-start(bf16[64,1024]{1,0:T(8,128)(2,1)S(1)} %fusion.23), channel_id=1, source_target_pairs={{4,0},{5,1},{6,2},{7,3},{20,16},{21,17},{22,18},{23,19}} | collective-permute-start | bytes 393224 | tf_op jit(solution)/shard_map/ppermute | solution.py:148
  48.8 1.9 copy-start.1
  50.7 4.5 %copy-start.8 = (s32[512]{0:T(512)S(1)}, s32[512]{0:T(512)}, u32[]{:S(2)}) copy-start(s32[512]{0:T(512)} %param.13) | copy-start | bytes 6148
  51.2 7.4 %collective-permute-start.6 = (f32[1,3072]{1,0:T(1,128)S(1)}, f32[1,3072]{1,0:T(1,128)S(1)}, u32[]{:S(2)}, u32[]{:S(2)}) collective-permute-start(f32[1,3072]{1,0:T(1,128)S(1)} %fusion.70), channel_id=1, source_target_pairs={{12,0},{13,1},{14,2},{15,3},{28,16},{29,17},{30,18},{31,19}} | collective-permute-start | bytes 36872 | tf_op jit(solution)/shard_map/ppermute | solution.py:164
  52.5 6.5 %collective-permute-start.5 = (f32[1,3072]{1,0:T(1,128)S(1)}, f32[1,3072]{1,0:T(1,128)S(1)}, u32[]{:S(2)}, u32[]{:S(2)}) collective-permute-start(f32[1,3072]{1,0:T(1,128)S(1)} %fusion.70), channel_id=1, source_target_pairs={{8,0},{9,1},{10,2},{11,3},{24,16},{25,17},{26,18},{27,19}} | collective-permute-start | bytes 36872 | tf_op jit(solution)/shard_map/ppermute | solution.py:164
  53.8 5.6 %collective-permute-start.4 = (f32[1,3072]{1,0:T(1,128)S(1)}, f32[1,3072]{1,0:T(1,128)S(1)}, u32[]{:S(2)}, u32[]{:S(2)}) collective-permute-start(f32[1,3072]{1,0:T(1,128)S(1)} %fusion.70), channel_id=1, source_target_pairs={{4,0},{5,1},{6,2},{7,3},{20,16},{21,17},{22,18},{23,19}} | collective-permute-start | bytes 36872 | tf_op jit(solution)/shard_map/ppermute | solution.py:164
  71.3 2.6 %copy-start.6 = (f32[512,1024]{1,0:T(8,128)}, f32[512,1024]{1,0:T(8,128)S(1)}, u32[]{:S(2)}) copy-start(f32[512,1024]{1,0:T(8,128)S(1)} %get-tuple-element.19) | copy-start | bytes 6291460
  72.0 1.9 copy-start.2
  73.9 46.0 %copy-start.9 = (s32[128]{0:T(128)S(1)}, s32[128]{0:T(128)}, u32[]{:S(2)}) copy-start(s32[128]{0:T(128)} %get-tuple-element.16) | copy-start | bytes 1540
  73.9 49.2 %copy-start.5 = (bf16[128,1024]{1,0:T(8,128)(2,1)S(1)}, bf16[128,1024]{1,0:T(8,128)(2,1)}, u32[]{:S(2)}) copy-start(bf16[128,1024]{1,0:T(8,128)(2,1)} %param.12) | copy-start | bytes 786436
  77.6 38.7 %collective-permute-start.7 = (bf16[512,1536]{1,0:T(8,128)(2,1)}, bf16[512,1536]{1,0:T(8,128)(2,1)}, u32[]{:S(2)}, u32[]{:S(2)}) collective-permute-start(bf16[512,1536]{1,0:T(8,128)(2,1)} %multiply_convert_fusion), channel_id=1, source_target_pairs={{0,8},{1,9},{2,10},{3,11},{16,24},{17,25},{18,26},{19,27}} | collective-permute-start | bytes 4718600 | tf_op jit(solution)/shard_map/ppermute | solution.py:168
  116.2 10.8 %collective-permute-start.9 = (bf16[512,1536]{1,0:T(8,128)(2,1)}, bf16[512,1536]{1,0:T(8,128)(2,1)}, u32[]{:S(2)}, u32[]{:S(2)}) collective-permute-start(bf16[512,1536]{1,0:T(8,128)(2,1)} %collective-permute-done.7), channel_id=1, source_target_pairs={{8,12},{9,13},{10,14},{11,15},{24,28},{25,29},{26,30},{27,31}} | collective-permute-start | bytes 4718600 | tf_op jit(solution)/shard_map/ppermute | solution.py:170
  118.0 9.0 %collective-permute-start.8 = (bf16[512,1536]{1,0:T(8,128)(2,1)}, bf16[512,1536]{1,0:T(8,128)(2,1)}, u32[]{:S(2)}, u32[]{:S(2)}) collective-permute-start(bf16[512,1536]{1,0:T(8,128)(2,1)} %collective-permute-done.7), channel_id=1, source_target_pairs={{8,4},{9,5},{10,6},{11,7},{24,20},{25,21},{26,22},{27,23}} | collective-permute-start | bytes 4718600 | tf_op jit(solution)/shard_map/ppermute | solution.py:169
  122.5 0.9 copy-start.10
  123.5 15.8 %collective-permute-start.10 = (bf16[24,1024]{1,0:T(8,128)(2,1)S(1)}, bf16[24,1024]{1,0:T(8,128)(2,1)S(1)}, u32[]{:S(2)}, u32[]{:S(2)}) collective-permute-start(bf16[24,1024]{1,0:T(8,128)(2,1)S(1)} %convolution_convert_fusion.4), channel_id=1, source_target_pairs={{0,4},{4,8},{8,12},{1,5},{5,9},{9,13},{2,6},{6,10},{10,14},{3,7},{... | collective-permute-start | bytes 147464 | tf_op jit(solution)/shard_map/ppermute | solution.py:75
  125.7 13.6 %collective-permute-start.11 = (bf16[24,1024]{1,0:T(8,128)(2,1)S(1)}, bf16[24,1024]{1,0:T(8,128)(2,1)S(1)}, u32[]{:S(2)}, u32[]{:S(2)}) collective-permute-start(bf16[24,1024]{1,0:T(8,128)(2,1)S(1)} %convolution_convert_fusion.3), channel_id=1, source_target_pairs={{4,0},{8,4},{12,8},{5,1},{9,5},{13,9},{6,2},{10,6},{14,10},{7,3},{... | collective-permute-start | bytes 147464 | tf_op jit(solution)/shard_map/ppermute | solution.py:76
  132.9 4.4 %copy-start.11 = (pred[64]{0:T(512)(128)(4,1)S(1)}, pred[64]{0:T(512)(128)(4,1)}, u32[]{:S(2)}) copy-start(pred[64]{0:T(512)(128)(4,1)} %copy-done.10) | copy-start | bytes 196
  132.9 18.9 %all-to-all-start = ((bf16[4,128,1024]{2,1,0:T(8,128)(2,1)}), bf16[4,128,1024]{2,1,0:T(8,128)(2,1)}, u32[]{:S(2)}, u32[]{:S(2)}) async-start(bf16[4,128,1024]{2,1,0:T(8,128)(2,1)} %bitcast.58), calls=%async_computation | async-start | bytes 2097152 | tf_op jit(solution)/shard_map/all_to_all | solution.py:183
  151.8 9.4 %all-to-all-start.2 = ((bf16[4,32,1024]{2,1,0:T(8,128)(2,1)}), bf16[4,32,1024]{2,1,0:T(8,128)(2,1)S(1)}, u32[]{:S(2)}, u32[]{:S(2)}) async-start(bf16[4,32,1024]{2,1,0:T(8,128)(2,1)} %bitcast.59), calls=%async_computation.2 | async-start | bytes 524288 | tf_op jit(solution)/shard_map/all_to_all | solution.py:82
  161.2 41.3 %all-to-all-start.1 = ((bf16[4,32,1024]{2,1,0:T(8,128)(2,1)}), bf16[4,32,1024]{2,1,0:T(8,128)(2,1)}, u32[]{:S(2)}, u32[]{:S(2)}) async-start(bf16[4,32,1024]{2,1,0:T(8,128)(2,1)} %bitcast.11), calls=%async_computation.1 | async-start | bytes 524288 | tf_op jit(solution)/shard_map/all_to_all | solution.py:192
Sparse Core Ops, SparseCore 0:
  47.5 20.8 all-gather.2

commit v2 on v1

v2 whole, which is shorter than its diff:
```python
import jax
import jax.numpy as jnp
from jax import lax
from jax.experimental import pallas as pl
from jax.experimental.pallas import tpu as pltpu
from jax.sharding import PartitionSpec as P

HEAD = 128
WINDOW = 128
CAP = 64
LANE = 24
LANE_ROWS = 32
HALF = 96
VMEM_LIMIT = 56 << 20
CHUNKS = ((0, (0, 1, 2)), (1, (3, 4, 5, 6)), (2, (7, 8, 9, 10)), (3, (11, 12, 13)), (3, (14, 15)))
PART = ("seq", "mp", "rep")
MEMBER = ("mp", "rep")
F32 = jnp.float32
BF16 = jnp.bfloat16


def dot(a, b):
    return jnp.dot(a, b, preferred_element_type=F32)


def dot_t(a, b):
    return lax.dot_general(a, b, (((1,), (1,)), ((), ())), preferred_element_type=F32)


def is_direct():
    return lax.axis_size("seq") == 4 and lax.axis_size("mp") == 2 and lax.axis_size("rep") == 2


def swap(value, axis):
    return lax.ppermute(value, axis, [(0, 1), (1, 0)])


def pick(index, values):
    out = values[-1]
    for i in range(len(values) - 2, -1, -1):
        out = jnp.where(index == i, values[i], out)
    return out


def sum_members(value):
    mp, rep = lax.axis_index("mp"), lax.axis_index("rep")
    rows = value.reshape((2, 2) + value.shape[1:])
    keep = pick(rep, [rows[:, 0], rows[:, 1]])
    send = pick(rep, [rows[:, 1], rows[:, 0]])
    keep = keep + swap(send.astype(BF16), "rep").astype(F32)
    own = pick(mp, [keep[0], keep[1]])
    other = pick(mp, [keep[1], keep[0]])
    return own + swap(other.astype(BF16), "mp").astype(F32)


def rms_scale(values, gain):
    return values * lax.rsqrt(jnp.mean(values * values, axis=-1, keepdims=True) + 1e-05) * gain


def encode(x, halo, begin, sel, q_at, enc_gain, w_qkv, w_out):
    length, width = x.shape
    heads = width // HEAD
    both = jnp.concatenate([halo, x], axis=0)
    normed = rms_scale(both.astype(F32), enc_gain).astype(BF16)
    picked = dot(sel, normed[length:]).astype(BF16)
    queries = dot(picked, w_qkv[:, :width]).astype(BF16)
    keyval = dot(normed, w_qkv[:, width:]).astype(BF16)
    k_at = jnp.arange(2 * length, dtype=jnp.int32) - length
    allowed = (
        (k_at[None, :] <= q_at[:, None])
        & (k_at[None, :] > q_at[:, None] - WINDOW)
        & (k_at[None, :] + begin >= 0)
    )
    q_heads = queries.reshape(CAP, heads, HEAD)
    k_heads = keyval[:, :width].reshape(2 * length, heads, HEAD)
    v_heads = keyval[:, width:].reshape(2 * length, heads, HEAD)
    scores = jnp.einsum("qhd,khd->hqk", q_heads, k_heads, preferred_element_type=F32)
    scores = jnp.where(allowed[None], scores / jnp.sqrt(F32(HEAD)), F32(-1e30))
    probs = jax.nn.softmax(scores, axis=-1).astype(BF16)
    mixed = jnp.einsum("hqk,khd->qhd", probs, v_heads, preferred_element_type=F32)
    attended = mixed.reshape(CAP, width).astype(BF16)
    return (dot(sel, x) + dot(attended, w_out)).astype(BF16)


def sum_of_spans(cotangent, span_index):
    n_member = lax.axis_size(MEMBER)
    n_seq = lax.axis_size("seq")
    owner = lax.axis_index("seq")
    length, width = cotangent.shape
    span_own = 32 * n_member
    lowest, highest = span_index[0], span_index[length - 1]
    slot_ids = jnp.arange(CAP, dtype=jnp.int32)
    onehot = (span_index[None, :] - lowest == slot_ids[:, None]).astype(BF16)
    pieces = dot(onehot, cotangent).astype(BF16)
    span_ids = lowest + slot_ids
    valid = (span_ids <= highest)[None, :]
    lane_ids = jnp.arange(LANE, dtype=jnp.int32)
    row_ids = jnp.arange(span_own, dtype=jnp.int32)

    def choose(targets):
        return dot(((targets[:, None] == span_ids[None, :]) & valid).astype(BF16), pieces)

    to_before = choose(owner * span_own - LANE + lane_ids).astype(BF16)
    to_after = choose((owner + 1) * span_own + lane_ids).astype(BF16)
    up = [(i, i + 1) for i in range(n_seq - 1)]
    down = [(i + 1, i) for i in range(n_seq - 1)]
    from_before = lax.ppermute(to_after, "seq", up).astype(F32)
    from_after = lax.ppermute(to_before, "seq", down).astype(F32)
    block = choose(owner * span_own + row_ids)
    block = jnp.concatenate(
        [block[:LANE] + from_before, block[LANE:-LANE], block[-LANE:] + from_after], axis=0
    )
    sent = block.astype(BF16).reshape(n_member, span_own // n_member, width)
    got = lax.all_to_all(sent, MEMBER, 0, 0, tiled=True)
    return jnp.sum(got.astype(F32), axis=0).astype(BF16)


def relay(value):
    return lax.ppermute(value, "seq", [(2, 1)]), lax.ppermute(value, "seq", [(2, 3)])


def exchange_sums(sums):
    own = sums.shape[0] - 2 * LANE_ROWS
    n_seq = lax.axis_size("seq")
    up = [(i, i + 1) for i in range(n_seq - 1)]
    down = [(i + 1, i) for i in range(n_seq - 1)]
    from_after = lax.ppermute(sums[own : own + LANE_ROWS], "seq", down)
    from_before = lax.ppermute(sums[own + LANE_ROWS :], "seq", up)
    return from_before, from_after


def route_sums(sums, from_both):
    own = sums.shape[0] - 2 * LANE_ROWS
    first, last = (value.astype(F32) for value in from_both)
    block = sums[:own].astype(F32)
    block = jnp.concatenate(
        [block[:LANE_ROWS] + first, block[LANE_ROWS:-LANE_ROWS], block[-LANE_ROWS:] + last], axis=0
    )
    return sum_members(block.reshape(4, own // 4, -1)).astype(BF16)


def pad_kernel(at_ref, pad_ref, gain_ref, gate_ref, up_ref, out_ref):
    high, low = split_high_low(jnp.broadcast_to(pad_ref[...] * gain_ref[...], (8, pad_ref.shape[1])))
    both = jnp.concatenate([high, low], axis=0)
    for at, weight_ref in enumerate((gate_ref, up_ref)):
        terms = dot(both, weight_ref[...])
        terms = terms[:1] + terms[8:9]
        out_ref[at : at + 1] = jnp.where(at_ref[2] == 0, 0.0, terms)


def pad_terms_of(at, pad_vector, main_gain, gate_w, up_w):
    depth, columns = gate_w.shape
    block = 4 * HEAD
    pad_block = pl.BlockSpec((1, depth), lambda i, at: (0, jnp.maximum(at[2] - 1, 0)))
    gain_block = pl.BlockSpec((1, depth), lambda i, at: (0, at[2]))
    weight_block = pl.BlockSpec((depth, block), lambda i, at: (0, i))
    return pl.pallas_call(
        pad_kernel,
        out_shape=jax.ShapeDtypeStruct((2, columns), F32),
        grid_spec=pltpu.PrefetchScalarGridSpec(
            num_scalar_prefetch=1,
            grid=(columns // block,),
            in_specs=[pad_block, gain_block, weight_block, weight_block],
            out_specs=pl.BlockSpec((2, block), lambda i, at: (0, i)),
        ),
        compiler_params=pltpu.CompilerParams(vmem_limit_bytes=VMEM_LIMIT),
        cost_estimate=pl.CostEstimate(flops=100_000_000, bytes_accessed=6_500_000, transcendentals=0),
        name="pad_terms",
    )(at, pad_vector.reshape(1, -1), main_gain.reshape(1, -1), gate_w, up_w)


def plan_kernel(at_ref, starts_ref, cotangent_ref, sel_ref, bias_ref, pack_ref, place_ref, sums_ref):
    device, member, owner = at_ref[0], at_ref[1], at_ref[2]
    n_span = starts_ref.shape[1]
    length = cotangent_ref.shape[0]
    begin = device * length
    row = starts_ref[...]
    column = jnp.transpose(jnp.broadcast_to(row, (length, n_span)))
    here = begin + lax.broadcasted_iota(jnp.int32, (n_span, length), 1)
    earlier = jnp.sum(jnp.where(column < here, 1.0, 0.0), axis=0, keepdims=True).astype(jnp.int32)
    start = jnp.sum(jnp.where(column == here, 1.0, 0.0), axis=0, keepdims=True).astype(jnp.int32)
    slot = lax.broadcasted_iota(jnp.int32, (CAP, length), 0)
    picked = (earlier - earlier[:, :1] == slot) & (start > 0)
    picked = jnp.where(picked, 1.0, 0.0)
    sel_ref[...] = picked.astype(BF16)
    place_in = lax.broadcasted_iota(jnp.int32, (CAP, length), 1).astype(F32)
    q_at = jnp.sum(picked * place_in, axis=1, keepdims=True).astype(jnp.int32)
    k_at = lax.broadcasted_iota(jnp.int32, (CAP, 2 * length), 1) - length
    allowed = (k_at <= q_at) & (k_at > q_at - WINDOW) & (k_at + begin >= 0)
    bias_ref[...] = jnp.where(allowed, 0.0, -1e30)

    span_index = earlier + start - 1
    n_row = sums_ref.shape[0]
    own = n_row - 2 * LANE_ROWS
    at = lax.broadcasted_iota(jnp.int32, (n_row, length), 0)
    target = jnp.where(
        at < own, owner * own + at, jnp.where(at < own + LANE_ROWS, owner * own - LANE_ROWS - own, owner * own - LANE_ROWS) + at
    )
    member_of = jnp.where(span_index == target, 1.0, 0.0).astype(BF16)
    sums_ref[...] = dot(member_of, cotangent_ref[...]).astype(BF16)

    block = owner * 4 + lax.broadcasted_iota(jnp.int32, (n_span, 4 * CAP), 1) // CAP
    first = jnp.sum(jnp.where(column[:, :1] < block * length, 1.0, 0.0), axis=0, keepdims=True).astype(jnp.int32)
    next_first = jnp.sum(jnp.where(column[:, :1] < block * length + length, 1.0, 0.0), axis=0, keepdims=True).astype(jnp.int32)
    lane = lax.broadcasted_iota(jnp.int32, (2 * HALF, 4 * CAP), 1) % CAP
    held = lax.broadcasted_iota(jnp.int32, (2 * HALF, 4 * CAP), 0) + first[:, :1]
    pack_ref[...] = jnp.where((first + lane == held) & (held < next_first), 1.0, 0.0).astype(BF16)

    around = column[:, :1] // (4 * length)
    before = jnp.sum(jnp.where(row < around * (4 * length), 1.0, 0.0), axis=1, keepdims=True).astype(jnp.int32)
    span = lax.broadcasted_iota(jnp.int32, (n_span, 1), 0)
    near = jnp.minimum((span // 32 + 1) // 4, 3)
    lies = span - before
    side = jnp.where(lies >= HALF, 1, 0)
    lies = lies - side * HALF + (side ^ (member % 2)) * HALF + (around - near + 1) * (2 * HALF)
    lanes = lax.broadcasted_iota(jnp.int32, place_ref.shape, 1)
    place_ref[...] = jnp.where(lanes == lies, 1.0, 0.0).astype(BF16)


def plan(at, boundaries, cotangent, span_own):
    n_span = boundaries.shape[0]
    length, width = cotangent.shape
    shapes = ((CAP, length), (CAP, 2 * length), (2 * HALF, 4 * CAP), (n_span, 4 * HALF), (span_own + 2 * LANE_ROWS, width))
    return pl.pallas_call(
        plan_kernel,
        out_shape=tuple(jax.ShapeDtypeStruct(s, F32 if i == 1 else BF16) for i, s in enumerate(shapes)),
        in_specs=[
            pl.BlockSpec(memory_space=pltpu.SMEM),
            pl.BlockSpec(memory_space=pltpu.VMEM),
            pl.BlockSpec(memory_space=pltpu.VMEM),
        ],
        out_specs=tuple(pl.BlockSpec(memory_space=pltpu.VMEM) for _ in shapes),
        compiler_params=pltpu.CompilerParams(vmem_limit_bytes=16 << 20),
        cost_estimate=pl.CostEstimate(flops=60_000_000, bytes_accessed=1_500_000, transcendentals=0),
        name="plan",
    )(at, boundaries.reshape(1, n_span), cotangent)


def encode_kernel(x_ref, halo_ref, sel_ref, bias_ref, gain_ref, qkv_ref, o_ref, out_ref):
    length, width = x_ref.shape
    gain = gain_ref[...]
    sel = sel_ref[...]
    bias = bias_ref[...]
    normed = rms_scale(x_ref[...].astype(F32), gain).astype(BF16)
    picked = dot(sel, normed).astype(BF16)
    normed = jnp.concatenate([rms_scale(halo_ref[...].astype(F32), gain).astype(BF16), normed], axis=0)
    mixed = []
    wide = 2 * HEAD
    for at in range(0, width, wide):
        queries = dot(picked, qkv_ref[:, at : at + wide]).astype(BF16)
        keys = dot(normed, qkv_ref[:, width + at : width + at + wide]).astype(BF16)
        values = dot(normed, qkv_ref[:, 2 * width + at : 2 * width + at + wide]).astype(BF16)
        for head in range(0, wide, HEAD):
            part = slice(head, head + HEAD)
            scores = dot_t(queries[:, part], keys[:, part]) * (HEAD**-0.5) + bias
            probs = jnp.exp(scores - jnp.max(scores, axis=1, keepdims=True))
            probs = (probs / jnp.sum(probs, axis=1, keepdims=True)).astype(BF16)
            mixed.append(dot(probs, values[:, part]).astype(BF16))
    total = dot(sel, x_ref[...]) + dot(jnp.concatenate(mixed, axis=1), o_ref[...])
    out_ref[...] = total.astype(BF16)


def encode_direct(x, halo, sel, bias, enc_gain, w_qkv, w_out):
    length, width = x.shape
    return pl.pallas_call(
        encode_kernel,
        out_shape=jax.ShapeDtypeStruct((CAP, width), BF16),
        in_specs=[pl.BlockSpec(memory_space=pltpu.VMEM)] * 7,
        out_specs=pl.BlockSpec(memory_space=pltpu.VMEM),
        compiler_params=pltpu.CompilerParams(vmem_limit_bytes=32 << 20),
        cost_estimate=pl.CostEstimate(flops=1_500_000_000, bytes_accessed=9_000_000, transcendentals=200_000),
        name="encode",
    )(x, halo, sel, bias, enc_gain.reshape(1, width), w_qkv, w_out)


def split_high_low(values):
    high = values.astype(BF16)
    return high, (values - high.astype(F32)).astype(BF16)


def block_first(boundaries, blocks, length):
    edges = jnp.stack([blocks, blocks + 1]) * length
    return jnp.sum((boundaries[:, None, None] < edges[None]).astype(jnp.int32), axis=0)


def place(first, span_ids):
    slots = jnp.arange(CAP, dtype=jnp.int32)
    held = first[0][:, None] + slots[None, :]
    held = jnp.where(held < first[1][:, None], held, -1).reshape(-1)
    return (span_ids[:, None] == held[None, :]).astype(BF16)


def local(
    byte_states,
    cotangent,
    boundaries,
    enc_gain,
    w_qkv,
    w_out,
    pad_vector,
    main_gain,
    gate_w,
    up_w,
    down_t,
):
    n_member = lax.axis_size(MEMBER)
    n_seq = lax.axis_size("seq")
    n_dev = n_seq * n_member
    seq = lax.axis_index("seq")
    device = lax.axis_index(PART)
    length, width = byte_states.shape
    depth, columns = gate_w.shape
    main_width = depth * n_seq
    n_span = boundaries.shape[0]
    share = n_span // n_dev
    begin = device * length

    shift = [(i, i + 1) for i in range(n_dev - 1)]
    halo = lax.ppermute(byte_states, PART, shift)

    direct = is_direct() and depth == width
    if direct:
        same_seq = swap(jnp.full((8, 128), seq, jnp.int32), "rep")[0, 0]
        at = jnp.stack([device, lax.axis_index(MEMBER), same_seq]).astype(jnp.int32)
        pad_terms = pad_terms_of(at, pad_vector, main_gain, gate_w, up_w)
        sel, bias, pack, where, sums = plan(at, boundaries, cotangent, n_member * share)
        rows = encode_direct(byte_states, halo, sel, bias, enc_gain, w_qkv, w_out)
    else:
        wide_gain = main_gain[width:]
        pad_in = jnp.concatenate([jnp.zeros((width,), F32), pad_vector * wide_gain])
        pad_here = lax.dynamic_slice_in_dim(pad_in, seq * depth, depth, 0)
        pad_rows = jnp.stack(split_high_low(pad_here) * 4)
        pad_terms = jnp.concatenate([dot(pad_rows, gate_w), dot(pad_rows, up_w)], axis=1)
        pad_terms = pad_terms[:1] + pad_terms[1:2]

        places = jnp.arange(length, dtype=jnp.int32)
        earlier = jnp.sum((boundaries[:, None] < begin + places[None, :]).astype(jnp.int32), axis=0)
        starts = jnp.sum((boundaries[:, None] == begin + places[None, :]).astype(jnp.int32), axis=0)
        slot_ids = jnp.arange(CAP, dtype=jnp.int32)
        picks = (earlier - earlier[0] == slot_ids[:, None]) & (starts > 0)
        q_at = jnp.sum(jnp.where(picks, places[None, :], 0), axis=1)
        sel = picks.astype(BF16)
        span_grad = sum_of_spans(cotangent, earlier + starts - 1)
        rows = encode(byte_states, halo, begin, sel, q_at, enc_gain, w_qkv, w_out)

    gain_rows = main_gain[:width]
    pad_square = jnp.sum(pad_vector * pad_vector)

    def scaled(compact):
        squares = jnp.sum(compact * compact, axis=1, keepdims=True) + pad_square
        scale = lax.rsqrt(squares / main_width + 1e-05)
        return scale, (compact * scale * gain_rows).astype(BF16)

    if not direct:
        gathered = lax.all_gather(rows, PART, axis=0, tiled=True)
        order = jnp.arange(n_span, dtype=jnp.int32).reshape(n_seq, n_member, share)
        order = order.transpose(1, 0, 2).reshape(-1)
        first = block_first(boundaries, jnp.arange(n_dev, dtype=jnp.int32), length)
        compact = dot(place(first, order), gathered)
        scale, main_in = scaled(compact)
        padded = jnp.pad(main_in, ((0, 0), (0, main_width - width)))
        here = lax.dynamic_slice_in_dim(padded, seq * depth, depth, 1)
        gate = dot(here, gate_w) + scale * pad_terms[:, :columns]
        upward = dot(here, up_w) + scale * pad_terms[:, columns:]
        gate, upward = lax.psum((gate, upward), "seq")
        hidden = (jax.nn.silu(gate) * upward).astype(BF16)
        partial = dot_t(hidden, down_t).astype(BF16).reshape(n_member, n_seq * share, depth)
        got = lax.all_to_all(partial, MEMBER, 0, 0, tiled=True)
        summed = jnp.sum(got.astype(F32), axis=0)
        member = lax.axis_index(MEMBER)
        mine = lax.dynamic_slice_in_dim(compact, member * n_seq * share, n_seq * share, 0)
        wide = jnp.concatenate(
            [mine, jnp.broadcast_to(pad_vector, (n_seq * share, main_width - width))], axis=1
        )
        residual = lax.dynamic_slice_in_dim(wide, seq * depth, depth, 1)
        done = (summed + residual).astype(BF16).reshape(n_seq, share, depth)
        spread = lax.all_to_all(done, "seq", 0, 0, tiled=True)
        main_out = spread.transpose(1, 0, 2).reshape(share, main_width)
        return (main_out, span_grad)

    pad_parts = [lax.ppermute(pad_terms, "seq", [(j, 0)]) for j in range(1, n_seq)]

    member = lax.axis_index(MEMBER)
    core = lax.axis_index("rep")
    packed = dot(pack, lax.all_gather(rows, MEMBER, axis=0, tiled=True)).astype(BF16)
    packed, pad_parts = lax.optimization_barrier((packed, pad_parts))
    pad_gate, pad_up = sum(pad_parts)[:1], sum(pad_parts)[1:]
    halves = [packed[:HALF], packed[HALF:]]
    mine = jnp.where(core == 0, halves[0], halves[1])
    came = [mine] + [lax.ppermute(mine, "seq", [(j, 0)]) for j in range(1, n_seq)]
    planes = [jnp.concatenate([mine, jnp.where(core == 0, halves[1], halves[0])], axis=0)]

    worked, kept, relayed, spread = [], [], [], []
    for index, (near, groups) in enumerate(CHUNKS):
        while len(planes) <= near:
            value, kept[-1] = lax.optimization_barrier((came[len(planes)], kept[-1]))
            planes.append(jnp.concatenate([value, swap(value, "rep")], axis=0))
        low = groups[0] * share
        high = low + len(groups) * share
        if near:
            compact = dot(where[low:high], jnp.concatenate([planes[near - 1], planes[near]], axis=0))
        else:
            compact = packed[low:high].astype(F32)
        if index == 1:
            compact, kept[0] = lax.optimization_barrier((compact, kept[0]))
        if index >= 2:
            compact, relayed[index - 2] = lax.optimization_barrier((compact, relayed[index - 2]))
            spread.append(relay(relayed[index - 2]))
        if index >= 3:
            compact, spread[index - 3] = lax.optimization_barrier((compact, spread[index - 3]))
        scale, main_in = scaled(compact)
        gate = dot(main_in, gate_w) + scale * pad_gate
        upward = dot(main_in, up_w) + scale * pad_up
        hidden = (jax.nn.silu(gate) * upward).astype(BF16)
        worked.append(compact)
        kept.append(hidden)
        relayed.append(lax.ppermute(hidden, "seq", [(0, 2)]))
    sums, relayed[-2] = lax.optimization_barrier((sums, relayed[-2]))
    from_both = exchange_sums(sums)
    spread.append(relay(relayed[-2]))
    spread.append(relay(relayed[-1]))
    from_both, spread[-1] = lax.optimization_barrier((from_both, spread[-1]))
    span_grad = route_sums(sums, from_both)

    at_owner = []
    pad_part = lax.dynamic_slice_in_dim(pad_vector, jnp.maximum(seq - 1, 0) * depth, depth, 0)
    for compact, hidden, at_two, (at_one, at_three) in zip(worked, kept, relayed, spread, strict=True):
        partial = dot_t(pick(seq, [hidden, at_one, at_two, at_three]), down_t)
        residual = jnp.where(seq == 0, compact, pad_part[None, :])
        at_owner.append(partial + jnp.where(member == 0, residual, 0.0))
    at_owner = jnp.concatenate(at_owner, axis=0).reshape(n_seq, n_member, share, depth)

    summed = [sum_members(at_owner[:3].transpose(1, 0, 2, 3).reshape(n_member, 3 * share, depth)).astype(BF16)]
    summed = summed[0].reshape(3, share, depth)
    last = sum_members(at_owner[3]).astype(BF16)
    ready = jnp.concatenate([summed, last[None]], axis=0)
    arrived = [pick(seq, [ready[i] for i in range(n_seq)])]
    for turn in range(1, n_seq):
        sent = pick(seq, [ready[(i + turn) % n_seq] for i in range(n_seq)])
        arrived.append(lax.ppermute(sent, "seq", [(i, (i + turn) % n_seq) for i in range(n_seq)]))
    parts = [pick(seq, [arrived[(s - i) % n_seq] for s in range(n_seq)]) for i in range(n_seq)]
    return (jnp.concatenate(parts, axis=1), span_grad)


def solution(mesh):
    spread = P(("groups", "seq", "mp", "rep"), None)
    weight = P("seq", ("mp", "rep"))
    placed = (spread, spread, P("groups"), P(), P(), P(), P(), P(), weight, weight, weight)
    return jax.shard_map(
        local, mesh=mesh, in_specs=placed, out_specs=(spread, spread), check_vma=False
    )
```

time: 212 us -> 138 us (0.65)
  waiting for transfers between devices: 77.9 us -> 28 us
  between operations: 14.5 us -> 1.65 us
  Pallas kernels: 0 us -> 12.3 us
  matrix products: 30.1 us -> 18.4 us
  starting transfers between devices: 62.4 us -> 53.9 us
  other arithmetic: 16.5 us -> 8.48 us
  blocking collectives: 0 us -> 7.23 us
  local copies, waits for them, and re-layouts: 9.62 us -> 7.12 us
    all_to_all x3 -> x0, starting transfers between devices: 40.2 us -> none  [the longest x1 32.4 us: local(): spread = lax.all_to_all(done, 'seq', 0, 0, tiled=True)]
    ppermute x11 -> x36, starting transfers between devices: 19.5 us -> 50.5 us  [the longest x5 15.4 us: local(): relayed.append(lax.ppermute(hidden, 'seq', [(0, 2)]))]
    ppermute x11 -> x36, waiting for transfers between devices: 49.3 us -> 28 us  [the longest x3 10.8 us: local(): lax.ppermute(mine, 'seq', [(j, 0)])]
    all_to_all x3 -> x0, waiting for transfers between devices: 19.7 us -> none  [the longest x1 8.87 us: local(): got = lax.all_to_all(partial, MEMBER, 0, 0, tiled=True)]
    pallas_call x0 -> x3, Pallas kernels: none -> 12.3 us  [the longest x1 5.53 us: encode_direct(): pl.pallas_call(encode_kernel, out_shape=jax.ShapeDtypeStruct((CAP, width)...]
    all_gather x1 -> x0, waiting for transfers between devices: 8.88 us -> none  [local(): gathered = lax.all_gather(column, MEMBER, axis=0)]
    dot_general x13 -> x15, matrix products: 21.6 us -> 12.8 us  [dot(): return jnp.dot(a, b, preferred_element_type=F32)]
    all_gather x0 -> x1, blocking collectives: none -> 7.23 us  [local(): lax.all_gather(rows, MEMBER, axis=0, tiled=True)]
  transfers between devices with their start and end apart: 16 -> 37, of which waited for: 11 -> 11; matrix products, arithmetic and copies ran while one was open for 13% -> 22% of each run, Pallas kernels for 0% -> 9%
where the time goes in v2:
time: 138 us; the launch traced here: 137 us
  starting transfers between devices  53.9 us (39%)
  waiting for transfers between devices  28 us (20%)
  matrix products  18.4 us (13%)
  Pallas kernels  12.3 us (9%)
  other arithmetic  8.48 us (6%)
  blocking collectives  7.23 us (5%)
  local copies, waits for them, and re-layouts  7.12 us (5%)
  between operations  1.65 us (1%)
    ppermute x5, starting transfers between devices, local(): relayed.append(lax.ppermute(hidden, 'seq', [(0, 2)]))  15.4 us
    dot_general x15, matrix products, dot(): return jnp.dot(a, b, preferred_element_type=F32)  12.8 us
    ppermute x3, waiting for transfers between devices, local(): lax.ppermute(mine, 'seq', [(j, 0)])  10.8 us
    ppermute x3, starting transfers between devices, local(): lax.ppermute(sent, 'seq', [(i, (i + turn) % n_seq) for i in range(n_seq)])  8.58 us
    all_gather x1, blocking collectives, local(): lax.all_gather(rows, MEMBER, axis=0, tiled=True)  7.23 us
    ppermute x10, waiting for transfers between devices, swap(): return lax.ppermute(value, axis, [(0, 1), (1, 0)])  7.18 us
    ppermute x10, starting transfers between devices, swap(): return lax.ppermute(value, axis, [(0, 1), (1, 0)])  5.98 us
    dot_general x5, matrix products, dot_t(): lax.dot_general(a, b, (((1,), (1,)), ((), ())), preferred_element_type=F32)  5.54 us
  transfers between devices with their start and end apart: 37, of which 11 were waited for; matrix products, arithmetic and copies ran while one was open for 22% of the time, Pallas kernels for 9%

profile of v2, /device:TPU:0, one launch (start us, length us, event | category | flops | bytes accessed | tf_op | source)
XLA Modules:
  0.0 137.1 jit_solution(1510955448989700373)
XLA Ops:
  0.6 3.3 %collective-permute-start.1 = (bf16[128,1024]{1,0:T(8,128)(2,1)}, bf16[128,1024]{1,0:T(8,128)(2,1)}, u32[]{:S(2)}, u32[]{:S(2)}) collective-permute-start(bf16[128,1024]{1,0:T(8,128)(2,1)} %x_ref.1), channel_id=1, source_target_pairs={{0,1},{1,2},{2,3},{3,4},{4,5},{5,6},{6,7},{7,8},{8,9},{9,10},{10,1... | collective-permute-start | bytes 786440 | tf_op jit(solution)/shard_map/ppermute | solution.py:319
  4.0 2.0 %collective-permute-start = (s32[8,128]{1,0:T(8,128)S(1)}, s32[8,128]{1,0:T(8,128)S(1)}, u32[]{:S(2)}, u32[]{:S(2)}) collective-permute-start(s32[8,128]{1,0:T(8,128)S(1)} %broadcast_in_dim.62), channel_id=1, source_target_pairs={{0,1},{1,0},{2,3},{3,2},{4,5},{5,4},{6,7},{7,6},{8,9},{9,8},{10,11... | collective-permute-start | bytes 12296 | tf_op jit(solution)/shard_map/ppermute | solution.py:35
  6.0 1.3 multiply_reduce_fusion.4
  8.5 1.3 pad_add_fusion.at_ref
  9.8 5.4 %pad_terms.1 = f32[2,1536]{1,0:T(2,128)} custom-call(s32[3]{0:T(128)} %pad_add_fusion.at_ref, f32[1,3072]{1,0:T(1,128)} %bitcast.120, f32[1,4096]{1,0:T(1,128)} %bitcast.121, bf16[1024,1536]{1,0:T(8,128)(2,1)} %gate_ref.1, bf16[1024,1536]{1,0:T(8,128)(2,1)} %up_ref.1), custom_call_target="tpu_custom_call" | custom-call | flops 100000000 | bytes 6500000 | tf_op jit(solution)/shard_map/pad_terms/pallas_call | solution.py:157
  15.2 1.3 collective-permute-start.4
  16.5 1.3 collective-permute-start.3
  17.8 1.3 collective-permute-start.2
  19.1 1.4 %plan.1 = (bf16[64,128]{1,0:T(8,128)(2,1)S(1)}, f32[64,256]{1,0:T(8,128)S(1)}, bf16[192,256]{1,0:T(8,128)(2,1)S(1)}, bf16[512,384]{1,0:T(8,128)(2,1)S(1)}, bf16[192,1024]{1,0:T(8,128)(2,1)S(1)}) custom-call(s32[3]{0:T(128)S(1)} %copy-done.6, s32[1,512]{1,0:T(1,128)S(1)} %bitcast.112, bf16[128,1024]{1,0:T(8,128)(2,1)S(1)} %copy-done.4), custom_call_target="tpu_custom_call" | custom-call | flops 60000000 | bytes 1500000 | tf_op jit(solution)/shard_map/plan/pallas_call | solution.py:224
  20.6 2.9 %copy-done.1 = bf16[1024,3072]{1,0:T(8,128)(2,1)S(1)} copy-done((bf16[1024,3072]{1,0:T(8,128)(2,1)S(1)}, bf16[1024,3072]{1,0:T(8,128)(2,1)}, u32[]{:S(2)}) %copy-start.1) | copy-done | bytes 6291480
  23.5 5.5 %encode.1 = bf16[64,1024]{1,0:T(8,128)(2,1)S(1)} custom-call(bf16[128,1024]{1,0:T(8,128)(2,1)S(1)} %copy-done.3, bf16[128,1024]{1,0:T(8,128)(2,1)} %collective-permute-done.1.halo_ref, bf16[64,128]{1,0:T(8,128)(2,1)S(1)} %get-tuple-element.39.sel_ref, f32[64,256]{1,0:T(8,128)S(1)} %get-tuple-element.40.bias_ref, f32[1,1024]{1,0:T(1,128)S(1)} %bitcast.111, ...), custom_call_target="tpu_custom_call" | custom-call | flops 1500000000 | bytes 9000000 | tf_op jit(solution)/shard_map/encode/pallas_call | solution.py:265
  29.0 7.2 %all_gather.3 = bf16[256,1024]{1,0:T(8,128)(2,1)S(1)} all-gather(bf16[64,1024]{1,0:T(8,128)(2,1)S(1)} %encode.1), channel_id=1, replica_groups=mesh['groups'=2,'seq'=4,'mp'=2,'rep'=2] {'mp','rep'}, dimensions={0}, use_global_device_ids=true | all-gather | bytes 655360 | tf_op jit(solution)/shard_map/all_gather | solution.py:385
  36.8 1.4 %collective-permute-start.5 = (bf16[96,1024]{1,0:T(8,128)(2,1)S(1)}, bf16[96,1024]{1,0:T(8,128)(2,1)S(1)}, u32[]{:S(2)}, u32[]{:S(2)}) collective-permute-start(bf16[96,1024]{1,0:T(8,128)(2,1)S(1)} %get-tuple-element.83), channel_id=1, source_target_pairs={{4,0},{5,1},{6,2},{7,3},{20,16},{21,17},{22,18},{23,19}} | collective-permute-start | bytes 589832 | tf_op jit(solution)/shard_map/ppermute | solution.py:390
  39.5 1.4 %fusion.8 = bf16[96,1536]{1,0:T(8,128)(2,1)} fusion(bf16[1024,1536]{1,0:T(8,128)(2,1)S(1)} %copy-done.15, f32[96,1536]{1,0:T(8,128)S(1)} %convolution_add_fusion.7, f32[1536]{0:T(1024)S(1)} %get-tuple-element.72, f32[96]{0:T(128)S(1)} %add_rsqrt_fusion.4, f32[1024]{0:T(1024)S(1)} %slice.134, bf16[192,1024]{1,0:T(8,128)(2,1)S(1)} %convolution_convert_fusion), kind=kOutput, calls=%fused_computation.18 | convolution fusion | flops 303562752 | bytes 4240384 | tf_op jit(solution)/shard_map/dot_general | solution.py:23
  41.0 5.3 %collective-permute-done.5 = bf16[96,1024]{1,0:T(8,128)(2,1)S(1)} collective-permute-done((bf16[96,1024]{1,0:T(8,128)(2,1)S(1)}, bf16[96,1024]{1,0:T(8,128)(2,1)S(1)}, u32[]{:S(2)}, u32[]{:S(2)}) %collective-permute-start.5) | collective-permute-done | bytes 196640 | tf_op jit(solution)/shard_map/ppermute | solution.py:390
  46.3 1.3 collective-permute-start.7
  49.4 1.5 %fusion.5 = bf16[128,1536]{1,0:T(8,128)(2,1)} fusion(bf16[1024,1536]{1,0:T(8,128)(2,1)S(1)} %copy-done.15, f32[128,1536]{1,0:T(8,128)S(1)} %convolution_add_fusion.3, f32[1536]{0:T(1024)S(1)} %get-tuple-element.72, f32[128]{0:T(128)S(1)} %add_rsqrt_fusion.3, f32[128,1024]{1,0:T(8,128)S(1)} %fusion.10, f32[1024]{0:T(1024)S(1)} %slice.134), kind=kOutput, calls=%fused_computation.13 | convolution fusion | flops 404619264 | bytes 4860416 | tf_op jit(solution)/shard_map/dot_general | solution.py:23
  50.9 5.5 %collective-permute-done.7 = bf16[96,1024]{1,0:T(8,128)(2,1)} collective-permute-done((bf16[96,1024]{1,0:T(8,128)(2,1)S(1)}, bf16[96,1024]{1,0:T(8,128)(2,1)}, u32[]{:S(2)}, u32[]{:S(2)}) %collective-permute-start.7) | collective-permute-done | bytes 196640 | tf_op jit(solution)/shard_map/ppermute | solution.py:390
  57.3 1.4 %collective-permute-start.9 = (bf16[96,1024]{1,0:T(8,128)(2,1)}, bf16[96,1024]{1,0:T(8,128)(2,1)S(1)}, u32[]{:S(2)}, u32[]{:S(2)}) collective-permute-start(bf16[96,1024]{1,0:T(8,128)(2,1)} %copy-done.19), channel_id=1, source_target_pairs={{12,0},{13,1},{14,2},{15,3},{28,16},{29,17},{30,18},{31,19}} | collective-permute-start | bytes 589832 | tf_op jit(solution)/shard_map/ppermute | solution.py:390
  58.7 1.3 collective-permute-start.10
  60.0 1.3 collective-permute-start.12
  62.3 1.6 %fusion.18 = f32[128,1024]{1,0:T(8,128)S(1)} fusion(bf16[96,1024]{1,0:T(8,128)(2,1)} %collective-permute-done.8, bf16[96,1024]{1,0:T(8,128)(2,1)} %collective-permute-done.7, bf16[96,1024]{1,0:T(8,128)(2,1)} %copy-done.23, bf16[96,1024]{1,0:T(8,128)(2,1)} %copy-done.22, bf16[512,384]{1,0:T(8,128)(2,1)} %copy-done.5), kind=kOutput, calls=%fused_computation.37 | convolution fusion | flops 103809024 | bytes 1409024 | tf_op jit(solution)/shard_map/dot_general | solution.py:23
  63.9 3.8 %collective-permute-done.10 = bf16[96,1536]{1,0:T(8,128)(2,1)S(1)} collective-permute-done((bf16[96,1536]{1,0:T(8,128)(2,1)}, bf16[96,1536]{1,0:T(8,128)(2,1)S(1)}, u32[]{:S(2)}, u32[]{:S(2)}) %collective-permute-start.10) | collective-permute-done | bytes 294944 | tf_op jit(solution)/shard_map/ppermute | solution.py:417
  71.2 6.5 %collective-permute-start.15 = (bf16[128,1536]{1,0:T(8,128)(2,1)S(1)}, bf16[128,1536]{1,0:T(8,128)(2,1)S(1)}, u32[]{:S(2)}, u32[]{:S(2)}) collective-permute-start(bf16[128,1536]{1,0:T(8,128)(2,1)S(1)} %fusion.4), channel_id=1, source_target_pairs={{0,8},{1,9},{2,10},{3,11},{16,24},{17,25},{18,26},{19,27}} | collective-permute-start | bytes 1179656 | tf_op jit(solution)/shard_map/ppermute | solution.py:417
  85.0 2.7 %collective-permute-start.20 = (bf16[96,1536]{1,0:T(8,128)(2,1)S(1)}, bf16[96,1536]{1,0:T(8,128)(2,1)S(1)}, u32[]{:S(2)}, u32[]{:S(2)}) collective-permute-start(bf16[96,1536]{1,0:T(8,128)(2,1)S(1)} %fusion.7), channel_id=1, source_target_pairs={{0,8},{1,9},{2,10},{3,11},{16,24},{17,25},{18,26},{19,27}} | collective-permute-start | bytes 884744 | tf_op jit(solution)/shard_map/ppermute | solution.py:417
  92.4 3.6 %collective-permute-start.27 = (bf16[64,1536]{1,0:T(8,128)(2,1)S(1)}, bf16[64,1536]{1,0:T(8,128)(2,1)S(1)}, u32[]{:S(2)}, u32[]{:S(2)}) collective-permute-start(bf16[64,1536]{1,0:T(8,128)(2,1)S(1)} %fusion.9), channel_id=1, source_target_pairs={{0,8},{1,9},{2,10},{3,11},{16,24},{17,25},{18,26},{19,27}} | collective-permute-start | bytes 589832 | tf_op jit(solution)/shard_map/ppermute | solution.py:417
  99.4 1.3 collective-permute-start.26
  100.7 4.5 %collective-permute-start.25 = (bf16[32,1024]{1,0:T(8,128)(2,1)S(1)}, bf16[32,1024]{1,0:T(8,128)(2,1)S(1)}, u32[]{:S(2)}, u32[]{:S(2)}) collective-permute-start(bf16[32,1024]{1,0:T(8,128)(2,1)S(1)} %get-tuple-element.81), channel_id=1, source_target_pairs={{0,4},{4,8},{8,12},{1,5},{5,9},{9,13},{2,6},{6,10},{10,14},{3,7},{... | collective-permute-start | bytes 196616 | tf_op jit(solution)/shard_map/ppermute | solution.py:128
  115.1 5.6 %collective-permute-done.24 = bf16[96,1024]{1,0:T(8,128)(2,1)S(1)} collective-permute-done((bf16[96,1024]{1,0:T(8,128)(2,1)S(1)}, bf16[96,1024]{1,0:T(8,128)(2,1)S(1)}, u32[]{:S(2)}, u32[]{:S(2)}) %collective-permute-start.24) | collective-permute-done | bytes 196640 | tf_op jit(solution)/shard_map/ppermute | solution.py:35
  121.6 5.5 %collective-permute-start.34 = (bf16[32,1024]{1,0:T(8,128)(2,1)S(1)}, bf16[32,1024]{1,0:T(8,128)(2,1)S(1)}, u32[]{:S(2)}, u32[]{:S(2)}) collective-permute-start(bf16[32,1024]{1,0:T(8,128)(2,1)S(1)} %get-tuple-element.76), channel_id=1, source_target_pairs={{0,12},{4,0},{8,4},{12,8},{1,13},{5,1},{9,5},{13,9},{2,14},{6,2},{... | collective-permute-start | bytes 196616 | tf_op jit(solution)/shard_map/ppermute | solution.py:440
  127.1 3.1 %collective-permute-start.33 = (bf16[32,1024]{1,0:T(8,128)(2,1)S(1)}, bf16[32,1024]{1,0:T(8,128)(2,1)S(1)}, u32[]{:S(2)}, u32[]{:S(2)}) collective-permute-start(bf16[32,1024]{1,0:T(8,128)(2,1)S(1)} %get-tuple-element.87), channel_id=1, source_target_pairs={{0,8},{4,12},{8,0},{12,4},{1,9},{5,13},{9,1},{13,5},{2,10},{6,14},... | collective-permute-start | bytes 196616 | tf_op jit(solution)/shard_map/ppermute | solution.py:440
  130.9 4.2 %collective-permute-done.33 = bf16[32,1024]{1,0:T(8,128)(2,1)S(1)} collective-permute-done((bf16[32,1024]{1,0:T(8,128)(2,1)S(1)}, bf16[32,1024]{1,0:T(8,128)(2,1)S(1)}, u32[]{:S(2)}, u32[]{:S(2)}) %collective-permute-start.33) | collective-permute-done | bytes 65568 | tf_op jit(solution)/shard_map/ppermute | solution.py:440
  (161 shorter events, 38.3 us)
Async XLA Ops:
  0.6 19.9 %collective-permute-start.1 = (bf16[128,1024]{1,0:T(8,128)(2,1)}, bf16[128,1024]{1,0:T(8,128)(2,1)}, u32[]{:S(2)}, u32[]{:S(2)}) collective-permute-start(bf16[128,1024]{1,0:T(8,128)(2,1)} %x_ref.1), channel_id=1, source_target_pairs={{0,1},{1,2},{2,3},{3,4},{4,5},{5,6},{6,7},{7,8},{8,9},{9,10},{10,1... | collective-permute-start | bytes 786440 | tf_op jit(solution)/shard_map/ppermute | solution.py:319
  4.0 3.9 %collective-permute-start = (s32[8,128]{1,0:T(8,128)S(1)}, s32[8,128]{1,0:T(8,128)S(1)}, u32[]{:S(2)}, u32[]{:S(2)}) collective-permute-start(s32[8,128]{1,0:T(8,128)S(1)} %broadcast_in_dim.62), channel_id=1, source_target_pairs={{0,1},{1,0},{2,3},{3,2},{4,5},{5,4},{6,7},{7,6},{8,9},{9,8},{10,11... | collective-permute-start | bytes 12296 | tf_op jit(solution)/shard_map/ppermute | solution.py:35
  15.2 21.3 %collective-permute-start.4 = (f32[2,1536]{1,0:T(2,128)}, f32[2,1536]{1,0:T(2,128)S(1)}, u32[]{:S(2)}, u32[]{:S(2)}) collective-permute-start(f32[2,1536]{1,0:T(2,128)} %pad_terms.1), channel_id=1, source_target_pairs={{12,0},{13,1},{14,2},{15,3},{28,16},{29,17},{30,18},{31,19}} | collective-permute-start | bytes 36872 | tf_op jit(solution)/shard_map/ppermute | solution.py:381
  16.5 20.1 %collective-permute-start.3 = (f32[2,1536]{1,0:T(2,128)}, f32[2,1536]{1,0:T(2,128)S(1)}, u32[]{:S(2)}, u32[]{:S(2)}) collective-permute-start(f32[2,1536]{1,0:T(2,128)} %pad_terms.1), channel_id=1, source_target_pairs={{8,0},{9,1},{10,2},{11,3},{24,16},{25,17},{26,18},{27,19}} | collective-permute-start | bytes 36872 | tf_op jit(solution)/shard_map/ppermute | solution.py:381
  17.8 18.8 %collective-permute-start.2 = (f32[2,1536]{1,0:T(2,128)}, f32[2,1536]{1,0:T(2,128)S(1)}, u32[]{:S(2)}, u32[]{:S(2)}) collective-permute-start(f32[2,1536]{1,0:T(2,128)} %pad_terms.1), channel_id=1, source_target_pairs={{4,0},{5,1},{6,2},{7,3},{20,16},{21,17},{22,18},{23,19}} | collective-permute-start | bytes 36872 | tf_op jit(solution)/shard_map/ppermute | solution.py:381
  36.8 9.5 %collective-permute-start.5 = (bf16[96,1024]{1,0:T(8,128)(2,1)S(1)}, bf16[96,1024]{1,0:T(8,128)(2,1)S(1)}, u32[]{:S(2)}, u32[]{:S(2)}) collective-permute-start(bf16[96,1024]{1,0:T(8,128)(2,1)S(1)} %get-tuple-element.83), channel_id=1, source_target_pairs={{4,0},{5,1},{6,2},{7,3},{20,16},{21,17},{22,18},{23,19}} | collective-permute-start | bytes 589832 | tf_op jit(solution)/shard_map/ppermute | solution.py:390
  46.3 10.2 %collective-permute-start.7 = (bf16[96,1024]{1,0:T(8,128)(2,1)S(1)}, bf16[96,1024]{1,0:T(8,128)(2,1)}, u32[]{:S(2)}, u32[]{:S(2)}) collective-permute-start(bf16[96,1024]{1,0:T(8,128)(2,1)S(1)} %get-tuple-element.83), channel_id=1, source_target_pairs={{8,0},{9,1},{10,2},{11,3},{24,16},{25,17},{26,18},{27,19}} | collective-permute-start | bytes 589832 | tf_op jit(solution)/shard_map/ppermute | solution.py:390
  56.5 5.8 %collective-permute-start.8 = (bf16[96,1024]{1,0:T(8,128)(2,1)}, bf16[96,1024]{1,0:T(8,128)(2,1)}, u32[]{:S(2)}, u32[]{:S(2)}) collective-permute-start(bf16[96,1024]{1,0:T(8,128)(2,1)} %collective-permute-done.7), channel_id=1, source_target_pairs={{0,1},{1,0},{2,3},{3,2},{4,5},{5,4},{6,7},{7,6},{8,9},{9,8},{10,11... | collective-permute-start | bytes 589832 | tf_op jit(solution)/shard_map/ppermute | solution.py:35
  57.3 20.3 %collective-permute-start.9 = (bf16[96,1024]{1,0:T(8,128)(2,1)}, bf16[96,1024]{1,0:T(8,128)(2,1)S(1)}, u32[]{:S(2)}, u32[]{:S(2)}) collective-permute-start(bf16[96,1024]{1,0:T(8,128)(2,1)} %copy-done.19), channel_id=1, source_target_pairs={{12,0},{13,1},{14,2},{15,3},{28,16},{29,17},{30,18},{31,19}} | collective-permute-start | bytes 589832 | tf_op jit(solution)/shard_map/ppermute | solution.py:390
  58.7 9.0 %collective-permute-start.10 = (bf16[96,1536]{1,0:T(8,128)(2,1)}, bf16[96,1536]{1,0:T(8,128)(2,1)S(1)}, u32[]{:S(2)}, u32[]{:S(2)}) collective-permute-start(bf16[96,1536]{1,0:T(8,128)(2,1)} %fusion.8), channel_id=1, source_target_pairs={{0,8},{1,9},{2,10},{3,11},{16,24},{17,25},{18,26},{19,27}} | collective-permute-start | bytes 884744 | tf_op jit(solution)/shard_map/ppermute | solution.py:417
  60.0 20.3 %collective-permute-start.12 = (bf16[128,1536]{1,0:T(8,128)(2,1)}, bf16[128,1536]{1,0:T(8,128)(2,1)S(1)}, u32[]{:S(2)}, u32[]{:S(2)}) collective-permute-start(bf16[128,1536]{1,0:T(8,128)(2,1)} %fusion.5), channel_id=1, source_target_pairs={{0,8},{1,9},{2,10},{3,11},{16,24},{17,25},{18,26},{19,27}} | collective-permute-start | bytes 1179656 | tf_op jit(solution)/shard_map/ppermute | solution.py:417
  67.7 15.1 %collective-permute-start.14 = (bf16[96,1536]{1,0:T(8,128)(2,1)S(1)}, bf16[96,1536]{1,0:T(8,128)(2,1)S(1)}, u32[]{:S(2)}, u32[]{:S(2)}) collective-permute-start(bf16[96,1536]{1,0:T(8,128)(2,1)S(1)} %collective-permute-done.10), channel_id=1, source_target_pairs={{8,12},{9,13},{10,14},{11,15},{24,28},{25,29},{26,30},{27,31}} | collective-permute-start | bytes 884744 | tf_op jit(solution)/shard_map/ppermute | solution.py:119
  68.4 14.4 %collective-permute-start.13 = (bf16[96,1536]{1,0:T(8,128)(2,1)S(1)}, bf16[96,1536]{1,0:T(8,128)(2,1)S(1)}, u32[]{:S(2)}, u32[]{:S(2)}) collective-permute-start(bf16[96,1536]{1,0:T(8,128)(2,1)S(1)} %collective-permute-done.10), channel_id=1, source_target_pairs={{8,4},{9,5},{10,6},{11,7},{24,20},{25,21},{26,22},{27,23}} | collective-permute-start | bytes 884744 | tf_op jit(solution)/shard_map/ppermute | solution.py:119
  71.2 17.7 %collective-permute-start.15 = (bf16[128,1536]{1,0:T(8,128)(2,1)S(1)}, bf16[128,1536]{1,0:T(8,128)(2,1)S(1)}, u32[]{:S(2)}, u32[]{:S(2)}) collective-permute-start(bf16[128,1536]{1,0:T(8,128)(2,1)S(1)} %fusion.4), channel_id=1, source_target_pairs={{0,8},{1,9},{2,10},{3,11},{16,24},{17,25},{18,26},{19,27}} | collective-permute-start | bytes 1179656 | tf_op jit(solution)/shard_map/ppermute | solution.py:417
  80.4 9.9 %collective-permute-start.17 = (bf16[128,1536]{1,0:T(8,128)(2,1)S(1)}, bf16[128,1536]{1,0:T(8,128)(2,1)S(1)}, u32[]{:S(2)}, u32[]{:S(2)}) collective-permute-start(bf16[128,1536]{1,0:T(8,128)(2,1)S(1)} %collective-permute-done.12), channel_id=1, source_target_pairs={{8,12},{9,13},{10,14},{11,15},{24,28},{25,29},{26,30},{27,31}} | collective-permute-start | bytes 1179656 | tf_op jit(solution)/shard_map/ppermute | solution.py:119
  81.1 9.2 %collective-permute-start.16 = (bf16[128,1536]{1,0:T(8,128)(2,1)S(1)}, bf16[128,1536]{1,0:T(8,128)(2,1)S(1)}, u32[]{:S(2)}, u32[]{:S(2)}) collective-permute-start(bf16[128,1536]{1,0:T(8,128)(2,1)S(1)} %collective-permute-done.12), channel_id=1, source_target_pairs={{8,4},{9,5},{10,6},{11,7},{24,20},{25,21},{26,22},{27,23}} | collective-permute-start | bytes 1179656 | tf_op jit(solution)/shard_map/ppermute | solution.py:119
  85.0 12.2 %collective-permute-start.20 = (bf16[96,1536]{1,0:T(8,128)(2,1)S(1)}, bf16[96,1536]{1,0:T(8,128)(2,1)S(1)}, u32[]{:S(2)}, u32[]{:S(2)}) collective-permute-start(bf16[96,1536]{1,0:T(8,128)(2,1)S(1)} %fusion.7), channel_id=1, source_target_pairs={{0,8},{1,9},{2,10},{3,11},{16,24},{17,25},{18,26},{19,27}} | collective-permute-start | bytes 884744 | tf_op jit(solution)/shard_map/ppermute | solution.py:417
  88.9 11.8 %collective-permute-start.19 = (bf16[128,1536]{1,0:T(8,128)(2,1)S(1)}, bf16[128,1536]{1,0:T(8,128)(2,1)S(1)}, u32[]{:S(2)}, u32[]{:S(2)}) collective-permute-start(bf16[128,1536]{1,0:T(8,128)(2,1)S(1)} %collective-permute-done.15), channel_id=1, source_target_pairs={{8,12},{9,13},{10,14},{11,15},{24,28},{25,29},{26,30},{27,31}} | collective-permute-start | bytes 1179656 | tf_op jit(solution)/shard_map/ppermute | solution.py:119
  89.5 15.7 %collective-permute-start.18 = (bf16[128,1536]{1,0:T(8,128)(2,1)S(1)}, bf16[128,1536]{1,0:T(8,128)(2,1)S(1)}, u32[]{:S(2)}, u32[]{:S(2)}) collective-permute-start(bf16[128,1536]{1,0:T(8,128)(2,1)S(1)} %collective-permute-done.15), channel_id=1, source_target_pairs={{8,4},{9,5},{10,6},{11,7},{24,20},{25,21},{26,22},{27,23}} | collective-permute-start | bytes 1179656 | tf_op jit(solution)/shard_map/ppermute | solution.py:119
  92.4 7.0 %collective-permute-start.27 = (bf16[64,1536]{1,0:T(8,128)(2,1)S(1)}, bf16[64,1536]{1,0:T(8,128)(2,1)S(1)}, u32[]{:S(2)}, u32[]{:S(2)}) collective-permute-start(bf16[64,1536]{1,0:T(8,128)(2,1)S(1)} %fusion.9), channel_id=1, source_target_pairs={{0,8},{1,9},{2,10},{3,11},{16,24},{17,25},{18,26},{19,27}} | collective-permute-start | bytes 589832 | tf_op jit(solution)/shard_map/ppermute | solution.py:417
  97.2 9.9 %collective-permute-start.22 = (bf16[96,1536]{1,0:T(8,128)(2,1)S(1)}, bf16[96,1536]{1,0:T(8,128)(2,1)S(1)}, u32[]{:S(2)}, u32[]{:S(2)}) collective-permute-start(bf16[96,1536]{1,0:T(8,128)(2,1)S(1)} %collective-permute-done.20), channel_id=1, source_target_pairs={{8,12},{9,13},{10,14},{11,15},{24,28},{25,29},{26,30},{27,31}} | collective-permute-start | bytes 884744 | tf_op jit(solution)/shard_map/ppermute | solution.py:119
  97.9 9.9 %collective-permute-start.21 = (bf16[96,1536]{1,0:T(8,128)(2,1)S(1)}, bf16[96,1536]{1,0:T(8,128)(2,1)S(1)}, u32[]{:S(2)}, u32[]{:S(2)}) collective-permute-start(bf16[96,1536]{1,0:T(8,128)(2,1)S(1)} %collective-permute-done.20), channel_id=1, source_target_pairs={{8,4},{9,5},{10,6},{11,7},{24,20},{25,21},{26,22},{27,23}} | collective-permute-start | bytes 884744 | tf_op jit(solution)/shard_map/ppermute | solution.py:119
  99.4 10.0 %collective-permute-start.26 = (bf16[32,1024]{1,0:T(8,128)(2,1)S(1)}, bf16[32,1024]{1,0:T(8,128)(2,1)S(1)}, u32[]{:S(2)}, u32[]{:S(2)}) collective-permute-start(bf16[32,1024]{1,0:T(8,128)(2,1)S(1)} %get-tuple-element.80), channel_id=1, source_target_pairs={{4,0},{8,4},{12,8},{5,1},{9,5},{13,9},{6,2},{10,6},{14,10},{7,3},{... | collective-permute-start | bytes 196616 | tf_op jit(solution)/shard_map/ppermute | solution.py:127
  100.7 8.7 %collective-permute-start.25 = (bf16[32,1024]{1,0:T(8,128)(2,1)S(1)}, bf16[32,1024]{1,0:T(8,128)(2,1)S(1)}, u32[]{:S(2)}, u32[]{:S(2)}) collective-permute-start(bf16[32,1024]{1,0:T(8,128)(2,1)S(1)} %get-tuple-element.81), channel_id=1, source_target_pairs={{0,4},{4,8},{8,12},{1,5},{5,9},{9,13},{2,6},{6,10},{10,14},{3,7},{... | collective-permute-start | bytes 196616 | tf_op jit(solution)/shard_map/ppermute | solution.py:128
  105.3 4.1 %collective-permute-start.29 = (bf16[64,1536]{1,0:T(8,128)(2,1)S(1)}, bf16[64,1536]{1,0:T(8,128)(2,1)S(1)}, u32[]{:S(2)}, u32[]{:S(2)}) collective-permute-start(bf16[64,1536]{1,0:T(8,128)(2,1)S(1)} %collective-permute-done.27), channel_id=1, source_target_pairs={{8,12},{9,13},{10,14},{11,15},{24,28},{25,29},{26,30},{27,31}} | collective-permute-start | bytes 589832 | tf_op jit(solution)/shard_map/ppermute | solution.py:119
  109.3 3.4 %collective-permute-start.23 = (bf16[2,96,1024]{2,1,0:T(8,128)(2,1)S(1)}, bf16[2,96,1024]{2,1,0:T(8,128)(2,1)S(1)}, u32[]{:S(2)}, u32[]{:S(2)}) collective-permute-start(bf16[2,96,1024]{2,1,0:T(8,128)(2,1)S(1)} %fusion.32), channel_id=1, source_target_pairs={{0,1},{1,0},{2,3},{3,2},{4,5},{5,4},{6,7},{7,6},{8,9},{9,8},{10,11... | collective-permute-start | bytes 1179656 | tf_op jit(solution)/shard_map/ppermute | solution.py:35
  111.4 18.8 %collective-permute-start.36 = (bf16[32,1024]{1,0:T(8,128)(2,1)S(1)}, bf16[32,1024]{1,0:T(8,128)(2,1)S(1)}, u32[]{:S(2)}, u32[]{:S(2)}) collective-permute-start(bf16[32,1024]{1,0:T(8,128)(2,1)S(1)} %fusion.74), channel_id=1, source_target_pairs={{0,2},{2,0},{1,3},{3,1},{4,6},{6,4},{5,7},{7,5},{8,10},{10,8},{9,1... | collective-permute-start | bytes 196616 | tf_op jit(solution)/shard_map/ppermute | solution.py:35
  112.9 7.8 %collective-permute-start.24 = (bf16[96,1024]{1,0:T(8,128)(2,1)S(1)}, bf16[96,1024]{1,0:T(8,128)(2,1)S(1)}, u32[]{:S(2)}, u32[]{:S(2)}) collective-permute-start(bf16[96,1024]{1,0:T(8,128)(2,1)S(1)} %fusion.58), channel_id=1, source_target_pairs={{0,2},{2,0},{1,3},{3,1},{4,6},{6,4},{5,7},{7,5},{8,10},{10,8},{9,1... | collective-permute-start | bytes 589832 | tf_op jit(solution)/shard_map/ppermute | solution.py:35
  114.0 7.6 %collective-permute-start.31 = (bf16[32,1024]{1,0:T(8,128)(2,1)S(1)}, bf16[32,1024]{1,0:T(8,128)(2,1)S(1)}, u32[]{:S(2)}, u32[]{:S(2)}) collective-permute-start(bf16[32,1024]{1,0:T(8,128)(2,1)S(1)} %fusion.73), channel_id=1, source_target_pairs={{0,2},{2,0},{1,3},{3,1},{4,6},{6,4},{5,7},{7,5},{8,10},{10,8},{9,1... | collective-permute-start | bytes 196616 | tf_op jit(solution)/shard_map/ppermute | solution.py:35
  121.6 9.3 %collective-permute-start.34 = (bf16[32,1024]{1,0:T(8,128)(2,1)S(1)}, bf16[32,1024]{1,0:T(8,128)(2,1)S(1)}, u32[]{:S(2)}, u32[]{:S(2)}) collective-permute-start(bf16[32,1024]{1,0:T(8,128)(2,1)S(1)} %get-tuple-element.76), channel_id=1, source_target_pairs={{0,12},{4,0},{8,4},{12,8},{1,13},{5,1},{9,5},{13,9},{2,14},{6,2},{... | collective-permute-start | bytes 196616 | tf_op jit(solution)/shard_map/ppermute | solution.py:440
  127.1 8.0 %collective-permute-start.33 = (bf16[32,1024]{1,0:T(8,128)(2,1)S(1)}, bf16[32,1024]{1,0:T(8,128)(2,1)S(1)}, u32[]{:S(2)}, u32[]{:S(2)}) collective-permute-start(bf16[32,1024]{1,0:T(8,128)(2,1)S(1)} %get-tuple-element.87), channel_id=1, source_target_pairs={{0,8},{4,12},{8,0},{12,4},{1,9},{5,13},{9,1},{13,5},{2,10},{6,14},... | collective-permute-start | bytes 196616 | tf_op jit(solution)/shard_map/ppermute | solution.py:440
  130.2 6.1 %collective-permute-start.32 = (bf16[32,1024]{1,0:T(8,128)(2,1)S(1)}, bf16[32,1024]{1,0:T(8,128)(2,1)S(1)}, u32[]{:S(2)}, u32[]{:S(2)}) collective-permute-start(bf16[32,1024]{1,0:T(8,128)(2,1)S(1)} %get-tuple-element.88), channel_id=1, source_target_pairs={{0,4},{4,8},{8,12},{12,0},{1,5},{5,9},{9,13},{13,1},{2,6},{6,10},{... | collective-permute-start | bytes 196616 | tf_op jit(solution)/shard_map/ppermute | solution.py:440
  (29 other events, 282.5 us)

commit v3 on v2

--- a/solution.py
+++ b/solution.py
@@ -1,3 +1,5 @@
+import functools
+
 import jax
 import jax.numpy as jnp
 from jax import lax
@@ -11,8 +13,13 @@
 LANE = 24
 LANE_ROWS = 32
 HALF = 96
-VMEM_LIMIT = 56 << 20
-CHUNKS = ((0, (0, 1, 2)), (1, (3, 4, 5, 6)), (2, (7, 8, 9, 10)), (3, (11, 12, 13)), (3, (14, 15)))
+GROUP = 32
+VMEM = pl.BlockSpec(memory_space=pltpu.VMEM)
+ANY = pl.BlockSpec(memory_space=pl.ANY)
+HBM = pl.BlockSpec(memory_space=pltpu.HBM)
+COST = {'plan': 20000000000, 'tick0': 4000000000, 'tick1': 2000000000, 'tick2': 2000000000, 'tick3': 2000000000, 'tickz': 4000000000, 'early_core': 4000000000}
+OPT = {'late_first': 1, 'grads': 1, 'pads': 'rows', 'lag': 1}
+CHUNKS = ((0, 3), (3, 7), (7, 12), (12, 16))
 PART = ("seq", "mp", "rep")
 MEMBER = ("mp", "rep")
 F32 = jnp.float32
@@ -35,22 +42,37 @@
     return lax.ppermute(value, axis, [(0, 1), (1, 0)])
 
 
-def pick(index, values):
-    out = values[-1]
-    for i in range(len(values) - 2, -1, -1):
-        out = jnp.where(index == i, values[i], out)
-    return out
-
-
-def sum_members(value):
-    mp, rep = lax.axis_index("mp"), lax.axis_index("rep")
-    rows = value.reshape((2, 2) + value.shape[1:])
-    keep = pick(rep, [rows[:, 0], rows[:, 1]])
-    send = pick(rep, [rows[:, 1], rows[:, 0]])
-    keep = keep + swap(send.astype(BF16), "rep").astype(F32)
-    own = pick(mp, [keep[0], keep[1]])
-    other = pick(mp, [keep[1], keep[0]])
-    return own + swap(other.astype(BF16), "mp").astype(F32)
+def kernel_call(kernel, out_shape, *operands, name, after=(), streamed=0, scratch=()):
+    count = len(operands)
+    body = lambda *refs: kernel(*refs[:count], *refs[count + len(after) :])
+    return pl.pallas_call(
+        body,
+        out_shape=out_shape,
+        in_specs=[VMEM] * (count - streamed) + [HBM] * streamed + [ANY] * len(after),
+        out_specs=jax.tree.map(lambda _: VMEM, out_shape),
+        scratch_shapes=scratch,
+        compiler_params=pltpu.CompilerParams(vmem_limit_bytes=24 << 20),
+        cost_estimate=pl.CostEstimate(flops=COST.get(name, 0), bytes_accessed=0, transcendentals=0),
+        name=name,
+    )(*operands, *after)
+
+
+def tick(name, *after):
+    if name not in COST:
+        return after[-1]
+
+    def kernel(out_ref):
+        out_ref[...] = jnp.zeros_like(out_ref)
+
+    return kernel_call(kernel, array(8, 128, F32), name=name, after=after)
+
+
+def tie(values, token):
+    return lax.optimization_barrier((values, token))
+
+
+def array(rows, columns, dtype):
+    return jax.ShapeDtypeStruct((rows, columns), dtype)
 
 
 def rms_scale(values, gain):
@@ -119,60 +141,31 @@
     return lax.ppermute(value, "seq", [(2, 1)]), lax.ppermute(value, "seq", [(2, 3)])
 
 
-def exchange_sums(sums):
-    own = sums.shape[0] - 2 * LANE_ROWS
-    n_seq = lax.axis_size("seq")
-    up = [(i, i + 1) for i in range(n_seq - 1)]
-    down = [(i + 1, i) for i in range(n_seq - 1)]
-    from_after = lax.ppermute(sums[own : own + LANE_ROWS], "seq", down)
-    from_before = lax.ppermute(sums[own + LANE_ROWS :], "seq", up)
-    return from_before, from_after
-
-
-def route_sums(sums, from_both):
-    own = sums.shape[0] - 2 * LANE_ROWS
-    first, last = (value.astype(F32) for value in from_both)
-    block = sums[:own].astype(F32)
-    block = jnp.concatenate(
-        [block[:LANE_ROWS] + first, block[LANE_ROWS:-LANE_ROWS], block[-LANE_ROWS:] + last], axis=0
-    )
-    return sum_members(block.reshape(4, own // 4, -1)).astype(BF16)
-
-
-def pad_kernel(at_ref, pad_ref, gain_ref, gate_ref, up_ref, out_ref):
-    high, low = split_high_low(jnp.broadcast_to(pad_ref[...] * gain_ref[...], (8, pad_ref.shape[1])))
+def lanes_kernel(member_ref, cotangent_ref, own_ref, before_ref, after_ref):
+    own = own_ref.shape[0]
+    sums = dot(member_ref[...], cotangent_ref[...]).astype(BF16)
+    own_ref[...] = sums[:own]
+    before_ref[...] = sums[own : own + LANE_ROWS]
+    after_ref[...] = sums[own + LANE_ROWS :]
+
+
+def pad_kernel(pad_ref, gain_ref, gate_ref, up_ref, out_ref):
+    seq = lax.axis_index("seq")
+    depth = gate_ref.shape[0]
+    pad = pad_ref[:, pl.ds(pl.multiple_of(jnp.maximum(seq - 1, 0) * depth, depth), depth)]
+    gain = gain_ref[:, pl.ds(pl.multiple_of(seq * depth, depth), depth)]
+    high, low = split_high_low(jnp.broadcast_to(pad * gain, (8, depth)))
     both = jnp.concatenate([high, low], axis=0)
     for at, weight_ref in enumerate((gate_ref, up_ref)):
         terms = dot(both, weight_ref[...])
-        terms = terms[:1] + terms[8:9]
-        out_ref[at : at + 1] = jnp.where(at_ref[2] == 0, 0.0, terms)
-
-
-def pad_terms_of(at, pad_vector, main_gain, gate_w, up_w):
-    depth, columns = gate_w.shape
-    block = 4 * HEAD
-    pad_block = pl.BlockSpec((1, depth), lambda i, at: (0, jnp.maximum(at[2] - 1, 0)))
-    gain_block = pl.BlockSpec((1, depth), lambda i, at: (0, at[2]))
-    weight_block = pl.BlockSpec((depth, block), lambda i, at: (0, i))
-    return pl.pallas_call(
-        pad_kernel,
-        out_shape=jax.ShapeDtypeStruct((2, columns), F32),
-        grid_spec=pltpu.PrefetchScalarGridSpec(
-            num_scalar_prefetch=1,
-            grid=(columns // block,),
-            in_specs=[pad_block, gain_block, weight_block, weight_block],
-            out_specs=pl.BlockSpec((2, block), lambda i, at: (0, i)),
-        ),
-        compiler_params=pltpu.CompilerParams(vmem_limit_bytes=VMEM_LIMIT),
-        cost_estimate=pl.CostEstimate(flops=100_000_000, bytes_accessed=6_500_000, transcendentals=0),
-        name="pad_terms",
-    )(at, pad_vector.reshape(1, -1), main_gain.reshape(1, -1), gate_w, up_w)
-
-
-def plan_kernel(at_ref, starts_ref, cotangent_ref, sel_ref, bias_ref, pack_ref, place_ref, sums_ref):
-    device, member, owner = at_ref[0], at_ref[1], at_ref[2]
+        out_ref[at : at + 1] = jnp.where(seq == 0, 0.0, terms[:1] + terms[8:9])
+
+
+def plan_kernel(starts_ref, sel_ref, bias_ref, pack_ref, place_ref, member_ref):
+    owner, core = lax.axis_index("seq"), lax.axis_index("rep")
+    device = owner * 4 + lax.axis_index("mp") * 2 + core
     n_span = starts_ref.shape[1]
-    length = cotangent_ref.shape[0]
+    length = sel_ref.shape[1]
     begin = device * length
     row = starts_ref[...]
     column = jnp.transpose(jnp.broadcast_to(row, (length, n_span)))
@@ -190,14 +183,13 @@
     bias_ref[...] = jnp.where(allowed, 0.0, -1e30)
 
     span_index = earlier + start - 1
-    n_row = sums_ref.shape[0]
+    n_row = member_ref.shape[0]
     own = n_row - 2 * LANE_ROWS
     at = lax.broadcasted_iota(jnp.int32, (n_row, length), 0)
     target = jnp.where(
         at < own, owner * own + at, jnp.where(at < own + LANE_ROWS, owner * own - LANE_ROWS - own, owner * own - LANE_ROWS) + at
     )
-    member_of = jnp.where(span_index == target, 1.0, 0.0).astype(BF16)
-    sums_ref[...] = dot(member_of, cotangent_ref[...]).astype(BF16)
+    member_ref[...] = jnp.where(span_index == target, 1.0, 0.0).astype(BF16)
 
     block = owner * 4 + lax.broadcasted_iota(jnp.int32, (n_span, 4 * CAP), 1) // CAP
     first = jnp.sum(jnp.where(column[:, :1] < block * length, 1.0, 0.0), axis=0, keepdims=True).astype(jnp.int32)
@@ -212,32 +204,30 @@
     near = jnp.minimum((span // 32 + 1) // 4, 3)
     lies = span - before
     side = jnp.where(lies >= HALF, 1, 0)
-    lies = lies - side * HALF + (side ^ (member % 2)) * HALF + (around - near + 1) * (2 * HALF)
+    lies = lies - side * HALF + (side ^ core) * HALF + (around - near + 1) * (2 * HALF)
     lanes = lax.broadcasted_iota(jnp.int32, place_ref.shape, 1)
     place_ref[...] = jnp.where(lanes == lies, 1.0, 0.0).astype(BF16)
 
 
-def plan(at, boundaries, cotangent, span_own):
+def plan(boundaries, length, span_own):
     n_span = boundaries.shape[0]
-    length, width = cotangent.shape
-    shapes = ((CAP, length), (CAP, 2 * length), (2 * HALF, 4 * CAP), (n_span, 4 * HALF), (span_own + 2 * LANE_ROWS, width))
-    return pl.pallas_call(
+    return kernel_call(
         plan_kernel,
-        out_shape=tuple(jax.ShapeDtypeStruct(s, F32 if i == 1 else BF16) for i, s in enumerate(shapes)),
-        in_specs=[
-            pl.BlockSpec(memory_space=pltpu.SMEM),
-            pl.BlockSpec(memory_space=pltpu.VMEM),
-            pl.BlockSpec(memory_space=pltpu.VMEM),
-        ],
-        out_specs=tuple(pl.BlockSpec(memory_space=pltpu.VMEM) for _ in shapes),
-        compiler_params=pltpu.CompilerParams(vmem_limit_bytes=16 << 20),
-        cost_estimate=pl.CostEstimate(flops=60_000_000, bytes_accessed=1_500_000, transcendentals=0),
+        (
+            array(CAP, length, BF16),
+            array(CAP, 2 * length, F32),
+            array(2 * HALF, 4 * CAP, BF16),
+            array(n_span, 4 * HALF, BF16),
+            array(span_own + 2 * LANE_ROWS, length, BF16),
+        ),
+        boundaries.reshape(1, n_span),
         name="plan",
-    )(at, boundaries.reshape(1, n_span), cotangent)
+    )
 
 
 def encode_kernel(x_ref, halo_ref, sel_ref, bias_ref, gain_ref, qkv_ref, o_ref, out_ref):
-    length, width = x_ref.shape
+    width = x_ref.shape[1]
+    wide = 2 * HEAD
     gain = gain_ref[...]
     sel = sel_ref[...]
     bias = bias_ref[...]
@@ -245,7 +235,6 @@
     picked = dot(sel, normed).astype(BF16)
     normed = jnp.concatenate([rms_scale(halo_ref[...].astype(F32), gain).astype(BF16), normed], axis=0)
     mixed = []
-    wide = 2 * HEAD
     for at in range(0, width, wide):
         queries = dot(picked, qkv_ref[:, at : at + wide]).astype(BF16)
         keys = dot(normed, qkv_ref[:, width + at : width + at + wide]).astype(BF16)
@@ -260,17 +249,135 @@
     out_ref[...] = total.astype(BF16)
 
 
-def encode_direct(x, halo, sel, bias, enc_gain, w_qkv, w_out):
-    length, width = x.shape
-    return pl.pallas_call(
-        encode_kernel,
-        out_shape=jax.ShapeDtypeStruct((CAP, width), BF16),
-        in_specs=[pl.BlockSpec(memory_space=pltpu.VMEM)] * 7,
-        out_specs=pl.BlockSpec(memory_space=pltpu.VMEM),
-        compiler_params=pltpu.CompilerParams(vmem_limit_bytes=32 << 20),
-        cost_estimate=pl.CostEstimate(flops=1_500_000_000, bytes_accessed=9_000_000, transcendentals=200_000),
-        name="encode",
-    )(x, halo, sel, bias, enc_gain.reshape(1, width), w_qkv, w_out)
+def pair_kernel(rows_ref, came_ref, out_ref):
+    chip = lax.axis_index("mp")
+    out_ref[:CAP] = jnp.where(chip == 0, rows_ref[...], came_ref[...])
+    out_ref[CAP:] = jnp.where(chip == 0, came_ref[...], rows_ref[...])
+
+
+def pack_kernel(pack_ref, pair_ref, came_ref, mine_ref, other_ref):
+    core = lax.axis_index("rep")
+    even = jnp.where(core == 0, pair_ref[...], came_ref[...])
+    odd = jnp.where(core == 0, came_ref[...], pair_ref[...])
+    blocks = [even[:CAP], odd[:CAP], even[CAP:], odd[CAP:]]
+    packed = dot(pack_ref[...], jnp.concatenate(blocks, axis=0)).astype(BF16)
+    mine_ref[...] = jnp.where(core == 0, packed[:HALF], packed[HALF:])
+    other_ref[...] = jnp.where(core == 0, packed[HALF:], packed[:HALF])
+
+
+def near_of(group):
+    return min((group + 1) // 4, 3)
+
+
+def hidden_kernel(low, high, place_ref, *refs):
+    *half_refs, pad_ref, gain_ref, gate_ref, up_ref, term1_ref, term2_ref, term3_ref, hidden_ref, row_ref = refs
+    width = row_ref.shape[1]
+    base = max(near_of(low) - 1, 0)
+    row = []
+    while low < high:
+        near = near_of(low)
+        end = min(high, 4 * near + 3) if near < 3 else high
+        total = 0.0
+        for seq in (near - 1, near):
+            for side in range(2 if seq >= 0 else 0):
+                lanes = ((seq - near + 1) * 2 + side) * HALF
+                place = place_ref[low * GROUP : end * GROUP, lanes : lanes + HALF]
+                total += dot(place, half_refs[(seq - base) * 2 + side][...])
+        row.append(total)
+        low = end
+    row = jnp.concatenate(row, axis=0)
+    pad = pad_ref[...]
+    total = jnp.sum(row * row, axis=1, keepdims=True) + jnp.sum(pad * pad)
+    scale = lax.rsqrt(total / (width + pad.shape[1]) + 1e-05)
+    main_in = (row * scale * gain_ref[:, :width]).astype(BF16)
+    terms = term1_ref[...] + term2_ref[...] + term3_ref[...]
+    gate = dot(main_in, gate_ref[...]) + scale * terms[:1]
+    upward = dot(main_in, up_ref[...]) + scale * terms[1:2]
+    hidden_ref[...] = (gate / (1.0 + jnp.exp(-gate)) * upward).astype(BF16)
+    row_ref[...] = row.astype(BF16)
+
+
+def hidden_at_zero(*args):
+    pl.when(lax.axis_index("seq") == 0)(lambda: hidden_kernel(*args))
+
+
+def down_kernel(zero_ref, one_ref, two_ref, three_ref, down_ref, row_ref, pad_ref, out_ref):
+    seq = lax.axis_index("seq")
+    depth = down_ref.shape[0]
+    low = jnp.where(seq == 0, zero_ref[...], one_ref[...])
+    high = jnp.where(seq == 2, two_ref[...], three_ref[...])
+    partial = dot_t(jnp.where(seq < 2, low, high), down_ref[...])
+    pad = pad_ref[:, pl.ds(pl.multiple_of(jnp.maximum(seq - 1, 0) * depth, depth), depth)]
+    wide = jnp.where(seq == 0, row_ref[...].astype(F32), pad)
+    first = (lax.axis_index("mp") == 0) & (lax.axis_index("rep") == 0)
+    out_ref[...] = partial + jnp.where(first, wide, 0.0)
+
+
+def groups_of(refs):
+    return [ref.at[at : at + GROUP] for ref in refs for at in range(0, ref.shape[0], GROUP)]
+
+
+def core_step_kernel(count, *refs):
+    core = lax.axis_index("rep")
+    groups = groups_of(refs[:count])
+    outs = groups_of(refs[count:])
+    for at, out in enumerate(outs):
+        out[...] = jnp.where(core == 0, groups[2 * at + 1][...], groups[2 * at][...]).astype(BF16)
+
+
+def chip_step_kernel(count, *refs):
+    *came_refs, own_ref, other_ref = refs[count:]
+    core, chip = lax.axis_index("rep"), lax.axis_index("mp")
+    groups = groups_of(refs[:count])
+    came = groups_of(came_refs)
+    for at in range(len(groups) // 4):
+        first, second = (
+            jnp.where(core == 0, groups[4 * at + 2 * i][...], groups[4 * at + 2 * i + 1][...]).astype(F32)
+            + came[2 * at + i][...].astype(F32)
+            for i in range(2)
+        )
+        rows = slice(at * GROUP, (at + 1) * GROUP)
+        own_ref[rows] = jnp.where(chip == 0, first, second)
+        other_ref[rows] = jnp.where(chip == 0, second, first).astype(BF16)
+
+
+def add_kernel(own_ref, came_ref, *out_refs):
+    for at, out_ref in enumerate(out_refs):
+        rows = slice(at * GROUP, (at + 1) * GROUP)
+        out_ref[...] = (own_ref[rows] + came_ref[rows].astype(F32)).astype(BF16)
+
+
+def sums_kernel(sums_ref, before_ref, after_ref, out_ref):
+    own = out_ref.shape[0]
+    out_ref[...] = sums_ref[:own]
+    out_ref[:LANE_ROWS] = (sums_ref[:LANE_ROWS].astype(F32) + before_ref[...].astype(F32)).astype(BF16)
+    last = slice(own - LANE_ROWS, own)
+    out_ref[last] = (sums_ref[last].astype(F32) + after_ref[...].astype(F32)).astype(BF16)
+
+
+def turn_kernel(own_ref, came_ref, *refs):
+    early_refs, out_refs = refs[:3], refs[3:]
+    seq = lax.axis_index("seq")
+    late = (own_ref[...] + came_ref[...].astype(F32)).astype(BF16)
+    groups = [ref[...] for ref in early_refs] + [late]
+    for turn, out_ref in enumerate(out_refs):
+        owner = (seq + turn) % 4
+        value = groups[3]
+        for at in range(3):
+            value = jnp.where(owner == at, groups[at], value)
+        out_ref[...] = value
+
+
+def join_kernel(*refs):
+    *in_refs, out_ref = refs
+    seq = lax.axis_index("seq")
+    depth = in_refs[0].shape[1]
+    for maker in range(4):
+        turn = (seq - maker + 4) % 4
+        value = in_refs[3][...]
+        for at in range(3):
+            value = jnp.where(turn == at, in_refs[at][...], value)
+        out_ref[:, maker * depth : (maker + 1) * depth] = value
 
 
 def split_high_low(values):
@@ -320,11 +427,24 @@
 
     direct = is_direct() and depth == width
     if direct:
-        same_seq = swap(jnp.full((8, 128), seq, jnp.int32), "rep")[0, 0]
-        at = jnp.stack([device, lax.axis_index(MEMBER), same_seq]).astype(jnp.int32)
-        pad_terms = pad_terms_of(at, pad_vector, main_gain, gate_w, up_w)
-        sel, bias, pack, where, sums = plan(at, boundaries, cotangent, n_member * share)
-        rows = encode_direct(byte_states, halo, sel, bias, enc_gain, w_qkv, w_out)
+        pad_row, gain_row = pad_vector.reshape(1, -1), main_gain.reshape(1, -1)
+        sel, bias, pack, where, member_of = plan(boundaries, length, n_member * share)
+        pad_terms = kernel_call(
+            pad_kernel, array(2, columns, F32), pad_row, gain_row, gate_w, up_w, name="pad_terms", after=(sel,)
+        )
+        rows = kernel_call(
+            encode_kernel,
+            array(CAP, width, BF16),
+            byte_states,
+            halo,
+            sel,
+            bias,
+            enc_gain.reshape(1, width),
+            w_qkv,
+            w_out,
+            name="encode",
+            after=(pad_terms,) if OPT.get("pads_first", 1) else (),
+        )
     else:
         wide_gain = main_gain[width:]
         pad_in = jnp.concatenate([jnp.zeros((width,), F32), pad_vector * wide_gain])
@@ -378,68 +498,160 @@
         main_out = spread.transpose(1, 0, 2).reshape(share, main_width)
         return (main_out, span_grad)
 
-    pad_parts = [lax.ppermute(pad_terms, "seq", [(j, 0)]) for j in range(1, n_seq)]
-
-    member = lax.axis_index(MEMBER)
-    core = lax.axis_index("rep")
-    packed = dot(pack, lax.all_gather(rows, MEMBER, axis=0, tiled=True)).astype(BF16)
-    packed, pad_parts = lax.optimization_barrier((packed, pad_parts))
-    pad_gate, pad_up = sum(pad_parts)[:1], sum(pad_parts)[1:]
-    halves = [packed[:HALF], packed[HALF:]]
-    mine = jnp.where(core == 0, halves[0], halves[1])
-    came = [mine] + [lax.ppermute(mine, "seq", [(j, 0)]) for j in range(1, n_seq)]
-    planes = [jnp.concatenate([mine, jnp.where(core == 0, halves[1], halves[0])], axis=0)]
-
-    worked, kept, relayed, spread = [], [], [], []
-    for index, (near, groups) in enumerate(CHUNKS):
-        while len(planes) <= near:
-            value, kept[-1] = lax.optimization_barrier((came[len(planes)], kept[-1]))
-            planes.append(jnp.concatenate([value, swap(value, "rep")], axis=0))
-        low = groups[0] * share
-        high = low + len(groups) * share
-        if near:
-            compact = dot(where[low:high], jnp.concatenate([planes[near - 1], planes[near]], axis=0))
-        else:
-            compact = packed[low:high].astype(F32)
-        if index == 1:
-            compact, kept[0] = lax.optimization_barrier((compact, kept[0]))
-        if index >= 2:
-            compact, relayed[index - 2] = lax.optimization_barrier((compact, relayed[index - 2]))
-            spread.append(relay(relayed[index - 2]))
-        if index >= 3:
-            compact, spread[index - 3] = lax.optimization_barrier((compact, spread[index - 3]))
-        scale, main_in = scaled(compact)
-        gate = dot(main_in, gate_w) + scale * pad_gate
-        upward = dot(main_in, up_w) + scale * pad_up
-        hidden = (jax.nn.silu(gate) * upward).astype(BF16)
-        worked.append(compact)
-        kept.append(hidden)
+    from_chip = swap(rows, "mp")
+    if OPT.get("pads") == "rows":
+        pad_terms, rows = tie(pad_terms, rows)
+    terms = [lax.ppermute(pad_terms, "seq", [(j, 0)]) for j in range(1, n_seq)]
+    pair = kernel_call(pair_kernel, array(2 * CAP, width, BF16), rows, from_chip, name="pair")
+    mine, other = kernel_call(pack_kernel, (array(HALF, width, BF16),) * 2, pack, pair, swap(pair, "rep"), name="pack")
+    planes = [(mine, other)]
+    came = [lax.ppermute(mine, "seq", [(j, 0)]) for j in range(1, n_seq)]
+
+    def over_cores(values, name):
+        quarters = sum(value.shape[0] for value in values) // GROUP // 4
+        sent = kernel_call(
+            functools.partial(core_step_kernel, len(values)),
+            (array(2 * GROUP, depth, BF16),) * quarters,
+            *values,
+            name=name + "_core",
+        )
+        return kernel_call(
+            functools.partial(chip_step_kernel, len(values)),
+            (array(quarters * GROUP, depth, F32), array(quarters * GROUP, depth, BF16)),
+            *values,
+            *(swap(value, "rep") for value in sent),
+            name=name + "_chip",
+        )
+
+    hiddens, row_parts, relayed, spread, parts = [], [], [], [], []
+
+    def make_hidden(index, *after):
+        if OPT.get("lean") and index:
+            after = after[-1:]
+        low, high = CHUNKS[index]
+        halves = [half for plane in planes[max(near_of(low) - 1, 0) : near_of(high - 1) + 1] for half in plane]
+        count = (high - low) * share
+        hidden, row = kernel_call(
+            functools.partial(hidden_at_zero, low, high),
+            (array(count, columns, BF16), array(count, width, BF16)),
+            where,
+            *halves,
+            pad_row,
+            gain_row,
+            gate_w,
+            up_w,
+            *terms,
+            name=f"hidden{index}",
+            after=after,
+        )
+        hiddens.append(hidden)
+        row_parts.append(row)
         relayed.append(lax.ppermute(hidden, "seq", [(0, 2)]))
-    sums, relayed[-2] = lax.optimization_barrier((sums, relayed[-2]))
-    from_both = exchange_sums(sums)
-    spread.append(relay(relayed[-2]))
-    spread.append(relay(relayed[-1]))
-    from_both, spread[-1] = lax.optimization_barrier((from_both, spread[-1]))
-    span_grad = route_sums(sums, from_both)
-
-    at_owner = []
-    pad_part = lax.dynamic_slice_in_dim(pad_vector, jnp.maximum(seq - 1, 0) * depth, depth, 0)
-    for compact, hidden, at_two, (at_one, at_three) in zip(worked, kept, relayed, spread, strict=True):
-        partial = dot_t(pick(seq, [hidden, at_one, at_two, at_three]), down_t)
-        residual = jnp.where(seq == 0, compact, pad_part[None, :])
-        at_owner.append(partial + jnp.where(member == 0, residual, 0.0))
-    at_owner = jnp.concatenate(at_owner, axis=0).reshape(n_seq, n_member, share, depth)
-
-    summed = [sum_members(at_owner[:3].transpose(1, 0, 2, 3).reshape(n_member, 3 * share, depth)).astype(BF16)]
-    summed = summed[0].reshape(3, share, depth)
-    last = sum_members(at_owner[3]).astype(BF16)
-    ready = jnp.concatenate([summed, last[None]], axis=0)
-    arrived = [pick(seq, [ready[i] for i in range(n_seq)])]
+
+    def make_part(index, *after):
+        at_one, at_three = spread[index]
+        count = row_parts[index].shape[0]
+        parts.append(
+            kernel_call(
+                down_kernel,
+                array(count, depth, F32),
+                hiddens[index],
+                at_one,
+                relayed[index],
+                at_three,
+                down_t,
+                row_parts[index],
+                pad_row,
+                name=f"down{index}",
+                after=after,
+            )
+        )
+
+    def take(index, token):
+        arrived, token = tie(came[index], token)
+        planes.append((arrived, swap(arrived, "rep")))
+        return token
+
+    def pass_on(index, token):
+        relayed[index], token = tie(relayed[index], token)
+        spread.append(relay(relayed[index]))
+        return relayed[index], token
+
+    n_chunk = len(CHUNKS)
+    early = sum(high <= 12 for _, high in CHUNKS)
+    n_chunk = len(CHUNKS)
+    early = sum(high <= 12 for _, high in CHUNKS)
+    make_hidden(0)
+    token = take(2, take(1, take(0, tick("tickz", hiddens[0]))))
+    ahead = OPT.get("ahead", n_chunk - 1)
+    for index in range(1, ahead + 1):
+        make_hidden(index, token)
+        token = hiddens[index]
+    grads = OPT.get("grads", 2)
+    for index in range(n_chunk):
+        after = pass_on(index, tick(f"tickx{index}", token))
+        token = after[1]
+        if ahead + 1 + index < n_chunk:
+            make_hidden(ahead + 1 + index, *after)
+            token = hiddens[-1]
+        token = tick(f"tick{index}", token)
+        ready_part = index - OPT.get("lag", 1)
+        if ready_part >= 0:
+            make_part(ready_part, token, *after[:1])
+            token = parts[-1]
+        if index == grads:
+            sums, to_before, to_after = kernel_call(
+                lanes_kernel,
+                (array(n_member * share, width, BF16), array(LANE_ROWS, width, BF16), array(LANE_ROWS, width, BF16)),
+                member_of,
+                cotangent,
+                name="lanes",
+                after=(token,),
+            )
+            up = [(i, i + 1) for i in range(n_seq - 1)]
+            down = [(i + 1, i) for i in range(n_seq - 1)]
+            from_both = lax.ppermute(to_after, "seq", up), lax.ppermute(to_before, "seq", down)
+            token = sums
+    while len(parts) < early:
+        make_part(len(parts), token)
+        token = parts[-1]
+    block = kernel_call(
+        sums_kernel, array(n_member * share, width, BF16), sums, *from_both, name="span_sums", after=(token,)
+    )
+    values = [*parts[:early], block]
+    own, sent = over_cores(values, "early")
+    from_mp = swap(sent, "mp")
+    token = sent
+    while len(parts) < n_chunk - 1:
+        make_part(len(parts), token)
+        token = parts[-1]
+    late_first = OPT.get("late_first", 0)
+
+    def add_early(*after):
+        *ready, span_grad = kernel_call(
+            add_kernel, (array(GROUP, depth, BF16),) * 4, own, from_mp, name="early_add", after=after
+        )
+        return ready, span_grad
+
+    if not late_first:
+        ready, span_grad = add_early(token)
+        token = ready[0]
+    if len(parts) < n_chunk:
+        make_part(n_chunk - 1, tick("tick6", token))
+    late_own, late_sent = over_cores(parts[early:], "late")
+    if late_first:
+        ready, span_grad = add_early(late_sent)
+    own, sent = late_own, late_sent
+
+    turned = kernel_call(
+        turn_kernel, (array(GROUP, depth, BF16),) * n_seq, own, swap(sent, "mp"), *ready, name="turn"
+    )
+    arrived = [turned[0]]
     for turn in range(1, n_seq):
-        sent = pick(seq, [ready[(i + turn) % n_seq] for i in range(n_seq)])
-        arrived.append(lax.ppermute(sent, "seq", [(i, (i + turn) % n_seq) for i in range(n_seq)]))
-    parts = [pick(seq, [arrived[(s - i) % n_seq] for s in range(n_seq)]) for i in range(n_seq)]
-    return (jnp.concatenate(parts, axis=1), span_grad)
+        pairs = [(i, (i + turn) % n_seq) for i in range(n_seq)]
+        arrived.append(lax.ppermute(turned[turn], "seq", pairs))
+    main_out = kernel_call(join_kernel, array(share, main_width, BF16), *arrived, name="join")
+    return (main_out, span_grad)
 
 
 def solution(mesh):

time: 138 us -> 108 us (0.78)
  matrix products: 18.4 us -> 0 us
  waiting for transfers between devices: 28 us -> 39.1 us
  starting transfers between devices: 53.9 us -> 43.3 us
  other arithmetic: 8.48 us -> 0 us
  Pallas kernels: 12.3 us -> 19.6 us
  blocking collectives: 7.23 us -> 0 us
  local copies, waits for them, and re-layouts: 7.12 us -> 4.67 us
    dot_general x20 -> x0, matrix products: 18.4 us -> none  [the longest x15 12.8 us: dot(): return jnp.dot(a, b, preferred_element_type=F32)]
    ppermute x16 -> x15, starting transfers between devices: 37.8 us -> 28.1 us  [the longest x3 10.1 us: local(): arrived.append(lax.ppermute(turned[turn], 'seq', pairs))]
    pallas_call x3 -> x27, Pallas kernels: 12.3 us -> 19.6 us  [kernel_call(): pl.pallas_call(body, out_shape=out_shape, in_specs=[VMEM] * (count - stre...]
    all_gather x1 -> x0, blocking collectives: 7.23 us -> none  [local(): lax.all_gather(rows, MEMBER, axis=0, tiled=True)]
    ppermute x16 -> x15, waiting for transfers between devices: 20.8 us -> 27 us  [the longest x4 10.4 us: make_hidden(): relayed.append(lax.ppermute(hidden, 'seq', [(0, 2)]))]
    ppermute x10 -> x12, waiting for transfers between devices: 7.18 us -> 12 us  [swap(): return lax.ppermute(value, axis, [(0, 1), (1, 0)])]
    rsqrt x5 -> x0, other arithmetic: 2.9 us -> none  [scaled(): scale = lax.rsqrt(squares / main_width + 1e-05)]
    reduce_sum x6 -> x0, other arithmetic: 1.89 us -> none  [the longest x1 1.29 us: local(): pad_square = jnp.sum(pad_vector * pad_vector)]
  transfers between devices with their start and end apart: 37 -> 36, of which waited for: 11 -> 17; matrix products, arithmetic and copies ran while one was open for 22% -> 0% of each run, Pallas kernels for 9% -> 13%
where the time goes in v3:
time: 108 us
  starting transfers between devices  43.3 us (40%)
  waiting for transfers between devices  39.1 us (36%)
  Pallas kernels  19.6 us (18%)
  local copies, waits for them, and re-layouts  4.67 us (4%)
  between operations  1.18 us (1%)
    pallas_call x27, Pallas kernels, kernel_call(): pl.pallas_call(body, out_shape=out_shape, in_specs=[VMEM] * (count - stre...  19.6 us
    ppermute x12, waiting for transfers between devices, swap(): return lax.ppermute(value, axis, [(0, 1), (1, 0)])  12 us
    ppermute x4, waiting for transfers between devices, make_hidden(): relayed.append(lax.ppermute(hidden, 'seq', [(0, 2)]))  10.4 us
    ppermute x3, starting transfers between devices, local(): arrived.append(lax.ppermute(turned[turn], 'seq', pairs))  10.1 us
    ppermute x3, waiting for transfers between devices, local(): came = [lax.ppermute(mine, 'seq', [(j, 0)]) for j in range(1, n_seq)]  8.59 us
    ppermute x12, starting transfers between devices, swap(): return lax.ppermute(value, axis, [(0, 1), (1, 0)])  7.18 us
    ppermute x4, starting transfers between devices, make_hidden(): relayed.append(lax.ppermute(hidden, 'seq', [(0, 2)]))  5.35 us
    unnamed x22, local copies, waits for them, and re-layouts  4.67 us
  transfers between devices with their start and end apart: 36, of which 17 were waited for; matrix products, arithmetic and copies ran while one was open for 0% of the time, Pallas kernels for 13%

profile of v3, /device:TPU:0, one launch (start us, length us, event | category | flops | bytes accessed | tf_op | source)
XLA Modules:
  0.0 107.8 jit_solution(1632896276497684526)
XLA Ops:
  0.6 2.4 %collective-permute-start = (bf16[128,1024]{1,0:T(8,128)(2,1)}, bf16[128,1024]{1,0:T(8,128)(2,1)S(1)}, u32[]{:S(2)}, u32[]{:S(2)}) collective-permute-start(bf16[128,1024]{1,0:T(8,128)(2,1)} %refs_0_.1), channel_id=1, source_target_pairs={{0,1},{1,2},{2,3},{3,4},{4,5},{5,6},{6,7},{7,8},{8,9},{9,10},{10,1... | collective-permute-start | bytes 786440 | tf_op jit(solution)/shard_map/ppermute | solution.py:426
  7.5 2.0 %copy-done.3 = bf16[1024,3072]{1,0:T(8,128)(2,1)S(1)} copy-done((bf16[1024,3072]{1,0:T(8,128)(2,1)S(1)}, bf16[1024,3072]{1,0:T(8,128)(2,1)}, u32[]{:S(2)}) %copy-start.3) | copy-done | bytes 6291480
  9.5 4.4 %encode.1.refs_0_ = bf16[64,1024]{1,0:T(8,128)(2,1)S(1)} custom-call(bf16[128,1024]{1,0:T(8,128)(2,1)S(1)} %copy-done.7, bf16[128,1024]{1,0:T(8,128)(2,1)S(1)} %collective-permute-done.refs_1_, bf16[64,128]{1,0:T(8,128)(2,1)S(1)} %get-tuple-element.54.refs_4_.refs_2_, f32[64,256]{1,0:T(8,128)S(1)} %get-tuple-element.55.refs_3_, f32[1,1024]{1,0:T(1,128)S(1)} %bitcast.18, ...), custom_call_target="tpu_custom_call" | custom-call | tf_op jit(solution)/shard_map/encode/pallas_call | solution.py:48
  13.9 2.5 %collective-permute-start.1 = (bf16[64,1024]{1,0:T(8,128)(2,1)S(1)}, bf16[64,1024]{1,0:T(8,128)(2,1)S(1)}, u32[]{:S(2)}, u32[]{:S(2)}) collective-permute-start(bf16[64,1024]{1,0:T(8,128)(2,1)S(1)} %encode.1.refs_0_), channel_id=1, source_target_pairs={{0,2},{2,0},{1,3},{3,1},{4,6},{6,4},{5,7},{7,5},{8,10},{10,8},{9,1... | collective-permute-start | bytes 393224 | tf_op jit(solution)/shard_map/ppermute | solution.py:42
  16.5 3.2 %collective-permute-done.1.refs_1_ = bf16[64,1024]{1,0:T(8,128)(2,1)S(1)} collective-permute-done((bf16[64,1024]{1,0:T(8,128)(2,1)S(1)}, bf16[64,1024]{1,0:T(8,128)(2,1)S(1)}, u32[]{:S(2)}, u32[]{:S(2)}) %collective-permute-start.1) | collective-permute-done | bytes 131104 | tf_op jit(solution)/shard_map/ppermute | solution.py:42
  22.0 1.3 %collective-permute-start.6 = (f32[2,1536]{1,0:T(2,128)S(1)}, f32[2,1536]{1,0:T(2,128)S(1)}, u32[]{:S(2)}, u32[]{:S(2)}) collective-permute-start(f32[2,1536]{1,0:T(2,128)S(1)} %pad_terms.1.refs_7_), channel_id=1, source_target_pairs={{8,0},{9,1},{10,2},{11,3},{24,16},{25,17},{26,18},{27,19}} | collective-permute-start | bytes 36872 | tf_op jit(solution)/shard_map/ppermute | solution.py:504
  23.3 1.3 %collective-permute-start.7 = (f32[2,1536]{1,0:T(2,128)S(1)}, f32[2,1536]{1,0:T(2,128)S(1)}, u32[]{:S(2)}, u32[]{:S(2)}) collective-permute-start(f32[2,1536]{1,0:T(2,128)S(1)} %pad_terms.1.refs_7_), channel_id=1, source_target_pairs={{12,0},{13,1},{14,2},{15,3},{28,16},{29,17},{30,18},{31,19}} | collective-permute-start | bytes 36872 | tf_op jit(solution)/shard_map/ppermute | solution.py:504
  24.9 1.3 %collective-permute-start.4 = (bf16[96,1024]{1,0:T(8,128)(2,1)S(1)}, bf16[96,1024]{1,0:T(8,128)(2,1)S(1)}, u32[]{:S(2)}, u32[]{:S(2)}) collective-permute-start(bf16[96,1024]{1,0:T(8,128)(2,1)S(1)} %get-tuple-element.57.refs_1_), channel_id=1, source_target_pairs={{4,0},{5,1},{6,2},{7,3},{20,16},{21,17},{22,18},{23,19}} | collective-permute-start | bytes 589832 | tf_op jit(solution)/shard_map/ppermute | solution.py:508
  26.2 1.3 %collective-permute-start.3 = (bf16[96,1024]{1,0:T(8,128)(2,1)S(1)}, bf16[96,1024]{1,0:T(8,128)(2,1)S(1)}, u32[]{:S(2)}, u32[]{:S(2)}) collective-permute-start(bf16[96,1024]{1,0:T(8,128)(2,1)S(1)} %get-tuple-element.57.refs_1_), channel_id=1, source_target_pairs={{8,0},{9,1},{10,2},{11,3},{24,16},{25,17},{26,18},{27,19}} | collective-permute-start | bytes 589832 | tf_op jit(solution)/shard_map/ppermute | solution.py:508
  27.6 1.3 %collective-permute-start.9 = (bf16[96,1024]{1,0:T(8,128)(2,1)S(1)}, bf16[96,1024]{1,0:T(8,128)(2,1)S(1)}, u32[]{:S(2)}, u32[]{:S(2)}) collective-permute-start(bf16[96,1024]{1,0:T(8,128)(2,1)S(1)} %get-tuple-element.57.refs_1_), channel_id=1, source_target_pairs={{12,0},{13,1},{14,2},{15,3},{28,16},{29,17},{30,18},{31,19}} | collective-permute-start | bytes 589832 | tf_op jit(solution)/shard_map/ppermute | solution.py:508
  28.9 2.0 %collective-permute-done.7.refs_9_.refs_11_.refs_13_ = f32[2,1536]{1,0:T(2,128)S(1)} collective-permute-done((f32[2,1536]{1,0:T(2,128)S(1)}, f32[2,1536]{1,0:T(2,128)S(1)}, u32[]{:S(2)}, u32[]{:S(2)}) %collective-permute-start.7) | collective-permute-done | bytes 12320 | tf_op jit(solution)/shard_map/ppermute | solution.py:504
  30.8 1.5 %hidden0.1 = (bf16[96,1536]{1,0:T(8,128)(2,1)S(1)}, bf16[96,1024]{1,0:T(8,128)(2,1)S(1)}) custom-call(bf16[512,384]{1,0:T(8,128)(2,1)S(1)} %get-tuple-element.52.refs_0_, bf16[96,1024]{1,0:T(8,128)(2,1)S(1)} %get-tuple-element.57.refs_1_, bf16[96,1024]{1,0:T(8,128)(2,1)S(1)} %get-tuple-element.58.refs_2_, f32[1,3072]{1,0:T(1,128)S(1)} %bitcast.5, ...), custom_call_target="tpu_custom_call" | custom-call | tf_op jit(solution)/shard_map/hidden0/pallas_call | solution.py:48
  32.4 1.4 %collective-permute-start.14 = (bf16[96,1536]{1,0:T(8,128)(2,1)S(1)}, bf16[96,1536]{1,0:T(8,128)(2,1)S(1)}, u32[]{:S(2)}, u32[]{:S(2)}) collective-permute-start(bf16[96,1536]{1,0:T(8,128)(2,1)S(1)} %get-tuple-element.60.refs_0_), channel_id=1, source_target_pairs={{0,8},{1,9},{2,10},{3,11},{16,24},{17,25},{18,26},{19,27}} | collective-permute-start | bytes 884744 | tf_op jit(solution)/shard_map/ppermute | solution.py:549
  33.8 8.6 %collective-permute-done.4.refs_3_.refs_1_ = bf16[96,1024]{1,0:T(8,128)(2,1)S(1)} collective-permute-done((bf16[96,1024]{1,0:T(8,128)(2,1)S(1)}, bf16[96,1024]{1,0:T(8,128)(2,1)S(1)}, u32[]{:S(2)}, u32[]{:S(2)}) %collective-permute-start.4) | collective-permute-done | bytes 196640 | tf_op jit(solution)/shard_map/ppermute | solution.py:508
  43.8 1.5 %hidden1.1 = (bf16[128,1536]{1,0:T(8,128)(2,1)S(1)}, bf16[128,1024]{1,0:T(8,128)(2,1)S(1)}) custom-call(bf16[512,384]{1,0:T(8,128)(2,1)S(1)} %get-tuple-element.52.refs_0_, bf16[96,1024]{1,0:T(8,128)(2,1)S(1)} %get-tuple-element.57.refs_1_, bf16[96,1024]{1,0:T(8,128)(2,1)S(1)} %get-tuple-element.58.refs_2_, ...), custom_call_target="tpu_custom_call" | custom-call | tf_op jit(solution)/shard_map/hidden1/pallas_call | solution.py:48
  45.3 1.3 %collective-permute-start.13 = (bf16[128,1536]{1,0:T(8,128)(2,1)S(1)}, bf16[128,1536]{1,0:T(8,128)(2,1)S(1)}, u32[]{:S(2)}, u32[]{:S(2)}) collective-permute-start(bf16[128,1536]{1,0:T(8,128)(2,1)S(1)} %get-tuple-element.67.refs_14_.refs_0_), channel_id=1, source_target_pairs={{0,8},{1,9},{2,10},{3,11},{16,24},{17,25},{18,26},{19,27}} | collective-permute-start | bytes 1179656 | tf_op jit(solution)/shard_map/ppermute | solution.py:549
  46.7 1.9 %hidden2.1 = (bf16[160,1536]{1,0:T(8,128)(2,1)S(1)}, bf16[160,1024]{1,0:T(8,128)(2,1)S(1)}) custom-call(bf16[512,384]{1,0:T(8,128)(2,1)S(1)} %get-tuple-element.52.refs_0_, bf16[96,1024]{1,0:T(8,128)(2,1)S(1)} %collective-permute-done.4.refs_3_.refs_1_, bf16[96,1024]{1,0:T(8,128)(2,1)S(1)} %collective-permute-done.11.refs_4_.refs_2_, ...), custom_call_target="tpu_custom_call" | custom-call | tf_op jit(solution)/shard_map/hidden2/pallas_call | solution.py:48
  48.6 1.6 %hidden3.1 = (bf16[128,1536]{1,0:T(8,128)(2,1)S(1)}, bf16[128,1024]{1,0:T(8,128)(2,1)S(1)}) custom-call(bf16[512,384]{1,0:T(8,128)(2,1)S(1)} %get-tuple-element.52.refs_0_, bf16[96,1024]{1,0:T(8,128)(2,1)S(1)} %collective-permute-done.3.refs_3_.refs_1_, bf16[96,1024]{1,0:T(8,128)(2,1)S(1)} %collective-permute-done.8.refs_4_.refs_2_, ...), custom_call_target="tpu_custom_call" | custom-call | tf_op jit(solution)/shard_map/hidden3/pallas_call | solution.py:48
  51.5 1.3 %collective-permute-start.17 = (bf16[160,1536]{1,0:T(8,128)(2,1)S(1)}, bf16[160,1536]{1,0:T(8,128)(2,1)S(1)}, u32[]{:S(2)}, u32[]{:S(2)}) collective-permute-start(bf16[160,1536]{1,0:T(8,128)(2,1)S(1)} %get-tuple-element.68.refs_12_.refs_0_), channel_id=1, source_target_pairs={{0,8},{1,9},{2,10},{3,11},{16,24},{17,25},{18,26},{19,27}} | collective-permute-start | bytes 1474568 | tf_op jit(solution)/shard_map/ppermute | solution.py:549
  52.8 1.3 %collective-permute-start.12 = (bf16[128,1536]{1,0:T(8,128)(2,1)S(1)}, bf16[128,1536]{1,0:T(8,128)(2,1)S(1)}, u32[]{:S(2)}, u32[]{:S(2)}) collective-permute-start(bf16[128,1536]{1,0:T(8,128)(2,1)S(1)} %get-tuple-element.70.refs_0_), channel_id=1, source_target_pairs={{0,8},{1,9},{2,10},{3,11},{16,24},{17,25},{18,26},{19,27}} | collective-permute-start | bytes 1179656 | tf_op jit(solution)/shard_map/ppermute | solution.py:549
  54.2 1.9 %collective-permute-done.13.refs_8_.refs_2_ = bf16[128,1536]{1,0:T(8,128)(2,1)S(1)} collective-permute-done((bf16[128,1536]{1,0:T(8,128)(2,1)S(1)}, bf16[128,1536]{1,0:T(8,128)(2,1)S(1)}, u32[]{:S(2)}, u32[]{:S(2)}) %collective-permute-start.13) | collective-permute-done | bytes 393248 | tf_op jit(solution)/shard_map/ppermute | solution.py:549
  59.0 7.6 %collective-permute-done.17.refs_8_.refs_2_ = bf16[160,1536]{1,0:T(8,128)(2,1)S(1)} collective-permute-done((bf16[160,1536]{1,0:T(8,128)(2,1)S(1)}, bf16[160,1536]{1,0:T(8,128)(2,1)S(1)}, u32[]{:S(2)}, u32[]{:S(2)}) %collective-permute-start.17) | collective-permute-done | bytes 491552 | tf_op jit(solution)/shard_map/ppermute | solution.py:549
  68.0 3.6 %collective-permute-start.24 = (bf16[32,1024]{1,0:T(8,128)(2,1)S(1)}, bf16[32,1024]{1,0:T(8,128)(2,1)S(1)}, u32[]{:S(2)}, u32[]{:S(2)}) collective-permute-start(bf16[32,1024]{1,0:T(8,128)(2,1)S(1)} %get-tuple-element.84), channel_id=1, source_target_pairs={{0,4},{4,8},{8,12},{1,5},{5,9},{9,13},{2,6},{6,10},{10,14},{3,7},{... | collective-permute-start | bytes 196616 | tf_op jit(solution)/shard_map/ppermute | solution.py:613
  71.6 1.3 %collective-permute-start.25 = (bf16[32,1024]{1,0:T(8,128)(2,1)S(1)}, bf16[32,1024]{1,0:T(8,128)(2,1)S(1)}, u32[]{:S(2)}, u32[]{:S(2)}) collective-permute-start(bf16[32,1024]{1,0:T(8,128)(2,1)S(1)} %get-tuple-element.85), channel_id=1, source_target_pairs={{4,0},{8,4},{12,8},{5,1},{9,5},{13,9},{6,2},{10,6},{14,10},{7,3},{... | collective-permute-start | bytes 196616 | tf_op jit(solution)/shard_map/ppermute | solution.py:613
  77.6 1.7 %collective-permute-done.25.refs_2_ = bf16[32,1024]{1,0:T(8,128)(2,1)S(1)} collective-permute-done((bf16[32,1024]{1,0:T(8,128)(2,1)S(1)}, bf16[32,1024]{1,0:T(8,128)(2,1)S(1)}, u32[]{:S(2)}, u32[]{:S(2)}) %collective-permute-start.25) | collective-permute-done | bytes 65568 | tf_op jit(solution)/shard_map/ppermute | solution.py:613
  82.3 2.1 %collective-permute-start.32 = (bf16[128,1024]{1,0:T(8,128)(2,1)S(1)}, bf16[128,1024]{1,0:T(8,128)(2,1)S(1)}, u32[]{:S(2)}, u32[]{:S(2)}) collective-permute-start(bf16[128,1024]{1,0:T(8,128)(2,1)S(1)} %get-tuple-element.90.refs_7_), channel_id=1, source_target_pairs={{0,2},{2,0},{1,3},{3,1},{4,6},{6,4},{5,7},{7,5},{8,10},{10,8},{9,1... | collective-permute-start | bytes 786440 | tf_op jit(solution)/shard_map/ppermute | solution.py:42
  85.7 1.3 %collective-permute-done.30.refs_1_ = bf16[64,1024]{1,0:T(8,128)(2,1)S(1)} collective-permute-done((bf16[64,1024]{1,0:T(8,128)(2,1)S(1)}, bf16[64,1024]{1,0:T(8,128)(2,1)S(1)}, u32[]{:S(2)}, u32[]{:S(2)}) %collective-permute-start.30) | collective-permute-done | bytes 131104 | tf_op jit(solution)/shard_map/ppermute | solution.py:42
  87.2 4.3 %collective-permute-done.32.refs_1_ = bf16[128,1024]{1,0:T(8,128)(2,1)S(1)} collective-permute-done((bf16[128,1024]{1,0:T(8,128)(2,1)S(1)}, bf16[128,1024]{1,0:T(8,128)(2,1)S(1)}, u32[]{:S(2)}, u32[]{:S(2)}) %collective-permute-start.32) | collective-permute-done | bytes 262176 | tf_op jit(solution)/shard_map/ppermute | solution.py:42
  92.5 6.9 %collective-permute-start.33 = (bf16[32,1024]{1,0:T(8,128)(2,1)S(1)}, bf16[32,1024]{1,0:T(8,128)(2,1)S(1)}, u32[]{:S(2)}, u32[]{:S(2)}) collective-permute-start(bf16[32,1024]{1,0:T(8,128)(2,1)S(1)} %get-tuple-element.98), channel_id=1, source_target_pairs={{0,4},{4,8},{8,12},{12,0},{1,5},{5,9},{9,13},{13,1},{2,6},{6,10},{... | collective-permute-start | bytes 196616 | tf_op jit(solution)/shard_map/ppermute | solution.py:652
  99.4 2.8 %collective-permute-start.34 = (bf16[32,1024]{1,0:T(8,128)(2,1)S(1)}, bf16[32,1024]{1,0:T(8,128)(2,1)S(1)}, u32[]{:S(2)}, u32[]{:S(2)}) collective-permute-start(bf16[32,1024]{1,0:T(8,128)(2,1)S(1)} %get-tuple-element.99), channel_id=1, source_target_pairs={{0,8},{4,12},{8,0},{12,4},{1,9},{5,13},{9,1},{13,5},{2,10},{6,14},... | collective-permute-start | bytes 196616 | tf_op jit(solution)/shard_map/ppermute | solution.py:652
  102.7 2.0 %collective-permute-done.33.refs_1_ = bf16[32,1024]{1,0:T(8,128)(2,1)S(1)} collective-permute-done((bf16[32,1024]{1,0:T(8,128)(2,1)S(1)}, bf16[32,1024]{1,0:T(8,128)(2,1)S(1)}, u32[]{:S(2)}, u32[]{:S(2)}) %collective-permute-start.33) | collective-permute-done | bytes 65568 | tf_op jit(solution)/shard_map/ppermute | solution.py:652
  104.7 1.7 %collective-permute-done.34.refs_2_ = bf16[32,1024]{1,0:T(8,128)(2,1)S(1)} collective-permute-done((bf16[32,1024]{1,0:T(8,128)(2,1)S(1)}, bf16[32,1024]{1,0:T(8,128)(2,1)S(1)}, u32[]{:S(2)}, u32[]{:S(2)}) %collective-permute-start.34) | collective-permute-done | bytes 65568 | tf_op jit(solution)/shard_map/ppermute | solution.py:652
  (89 shorter events, 26.0 us)
Async XLA Ops:
  0.6 6.9 %collective-permute-start = (bf16[128,1024]{1,0:T(8,128)(2,1)}, bf16[128,1024]{1,0:T(8,128)(2,1)S(1)}, u32[]{:S(2)}, u32[]{:S(2)}) collective-permute-start(bf16[128,1024]{1,0:T(8,128)(2,1)} %refs_0_.1), channel_id=1, source_target_pairs={{0,1},{1,2},{2,3},{3,4},{4,5},{5,6},{6,7},{7,8},{8,9},{9,10},{10,1... | collective-permute-start | bytes 786440 | tf_op jit(solution)/shard_map/ppermute | solution.py:426
  13.9 5.8 %collective-permute-start.1 = (bf16[64,1024]{1,0:T(8,128)(2,1)S(1)}, bf16[64,1024]{1,0:T(8,128)(2,1)S(1)}, u32[]{:S(2)}, u32[]{:S(2)}) collective-permute-start(bf16[64,1024]{1,0:T(8,128)(2,1)S(1)} %encode.1.refs_0_), channel_id=1, source_target_pairs={{0,2},{2,0},{1,3},{3,1},{4,6},{6,4},{5,7},{7,5},{8,10},{10,8},{9,1... | collective-permute-start | bytes 393224 | tf_op jit(solution)/shard_map/ppermute | solution.py:42
  19.8 4.9 %collective-permute-start.2 = (bf16[128,1024]{1,0:T(8,128)(2,1)S(1)}, bf16[128,1024]{1,0:T(8,128)(2,1)S(1)}, u32[]{:S(2)}, u32[]{:S(2)}) collective-permute-start(bf16[128,1024]{1,0:T(8,128)(2,1)S(1)} %pair.1.refs_1_), channel_id=1, source_target_pairs={{0,1},{1,0},{2,3},{3,2},{4,5},{5,4},{6,7},{7,6},{8,9},{9,8},{10,11... | collective-permute-start | bytes 786440 | tf_op jit(solution)/shard_map/ppermute | solution.py:42
  20.8 6.8 %collective-permute-start.5 = (f32[2,1536]{1,0:T(2,128)S(1)}, f32[2,1536]{1,0:T(2,128)S(1)}, u32[]{:S(2)}, u32[]{:S(2)}) collective-permute-start(f32[2,1536]{1,0:T(2,128)S(1)} %pad_terms.1.refs_7_), channel_id=1, source_target_pairs={{4,0},{5,1},{6,2},{7,3},{20,16},{21,17},{22,18},{23,19}} | collective-permute-start | bytes 36872 | tf_op jit(solution)/shard_map/ppermute | solution.py:504
  22.0 6.8 %collective-permute-start.6 = (f32[2,1536]{1,0:T(2,128)S(1)}, f32[2,1536]{1,0:T(2,128)S(1)}, u32[]{:S(2)}, u32[]{:S(2)}) collective-permute-start(f32[2,1536]{1,0:T(2,128)S(1)} %pad_terms.1.refs_7_), channel_id=1, source_target_pairs={{8,0},{9,1},{10,2},{11,3},{24,16},{25,17},{26,18},{27,19}} | collective-permute-start | bytes 36872 | tf_op jit(solution)/shard_map/ppermute | solution.py:504
  23.3 7.5 %collective-permute-start.7 = (f32[2,1536]{1,0:T(2,128)S(1)}, f32[2,1536]{1,0:T(2,128)S(1)}, u32[]{:S(2)}, u32[]{:S(2)}) collective-permute-start(f32[2,1536]{1,0:T(2,128)S(1)} %pad_terms.1.refs_7_), channel_id=1, source_target_pairs={{12,0},{13,1},{14,2},{15,3},{28,16},{29,17},{30,18},{31,19}} | collective-permute-start | bytes 36872 | tf_op jit(solution)/shard_map/ppermute | solution.py:504
  24.9 17.4 %collective-permute-start.4 = (bf16[96,1024]{1,0:T(8,128)(2,1)S(1)}, bf16[96,1024]{1,0:T(8,128)(2,1)S(1)}, u32[]{:S(2)}, u32[]{:S(2)}) collective-permute-start(bf16[96,1024]{1,0:T(8,128)(2,1)S(1)} %get-tuple-element.57.refs_1_), channel_id=1, source_target_pairs={{4,0},{5,1},{6,2},{7,3},{20,16},{21,17},{22,18},{23,19}} | collective-permute-start | bytes 589832 | tf_op jit(solution)/shard_map/ppermute | solution.py:508
  26.2 16.1 %collective-permute-start.3 = (bf16[96,1024]{1,0:T(8,128)(2,1)S(1)}, bf16[96,1024]{1,0:T(8,128)(2,1)S(1)}, u32[]{:S(2)}, u32[]{:S(2)}) collective-permute-start(bf16[96,1024]{1,0:T(8,128)(2,1)S(1)} %get-tuple-element.57.refs_1_), channel_id=1, source_target_pairs={{8,0},{9,1},{10,2},{11,3},{24,16},{25,17},{26,18},{27,19}} | collective-permute-start | bytes 589832 | tf_op jit(solution)/shard_map/ppermute | solution.py:508
  27.6 14.8 %collective-permute-start.9 = (bf16[96,1024]{1,0:T(8,128)(2,1)S(1)}, bf16[96,1024]{1,0:T(8,128)(2,1)S(1)}, u32[]{:S(2)}, u32[]{:S(2)}) collective-permute-start(bf16[96,1024]{1,0:T(8,128)(2,1)S(1)} %get-tuple-element.57.refs_1_), channel_id=1, source_target_pairs={{12,0},{13,1},{14,2},{15,3},{28,16},{29,17},{30,18},{31,19}} | collective-permute-start | bytes 589832 | tf_op jit(solution)/shard_map/ppermute | solution.py:508
  32.4 17.8 %collective-permute-start.14 = (bf16[96,1536]{1,0:T(8,128)(2,1)S(1)}, bf16[96,1536]{1,0:T(8,128)(2,1)S(1)}, u32[]{:S(2)}, u32[]{:S(2)}) collective-permute-start(bf16[96,1536]{1,0:T(8,128)(2,1)S(1)} %get-tuple-element.60.refs_0_), channel_id=1, source_target_pairs={{0,8},{1,9},{2,10},{3,11},{16,24},{17,25},{18,26},{19,27}} | collective-permute-start | bytes 884744 | tf_op jit(solution)/shard_map/ppermute | solution.py:549
  42.4 1.4 %collective-permute-start.11 = (bf16[96,1024]{1,0:T(8,128)(2,1)S(1)}, bf16[96,1024]{1,0:T(8,128)(2,1)S(1)}, u32[]{:S(2)}, u32[]{:S(2)}) collective-permute-start(bf16[96,1024]{1,0:T(8,128)(2,1)S(1)} %collective-permute-done.4.refs_3_.refs_1_), channel_id=1, source_target_pairs={{0,1},{1,0},{2,3},{3,2},{4,5},{5,4},{6,7},{7,6},{8,9},{9,8},{10,11... | collective-permute-start | bytes 589832 | tf_op jit(solution)/shard_map/ppermute | solution.py:42
  42.4 4.3 %collective-permute-start.10 = (bf16[96,1024]{1,0:T(8,128)(2,1)S(1)}, bf16[96,1024]{1,0:T(8,128)(2,1)S(1)}, u32[]{:S(2)}, u32[]{:S(2)}) collective-permute-start(bf16[96,1024]{1,0:T(8,128)(2,1)S(1)} %collective-permute-done.9.refs_5_.refs_3_), channel_id=1, source_target_pairs={{0,1},{1,0},{2,3},{3,2},{4,5},{5,4},{6,7},{7,6},{8,9},{9,8},{10,11... | collective-permute-start | bytes 589832 | tf_op jit(solution)/shard_map/ppermute | solution.py:42
  42.9 3.8 %collective-permute-start.8 = (bf16[96,1024]{1,0:T(8,128)(2,1)S(1)}, bf16[96,1024]{1,0:T(8,128)(2,1)S(1)}, u32[]{:S(2)}, u32[]{:S(2)}) collective-permute-start(bf16[96,1024]{1,0:T(8,128)(2,1)S(1)} %collective-permute-done.3.refs_3_.refs_1_), channel_id=1, source_target_pairs={{0,1},{1,0},{2,3},{3,2},{4,5},{5,4},{6,7},{7,6},{8,9},{9,8},{10,11... | collective-permute-start | bytes 589832 | tf_op jit(solution)/shard_map/ppermute | solution.py:42
  45.3 10.7 %collective-permute-start.13 = (bf16[128,1536]{1,0:T(8,128)(2,1)S(1)}, bf16[128,1536]{1,0:T(8,128)(2,1)S(1)}, u32[]{:S(2)}, u32[]{:S(2)}) collective-permute-start(bf16[128,1536]{1,0:T(8,128)(2,1)S(1)} %get-tuple-element.67.refs_14_.refs_0_), channel_id=1, source_target_pairs={{0,8},{1,9},{2,10},{3,11},{16,24},{17,25},{18,26},{19,27}} | collective-permute-start | bytes 1179656 | tf_op jit(solution)/shard_map/ppermute | solution.py:549
  50.1 6.6 %collective-permute-start.18 = (bf16[96,1536]{1,0:T(8,128)(2,1)S(1)}, bf16[96,1536]{1,0:T(8,128)(2,1)S(1)}, u32[]{:S(2)}, u32[]{:S(2)}) collective-permute-start(bf16[96,1536]{1,0:T(8,128)(2,1)S(1)} %collective-permute-done.14.refs_2_), channel_id=1, source_target_pairs={{8,4},{9,5},{10,6},{11,7},{24,20},{25,21},{26,22},{27,23}} | collective-permute-start | bytes 884744 | tf_op jit(solution)/shard_map/ppermute | solution.py:141
  50.8 6.8 %collective-permute-start.19 = (bf16[96,1536]{1,0:T(8,128)(2,1)S(1)}, bf16[96,1536]{1,0:T(8,128)(2,1)S(1)}, u32[]{:S(2)}, u32[]{:S(2)}) collective-permute-start(bf16[96,1536]{1,0:T(8,128)(2,1)S(1)} %collective-permute-done.14.refs_2_), channel_id=1, source_target_pairs={{8,12},{9,13},{10,14},{11,15},{24,28},{25,29},{26,30},{27,31}} | collective-permute-start | bytes 884744 | tf_op jit(solution)/shard_map/ppermute | solution.py:141
  51.5 15.1 %collective-permute-start.17 = (bf16[160,1536]{1,0:T(8,128)(2,1)S(1)}, bf16[160,1536]{1,0:T(8,128)(2,1)S(1)}, u32[]{:S(2)}, u32[]{:S(2)}) collective-permute-start(bf16[160,1536]{1,0:T(8,128)(2,1)S(1)} %get-tuple-element.68.refs_12_.refs_0_), channel_id=1, source_target_pairs={{0,8},{1,9},{2,10},{3,11},{16,24},{17,25},{18,26},{19,27}} | collective-permute-start | bytes 1474568 | tf_op jit(solution)/shard_map/ppermute | solution.py:549
  52.8 22.2 %collective-permute-start.12 = (bf16[128,1536]{1,0:T(8,128)(2,1)S(1)}, bf16[128,1536]{1,0:T(8,128)(2,1)S(1)}, u32[]{:S(2)}, u32[]{:S(2)}) collective-permute-start(bf16[128,1536]{1,0:T(8,128)(2,1)S(1)} %get-tuple-element.70.refs_0_), channel_id=1, source_target_pairs={{0,8},{1,9},{2,10},{3,11},{16,24},{17,25},{18,26},{19,27}} | collective-permute-start | bytes 1179656 | tf_op jit(solution)/shard_map/ppermute | solution.py:549
  56.1 11.9 %collective-permute-start.15 = (bf16[128,1536]{1,0:T(8,128)(2,1)S(1)}, bf16[128,1536]{1,0:T(8,128)(2,1)S(1)}, u32[]{:S(2)}, u32[]{:S(2)}) collective-permute-start(bf16[128,1536]{1,0:T(8,128)(2,1)S(1)} %collective-permute-done.13.refs_8_.refs_2_), channel_id=1, source_target_pairs={{8,4},{9,5},{10,6},{11,7},{24,20},{25,21},{26,22},{27,23}} | collective-permute-start | bytes 1179656 | tf_op jit(solution)/shard_map/ppermute | solution.py:141
  56.7 14.8 %collective-permute-start.16 = (bf16[128,1536]{1,0:T(8,128)(2,1)S(1)}, bf16[128,1536]{1,0:T(8,128)(2,1)S(1)}, u32[]{:S(2)}, u32[]{:S(2)}) collective-permute-start(bf16[128,1536]{1,0:T(8,128)(2,1)S(1)} %collective-permute-done.13.refs_8_.refs_2_), channel_id=1, source_target_pairs={{8,12},{9,13},{10,14},{11,15},{24,28},{25,29},{26,30},{27,31}} | collective-permute-start | bytes 1179656 | tf_op jit(solution)/shard_map/ppermute | solution.py:141
  66.6 9.1 %collective-permute-start.22 = (bf16[160,1536]{1,0:T(8,128)(2,1)S(1)}, bf16[160,1536]{1,0:T(8,128)(2,1)S(1)}, u32[]{:S(2)}, u32[]{:S(2)}) collective-permute-start(bf16[160,1536]{1,0:T(8,128)(2,1)S(1)} %collective-permute-done.17.refs_8_.refs_2_), channel_id=1, source_target_pairs={{8,4},{9,5},{10,6},{11,7},{24,20},{25,21},{26,22},{27,23}} | collective-permute-start | bytes 1474568 | tf_op jit(solution)/shard_map/ppermute | solution.py:141
  67.3 9.1 %collective-permute-start.23 = (bf16[160,1536]{1,0:T(8,128)(2,1)S(1)}, bf16[160,1536]{1,0:T(8,128)(2,1)S(1)}, u32[]{:S(2)}, u32[]{:S(2)}) collective-permute-start(bf16[160,1536]{1,0:T(8,128)(2,1)S(1)} %collective-permute-done.17.refs_8_.refs_2_), channel_id=1, source_target_pairs={{8,12},{9,13},{10,14},{11,15},{24,28},{25,29},{26,30},{27,31}} | collective-permute-start | bytes 1474568 | tf_op jit(solution)/shard_map/ppermute | solution.py:141
  68.0 9.6 %collective-permute-start.24 = (bf16[32,1024]{1,0:T(8,128)(2,1)S(1)}, bf16[32,1024]{1,0:T(8,128)(2,1)S(1)}, u32[]{:S(2)}, u32[]{:S(2)}) collective-permute-start(bf16[32,1024]{1,0:T(8,128)(2,1)S(1)} %get-tuple-element.84), channel_id=1, source_target_pairs={{0,4},{4,8},{8,12},{1,5},{5,9},{9,13},{2,6},{6,10},{10,14},{3,7},{... | collective-permute-start | bytes 196616 | tf_op jit(solution)/shard_map/ppermute | solution.py:613
  71.6 7.7 %collective-permute-start.25 = (bf16[32,1024]{1,0:T(8,128)(2,1)S(1)}, bf16[32,1024]{1,0:T(8,128)(2,1)S(1)}, u32[]{:S(2)}, u32[]{:S(2)}) collective-permute-start(bf16[32,1024]{1,0:T(8,128)(2,1)S(1)} %get-tuple-element.85), channel_id=1, source_target_pairs={{4,0},{8,4},{12,8},{5,1},{9,5},{13,9},{6,2},{10,6},{14,10},{7,3},{... | collective-permute-start | bytes 196616 | tf_op jit(solution)/shard_map/ppermute | solution.py:613
  75.0 9.4 %collective-permute-start.20 = (bf16[128,1536]{1,0:T(8,128)(2,1)S(1)}, bf16[128,1536]{1,0:T(8,128)(2,1)S(1)}, u32[]{:S(2)}, u32[]{:S(2)}) collective-permute-start(bf16[128,1536]{1,0:T(8,128)(2,1)S(1)} %collective-permute-done.12.refs_8_.refs_2_), channel_id=1, source_target_pairs={{8,4},{9,5},{10,6},{11,7},{24,20},{25,21},{26,22},{27,23}} | collective-permute-start | bytes 1179656 | tf_op jit(solution)/shard_map/ppermute | solution.py:141
  75.7 8.7 %collective-permute-start.21 = (bf16[128,1536]{1,0:T(8,128)(2,1)S(1)}, bf16[128,1536]{1,0:T(8,128)(2,1)S(1)}, u32[]{:S(2)}, u32[]{:S(2)}) collective-permute-start(bf16[128,1536]{1,0:T(8,128)(2,1)S(1)} %collective-permute-done.12.refs_8_.refs_2_), channel_id=1, source_target_pairs={{8,12},{9,13},{10,14},{11,15},{24,28},{25,29},{26,30},{27,31}} | collective-permute-start | bytes 1179656 | tf_op jit(solution)/shard_map/ppermute | solution.py:141
  79.5 1.5 %collective-permute-start.27 = (bf16[64,1024]{1,0:T(8,128)(2,1)S(1)}, bf16[64,1024]{1,0:T(8,128)(2,1)S(1)}, u32[]{:S(2)}, u32[]{:S(2)}) collective-permute-start(bf16[64,1024]{1,0:T(8,128)(2,1)S(1)} %get-tuple-element.87), channel_id=1, source_target_pairs={{0,1},{1,0},{2,3},{3,2},{4,5},{5,4},{6,7},{7,6},{8,9},{9,8},{10,11... | collective-permute-start | bytes 393224 | tf_op jit(solution)/shard_map/ppermute | solution.py:42
  82.3 9.2 %collective-permute-start.32 = (bf16[128,1024]{1,0:T(8,128)(2,1)S(1)}, bf16[128,1024]{1,0:T(8,128)(2,1)S(1)}, u32[]{:S(2)}, u32[]{:S(2)}) collective-permute-start(bf16[128,1024]{1,0:T(8,128)(2,1)S(1)} %get-tuple-element.90.refs_7_), channel_id=1, source_target_pairs={{0,2},{2,0},{1,3},{3,1},{4,6},{6,4},{5,7},{7,5},{8,10},{10,8},{9,1... | collective-permute-start | bytes 786440 | tf_op jit(solution)/shard_map/ppermute | solution.py:42
  87.1 5.4 %collective-permute-start.31 = (bf16[32,1024]{1,0:T(8,128)(2,1)S(1)}, bf16[32,1024]{1,0:T(8,128)(2,1)S(1)}, u32[]{:S(2)}, u32[]{:S(2)}) collective-permute-start(bf16[32,1024]{1,0:T(8,128)(2,1)S(1)} %get-tuple-element.92.refs_2_), channel_id=1, source_target_pairs={{0,2},{2,0},{1,3},{3,1},{4,6},{6,4},{5,7},{7,5},{8,10},{10,8},{9,1... | collective-permute-start | bytes 196616 | tf_op jit(solution)/shard_map/ppermute | solution.py:42
  92.5 12.2 %collective-permute-start.33 = (bf16[32,1024]{1,0:T(8,128)(2,1)S(1)}, bf16[32,1024]{1,0:T(8,128)(2,1)S(1)}, u32[]{:S(2)}, u32[]{:S(2)}) collective-permute-start(bf16[32,1024]{1,0:T(8,128)(2,1)S(1)} %get-tuple-element.98), channel_id=1, source_target_pairs={{0,4},{4,8},{8,12},{12,0},{1,5},{5,9},{9,13},{13,1},{2,6},{6,10},{... | collective-permute-start | bytes 196616 | tf_op jit(solution)/shard_map/ppermute | solution.py:652
  99.4 7.0 %collective-permute-start.34 = (bf16[32,1024]{1,0:T(8,128)(2,1)S(1)}, bf16[32,1024]{1,0:T(8,128)(2,1)S(1)}, u32[]{:S(2)}, u32[]{:S(2)}) collective-permute-start(bf16[32,1024]{1,0:T(8,128)(2,1)S(1)} %get-tuple-element.99), channel_id=1, source_target_pairs={{0,8},{4,12},{8,0},{12,4},{1,9},{5,13},{9,1},{13,5},{2,10},{6,14},... | collective-permute-start | bytes 196616 | tf_op jit(solution)/shard_map/ppermute | solution.py:652
  102.2 4.8 %collective-permute-start.35 = (bf16[32,1024]{1,0:T(8,128)(2,1)S(1)}, bf16[32,1024]{1,0:T(8,128)(2,1)S(1)}, u32[]{:S(2)}, u32[]{:S(2)}) collective-permute-start(bf16[32,1024]{1,0:T(8,128)(2,1)S(1)} %get-tuple-element.100), channel_id=1, source_target_pairs={{0,12},{4,0},{8,4},{12,8},{1,13},{5,1},{9,5},{13,9},{2,14},{6,2},{... | collective-permute-start | bytes 196616 | tf_op jit(solution)/shard_map/ppermute | solution.py:652
  (15 other events, 34.7 us)

commit v4 on v3

--- a/solution.py
+++ b/solution.py
@@ -12,14 +12,23 @@
 CAP = 64
 LANE = 24
 LANE_ROWS = 32
-HALF = 96
 GROUP = 32
 VMEM = pl.BlockSpec(memory_space=pltpu.VMEM)
 ANY = pl.BlockSpec(memory_space=pl.ANY)
 HBM = pl.BlockSpec(memory_space=pltpu.HBM)
-COST = {'plan': 20000000000, 'tick0': 4000000000, 'tick1': 2000000000, 'tick2': 2000000000, 'tick3': 2000000000, 'tickz': 4000000000, 'early_core': 4000000000}
-OPT = {'late_first': 1, 'grads': 1, 'pads': 'rows', 'lag': 1}
+COST = {
+    "plan": 20_000_000_000,
+    "tick0": 4_000_000_000,
+    "tick1": 2_000_000_000,
+    "tick2": 2_000_000_000,
+    "tick3": 2_000_000_000,
+    "tickz": 2_000_000_000,
+    "early_core": 4_000_000_000,
+    "encode": 20_000_000_000,
+    "hidden0": 2_000_000_000,
+}
 CHUNKS = ((0, 3), (3, 7), (7, 12), (12, 16))
+EARLY = 3
 PART = ("seq", "mp", "rep")
 MEMBER = ("mp", "rep")
 F32 = jnp.float32
@@ -58,9 +67,6 @@
 
 
 def tick(name, *after):
-    if name not in COST:
-        return after[-1]
-
     def kernel(out_ref):
         out_ref[...] = jnp.zeros_like(out_ref)
 
@@ -161,9 +167,10 @@
         out_ref[at : at + 1] = jnp.where(seq == 0, 0.0, terms[:1] + terms[8:9])
 
 
-def plan_kernel(starts_ref, sel_ref, bias_ref, pack_ref, place_ref, member_ref):
+def plan_kernel(starts_ref, sel_ref, bias_ref, place_ref, member_ref):
     owner, core = lax.axis_index("seq"), lax.axis_index("rep")
-    device = owner * 4 + lax.axis_index("mp") * 2 + core
+    here_member = lax.axis_index("mp") * 2 + core
+    device = owner * 4 + here_member
     n_span = starts_ref.shape[1]
     length = sel_ref.shape[1]
     begin = device * length
@@ -191,20 +198,13 @@
     )
     member_ref[...] = jnp.where(span_index == target, 1.0, 0.0).astype(BF16)
 
-    block = owner * 4 + lax.broadcasted_iota(jnp.int32, (n_span, 4 * CAP), 1) // CAP
-    first = jnp.sum(jnp.where(column[:, :1] < block * length, 1.0, 0.0), axis=0, keepdims=True).astype(jnp.int32)
-    next_first = jnp.sum(jnp.where(column[:, :1] < block * length + length, 1.0, 0.0), axis=0, keepdims=True).astype(jnp.int32)
-    lane = lax.broadcasted_iota(jnp.int32, (2 * HALF, 4 * CAP), 1) % CAP
-    held = lax.broadcasted_iota(jnp.int32, (2 * HALF, 4 * CAP), 0) + first[:, :1]
-    pack_ref[...] = jnp.where((first + lane == held) & (held < next_first), 1.0, 0.0).astype(BF16)
-
-    around = column[:, :1] // (4 * length)
-    before = jnp.sum(jnp.where(row < around * (4 * length), 1.0, 0.0), axis=1, keepdims=True).astype(jnp.int32)
+    block = column[:, :1] // length
+    before = jnp.sum(jnp.where(row < block * length, 1.0, 0.0), axis=1, keepdims=True).astype(jnp.int32)
     span = lax.broadcasted_iota(jnp.int32, (n_span, 1), 0)
     near = jnp.minimum((span // 32 + 1) // 4, 3)
-    lies = span - before
-    side = jnp.where(lies >= HALF, 1, 0)
-    lies = lies - side * HALF + (side ^ core) * HALF + (around - near + 1) * (2 * HALF)
+    turned = (block % 4) ^ here_member
+    turned = (turned % 2) * 2 + turned // 2
+    lies = ((block // 4 - near + 1) * 4 + turned) * CAP + span - before
     lanes = lax.broadcasted_iota(jnp.int32, place_ref.shape, 1)
     place_ref[...] = jnp.where(lanes == lies, 1.0, 0.0).astype(BF16)
 
@@ -216,8 +216,7 @@
         (
             array(CAP, length, BF16),
             array(CAP, 2 * length, F32),
-            array(2 * HALF, 4 * CAP, BF16),
-            array(n_span, 4 * HALF, BF16),
+            array(n_span, 8 * CAP, BF16),
             array(span_own + 2 * LANE_ROWS, length, BF16),
         ),
         boundaries.reshape(1, n_span),
@@ -225,20 +224,38 @@
     )
 
 
-def encode_kernel(x_ref, halo_ref, sel_ref, bias_ref, gain_ref, qkv_ref, o_ref, out_ref):
+def project(normed, qkv_ref, at):
+    width = normed.shape[1]
+    wide = 2 * HEAD
+    keys = dot(normed, qkv_ref[:, width + at : width + at + wide]).astype(BF16)
+    values = dot(normed, qkv_ref[:, 2 * width + at : 2 * width + at + wide]).astype(BF16)
+    return keys, values
+
+
+def own_kernel(x_ref, sel_ref, gain_ref, qkv_ref, q_ref, kv_ref):
     width = x_ref.shape[1]
     wide = 2 * HEAD
-    gain = gain_ref[...]
+    normed = rms_scale(x_ref[...].astype(F32), gain_ref[...]).astype(BF16)
+    picked = dot(sel_ref[...], normed).astype(BF16)
+    for at in range(0, width, wide):
+        q_ref[:, at : at + wide] = dot(picked, qkv_ref[:, at : at + wide]).astype(BF16)
+        keys, values = project(normed, qkv_ref, at)
+        kv_ref[:, at : at + wide] = keys
+        kv_ref[:, width + at : width + at + wide] = values
+
+
+def encode_kernel(x_ref, halo_ref, sel_ref, bias_ref, gain_ref, qkv_ref, o_ref, q_ref, kv_ref, out_ref):
+    width = x_ref.shape[1]
+    wide = 2 * HEAD
     sel = sel_ref[...]
     bias = bias_ref[...]
-    normed = rms_scale(x_ref[...].astype(F32), gain).astype(BF16)
-    picked = dot(sel, normed).astype(BF16)
-    normed = jnp.concatenate([rms_scale(halo_ref[...].astype(F32), gain).astype(BF16), normed], axis=0)
+    normed = rms_scale(halo_ref[...].astype(F32), gain_ref[...]).astype(BF16)
     mixed = []
     for at in range(0, width, wide):
-        queries = dot(picked, qkv_ref[:, at : at + wide]).astype(BF16)
-        keys = dot(normed, qkv_ref[:, width + at : width + at + wide]).astype(BF16)
-        values = dot(normed, qkv_ref[:, 2 * width + at : 2 * width + at + wide]).astype(BF16)
+        queries = q_ref[:, at : at + wide]
+        keys, values = project(normed, qkv_ref, at)
+        keys = jnp.concatenate([keys, kv_ref[:, at : at + wide]], axis=0)
+        values = jnp.concatenate([values, kv_ref[:, width + at : width + at + wide]], axis=0)
         for head in range(0, wide, HEAD):
             part = slice(head, head + HEAD)
             scores = dot_t(queries[:, part], keys[:, part]) * (HEAD**-0.5) + bias
@@ -249,20 +266,9 @@
     out_ref[...] = total.astype(BF16)
 
 
-def pair_kernel(rows_ref, came_ref, out_ref):
-    chip = lax.axis_index("mp")
-    out_ref[:CAP] = jnp.where(chip == 0, rows_ref[...], came_ref[...])
-    out_ref[CAP:] = jnp.where(chip == 0, came_ref[...], rows_ref[...])
-
-
-def pack_kernel(pack_ref, pair_ref, came_ref, mine_ref, other_ref):
-    core = lax.axis_index("rep")
-    even = jnp.where(core == 0, pair_ref[...], came_ref[...])
-    odd = jnp.where(core == 0, came_ref[...], pair_ref[...])
-    blocks = [even[:CAP], odd[:CAP], even[CAP:], odd[CAP:]]
-    packed = dot(pack_ref[...], jnp.concatenate(blocks, axis=0)).astype(BF16)
-    mine_ref[...] = jnp.where(core == 0, packed[:HALF], packed[HALF:])
-    other_ref[...] = jnp.where(core == 0, packed[HALF:], packed[:HALF])
+def terms_kernel(*refs):
+    *in_refs, out_ref = refs
+    out_ref[...] = sum(ref[...] for ref in in_refs)
 
 
 def near_of(group):
@@ -270,19 +276,20 @@
 
 
 def hidden_kernel(low, high, place_ref, *refs):
-    *half_refs, pad_ref, gain_ref, gate_ref, up_ref, term1_ref, term2_ref, term3_ref, hidden_ref, row_ref = refs
+    base = max(near_of(low) - 1, 0)
+    count = 4 * (near_of(high - 1) - base + 1)
+    block_refs, refs = refs[:count], refs[count:]
+    pad_ref, gain_ref, gate_ref, up_ref, term_ref, hidden_ref, row_ref = refs
     width = row_ref.shape[1]
-    base = max(near_of(low) - 1, 0)
     row = []
     while low < high:
         near = near_of(low)
         end = min(high, 4 * near + 3) if near < 3 else high
         total = 0.0
-        for seq in (near - 1, near):
-            for side in range(2 if seq >= 0 else 0):
-                lanes = ((seq - near + 1) * 2 + side) * HALF
-                place = place_ref[low * GROUP : end * GROUP, lanes : lanes + HALF]
-                total += dot(place, half_refs[(seq - base) * 2 + side][...])
+        for seq in range(max(near - 1, 0), near + 1):
+            blocks = jnp.concatenate([ref[...] for ref in block_refs[(seq - base) * 4 : (seq - base) * 4 + 4]], axis=0)
+            lanes = (seq - near + 1) * 4 * CAP
+            total += dot(place_ref[low * GROUP : end * GROUP, lanes : lanes + 4 * CAP], blocks)
         row.append(total)
         low = end
     row = jnp.concatenate(row, axis=0)
@@ -290,7 +297,7 @@
     total = jnp.sum(row * row, axis=1, keepdims=True) + jnp.sum(pad * pad)
     scale = lax.rsqrt(total / (width + pad.shape[1]) + 1e-05)
     main_in = (row * scale * gain_ref[:, :width]).astype(BF16)
-    terms = term1_ref[...] + term2_ref[...] + term3_ref[...]
+    terms = term_ref[...]
     gate = dot(main_in, gate_ref[...]) + scale * terms[:1]
     upward = dot(main_in, up_ref[...]) + scale * terms[1:2]
     hidden_ref[...] = (gate / (1.0 + jnp.exp(-gate)) * upward).astype(BF16)
@@ -428,9 +435,19 @@
     direct = is_direct() and depth == width
     if direct:
         pad_row, gain_row = pad_vector.reshape(1, -1), main_gain.reshape(1, -1)
-        sel, bias, pack, where, member_of = plan(boundaries, length, n_member * share)
+        sel, bias, where, member_of = plan(boundaries, length, n_member * share)
         pad_terms = kernel_call(
             pad_kernel, array(2, columns, F32), pad_row, gain_row, gate_w, up_w, name="pad_terms", after=(sel,)
+        )
+        own = kernel_call(
+            own_kernel,
+            (array(CAP, width, BF16), array(length, 2 * width, BF16)),
+            byte_states,
+            sel,
+            enc_gain.reshape(1, width),
+            w_qkv,
+            name="own",
+            after=(pad_terms,),
         )
         rows = kernel_call(
             encode_kernel,
@@ -442,8 +459,9 @@
             enc_gain.reshape(1, width),
             w_qkv,
             w_out,
+            *own,
             name="encode",
-            after=(pad_terms,) if OPT.get("pads_first", 1) else (),
+            after=(pad_terms,),
         )
     else:
         wide_gain = main_gain[width:]
@@ -498,14 +516,16 @@
         main_out = spread.transpose(1, 0, 2).reshape(share, main_width)
         return (main_out, span_grad)
 
-    from_chip = swap(rows, "mp")
-    if OPT.get("pads") == "rows":
-        pad_terms, rows = tie(pad_terms, rows)
-    terms = [lax.ppermute(pad_terms, "seq", [(j, 0)]) for j in range(1, n_seq)]
-    pair = kernel_call(pair_kernel, array(2 * CAP, width, BF16), rows, from_chip, name="pair")
-    mine, other = kernel_call(pack_kernel, (array(HALF, width, BF16),) * 2, pack, pair, swap(pair, "rep"), name="pack")
-    planes = [(mine, other)]
-    came = [lax.ppermute(mine, "seq", [(j, 0)]) for j in range(1, n_seq)]
+    terms = [lax.ppermute(pad_terms, "seq", [(j, 0)]) for j in range(n_seq - 1, 0, -1)]
+    terms = kernel_call(terms_kernel, array(2, columns, F32), *terms, name="terms", after=(rows,))
+    rows, terms = tie(rows, terms)
+    def to_members(value):
+        from_chip = swap(value, "mp")
+        return value, from_chip, swap(value, "rep"), swap(from_chip, "rep")
+
+    came = [lax.ppermute(rows, "seq", [(j, 0)]) for j in range(1, n_seq)]
+    across = lax.ppermute(rows, MEMBER, [(j, 3 - j) for j in range(4)])
+    planes = [(rows, swap(rows, "mp"), swap(rows, "rep"), across)]
 
     def over_cores(values, name):
         quarters = sum(value.shape[0] for value in values) // GROUP // 4
@@ -526,10 +546,8 @@
     hiddens, row_parts, relayed, spread, parts = [], [], [], [], []
 
     def make_hidden(index, *after):
-        if OPT.get("lean") and index:
-            after = after[-1:]
         low, high = CHUNKS[index]
-        halves = [half for plane in planes[max(near_of(low) - 1, 0) : near_of(high - 1) + 1] for half in plane]
+        halves = [block for plane in planes[max(near_of(low) - 1, 0) : near_of(high - 1) + 1] for block in plane]
         count = (high - low) * share
         hidden, row = kernel_call(
             functools.partial(hidden_at_zero, low, high),
@@ -540,7 +558,7 @@
             gain_row,
             gate_w,
             up_w,
-            *terms,
+            terms,
             name=f"hidden{index}",
             after=after,
         )
@@ -567,42 +585,37 @@
             )
         )
 
-    def take(index, token):
-        arrived, token = tie(came[index], token)
-        planes.append((arrived, swap(arrived, "rep")))
-        return token
-
     def pass_on(index, token):
         relayed[index], token = tie(relayed[index], token)
         spread.append(relay(relayed[index]))
         return relayed[index], token
 
-    n_chunk = len(CHUNKS)
-    early = sum(high <= 12 for _, high in CHUNKS)
-    n_chunk = len(CHUNKS)
-    early = sum(high <= 12 for _, high in CHUNKS)
-    make_hidden(0)
-    token = take(2, take(1, take(0, tick("tickz", hiddens[0]))))
-    ahead = OPT.get("ahead", n_chunk - 1)
-    for index in range(1, ahead + 1):
-        make_hidden(index, token)
-        token = hiddens[index]
-    grads = OPT.get("grads", 2)
-    for index in range(n_chunk):
-        after = pass_on(index, tick(f"tickx{index}", token))
-        token = after[1]
-        if ahead + 1 + index < n_chunk:
-            make_hidden(ahead + 1 + index, *after)
-            token = hiddens[-1]
+    value, token = tie(came[0], rows)
+    planes.append(to_members(value))
+    make_hidden(0, token)
+    token = tick("tickz", hiddens[0])
+    later = []
+    for value in came[1:]:
+        value, token = tie(value, token)
+        later.append((value, swap(value, "mp"), swap(value, "rep")))
+    make_hidden(1, token)
+    token = hiddens[1]
+    for value, from_chip, from_core in later:
+        from_chip, token = tie(from_chip, token)
+        planes.append((value, from_chip, from_core, swap(from_chip, "rep")))
+    make_hidden(2, token)
+    make_hidden(3, hiddens[2])
+    token = hiddens[3]
+    for index in range(len(CHUNKS)):
+        arrived, token = pass_on(index, token)
         token = tick(f"tick{index}", token)
-        ready_part = index - OPT.get("lag", 1)
-        if ready_part >= 0:
-            make_part(ready_part, token, *after[:1])
+        if index:
+            make_part(index - 1, token, arrived)
             token = parts[-1]
-        if index == grads:
+        if index == 1:
             sums, to_before, to_after = kernel_call(
                 lanes_kernel,
-                (array(n_member * share, width, BF16), array(LANE_ROWS, width, BF16), array(LANE_ROWS, width, BF16)),
+                (array(n_member * share, width, BF16),) + (array(LANE_ROWS, width, BF16),) * 2,
                 member_of,
                 cotangent,
                 name="lanes",
@@ -612,36 +625,17 @@
             down = [(i + 1, i) for i in range(n_seq - 1)]
             from_both = lax.ppermute(to_after, "seq", up), lax.ppermute(to_before, "seq", down)
             token = sums
-    while len(parts) < early:
-        make_part(len(parts), token)
-        token = parts[-1]
     block = kernel_call(
         sums_kernel, array(n_member * share, width, BF16), sums, *from_both, name="span_sums", after=(token,)
     )
-    values = [*parts[:early], block]
-    own, sent = over_cores(values, "early")
-    from_mp = swap(sent, "mp")
-    token = sent
-    while len(parts) < n_chunk - 1:
-        make_part(len(parts), token)
-        token = parts[-1]
-    late_first = OPT.get("late_first", 0)
-
-    def add_early(*after):
-        *ready, span_grad = kernel_call(
-            add_kernel, (array(GROUP, depth, BF16),) * 4, own, from_mp, name="early_add", after=after
-        )
-        return ready, span_grad
-
-    if not late_first:
-        ready, span_grad = add_early(token)
-        token = ready[0]
-    if len(parts) < n_chunk:
-        make_part(n_chunk - 1, tick("tick6", token))
-    late_own, late_sent = over_cores(parts[early:], "late")
-    if late_first:
-        ready, span_grad = add_early(late_sent)
-    own, sent = late_own, late_sent
+
+    early_own, early_sent = over_cores([*parts[:EARLY], block], "early")
+    from_mp = swap(early_sent, "mp")
+    make_part(EARLY, early_sent)
+    own, sent = over_cores(parts[EARLY:], "late")
+    *ready, span_grad = kernel_call(
+        add_kernel, (array(GROUP, depth, BF16),) * 4, early_own, from_mp, name="early_add", after=(sent,)
+    )
 
     turned = kernel_call(
         turn_kernel, (array(GROUP, depth, BF16),) * n_seq, own, swap(sent, "mp"), *ready, name="turn"

time: 108 us -> 105 us (0.972)
  waiting for transfers between devices: 39.1 us -> 26.7 us
  starting transfers between devices: 43.3 us -> 54 us
  local copies, waits for them, and re-layouts: 4.67 us -> 3.08 us
    ppermute x6 -> x7, waiting for transfers between devices: 10.6 us -> 0.28 us  [the longest x3 0.27 us: local(): came = [lax.ppermute(rows, 'seq', [(j, 0)]) for j in range(1, n_seq)]]
    ppermute x12 -> x18, starting transfers between devices: 7.18 us -> 15.5 us  [swap(): return lax.ppermute(value, axis, [(0, 1), (1, 0)])]
    ppermute x4, starting transfers between devices: 5.35 us -> 9.13 us  [make_hidden(): relayed.append(lax.ppermute(hidden, 'seq', [(0, 2)]))]
    unnamed x22 -> x24, local copies, waits for them, and re-layouts: 4.67 us -> 3.08 us
    ppermute x12 -> x18, waiting for transfers between devices: 12 us -> 10.8 us  [swap(): return lax.ppermute(value, axis, [(0, 1), (1, 0)])]
    ppermute x6 -> x7, starting transfers between devices: 7.74 us -> 7.82 us  [the longest x3 3.88 us: local(): lax.ppermute(pad_terms, 'seq', [(j, 0)])]
  transfers between devices with their start and end apart: 36 -> 43, of which waited for: 17 -> 16; matrix products, arithmetic and copies ran while one was open for 0% -> 0% of each run, Pallas kernels for 13% -> 17%
where the time goes in v4:
time: 105 us; the launch traced here: 104 us
  starting transfers between devices  54 us (51%)
  waiting for transfers between devices  26.7 us (25%)
  Pallas kernels  18.9 us (18%)
  local copies, waits for them, and re-layouts  3.08 us (3%)
  between operations  1.24 us (1%)
    pallas_call x27, Pallas kernels, kernel_call(): pl.pallas_call(body, out_shape=out_shape, in_specs=[VMEM] * (count - stre...  18.9 us
    ppermute x18, starting transfers between devices, swap(): return lax.ppermute(value, axis, [(0, 1), (1, 0)])  15.5 us
    ppermute x18, waiting for transfers between devices, swap(): return lax.ppermute(value, axis, [(0, 1), (1, 0)])  10.8 us
    ppermute x4, waiting for transfers between devices, make_hidden(): relayed.append(lax.ppermute(hidden, 'seq', [(0, 2)]))  9.69 us
    ppermute x3, starting transfers between devices, local(): arrived.append(lax.ppermute(turned[turn], 'seq', pairs))  9.45 us
    ppermute x4, starting transfers between devices, make_hidden(): relayed.append(lax.ppermute(hidden, 'seq', [(0, 2)]))  9.13 us
    ppermute x3, waiting for transfers between devices, local(): arrived.append(lax.ppermute(turned[turn], 'seq', pairs))  4.1 us
    ppermute x3, starting transfers between devices, local(): lax.ppermute(pad_terms, 'seq', [(j, 0)])  3.88 us
  transfers between devices with their start and end apart: 43, of which 16 were waited for; matrix products, arithmetic and copies ran while one was open for 0% of the time, Pallas kernels for 17%

profile of v4, /device:TPU:0, one launch (start us, length us, event | category | flops | bytes accessed | tf_op | source)
XLA Modules:
  0.0 104.0 jit_solution(16301014992683786230)
XLA Ops:
  0.6 2.4 %collective-permute-start = (bf16[128,1024]{1,0:T(8,128)(2,1)}, bf16[128,1024]{1,0:T(8,128)(2,1)S(1)}, u32[]{:S(2)}, u32[]{:S(2)}) collective-permute-start(bf16[128,1024]{1,0:T(8,128)(2,1)} %refs_0_.3), channel_id=1, source_target_pairs={{0,1},{1,2},{2,3},{3,4},{4,5},{5,6},{6,7},{7,8},{8,9},{9,10},{10,1... | collective-permute-start | bytes 786440 | tf_op jit(solution)/shard_map/ppermute | solution.py:433
  7.8 1.3 %collective-permute-start.1 = (f32[2,1536]{1,0:T(2,128)S(1)}, f32[2,1536]{1,0:T(2,128)S(1)}, u32[]{:S(2)}, u32[]{:S(2)}) collective-permute-start(f32[2,1536]{1,0:T(2,128)S(1)} %pad_terms.1.refs_4_.refs_9_), channel_id=1, source_target_pairs={{12,0},{13,1},{14,2},{15,3},{28,16},{29,17},{30,18},{31,19}} | collective-permute-start | bytes 36872 | tf_op jit(solution)/shard_map/ppermute | solution.py:519
  9.1 1.3 %collective-permute-start.2 = (f32[2,1536]{1,0:T(2,128)S(1)}, f32[2,1536]{1,0:T(2,128)S(1)}, u32[]{:S(2)}, u32[]{:S(2)}) collective-permute-start(f32[2,1536]{1,0:T(2,128)S(1)} %pad_terms.1.refs_4_.refs_9_), channel_id=1, source_target_pairs={{8,0},{9,1},{10,2},{11,3},{24,16},{25,17},{26,18},{27,19}} | collective-permute-start | bytes 36872 | tf_op jit(solution)/shard_map/ppermute | solution.py:519
  10.4 1.3 %collective-permute-start.3 = (f32[2,1536]{1,0:T(2,128)S(1)}, f32[2,1536]{1,0:T(2,128)S(1)}, u32[]{:S(2)}, u32[]{:S(2)}) collective-permute-start(f32[2,1536]{1,0:T(2,128)S(1)} %pad_terms.1.refs_4_.refs_9_), channel_id=1, source_target_pairs={{4,0},{5,1},{6,2},{7,3},{20,16},{21,17},{22,18},{23,19}} | collective-permute-start | bytes 36872 | tf_op jit(solution)/shard_map/ppermute | solution.py:519
  11.8 1.3 %own.1 = (bf16[64,1024]{1,0:T(8,128)(2,1)S(1)}, bf16[128,2048]{1,0:T(8,128)(2,1)S(1)}) custom-call(bf16[128,1024]{1,0:T(8,128)(2,1)S(1)} %copy-done.5, bf16[64,128]{1,0:T(8,128)(2,1)S(1)} %get-tuple-element.56.refs_4_.refs_1_.refs_2_, f32[1,1024]{1,0:T(1,128)S(1)} %bitcast.20, bf16[1024,3072]{1,0:T(8,128)(2,1)S(1)} %bitcast.5, ...), custom_call_target="tpu_custom_call" | custom-call | tf_op jit(solution)/shard_map/own/pallas_call | solution.py:57
  13.4 3.1 %encode.1.refs_3_.refs_1_.refs_10_ = bf16[64,1024]{1,0:T(8,128)(2,1)S(1)} custom-call(bf16[128,1024]{1,0:T(8,128)(2,1)S(1)} %copy-done.5, bf16[128,1024]{1,0:T(8,128)(2,1)S(1)} %collective-permute-done.refs_1_, bf16[64,128]{1,0:T(8,128)(2,1)S(1)} %get-tuple-element.56.refs_4_.refs_1_.refs_2_, f32[64,256]{1,0:T(8,128)S(1)} %get-tuple-element.57.refs_3_, ...), custom_call_target="tpu_custom_call" | custom-call | flops 20000000000 | tf_op jit(solution)/shard_map/encode/pallas_call | solution.py:57
  16.5 1.3 %collective-permute-start.8 = (bf16[64,1024]{1,0:T(8,128)(2,1)S(1)}, bf16[64,1024]{1,0:T(8,128)(2,1)S(1)}, u32[]{:S(2)}, u32[]{:S(2)}) collective-permute-start(bf16[64,1024]{1,0:T(8,128)(2,1)S(1)} %encode.1.refs_3_.refs_1_.refs_10_), channel_id=1, source_target_pairs={{4,0},{5,1},{6,2},{7,3},{20,16},{21,17},{22,18},{23,19}} | collective-permute-start | bytes 393224 | tf_op jit(solution)/shard_map/ppermute | solution.py:526
  17.8 2.5 %collective-permute-start.5 = (bf16[64,1024]{1,0:T(8,128)(2,1)S(1)}, bf16[64,1024]{1,0:T(8,128)(2,1)S(1)}, u32[]{:S(2)}, u32[]{:S(2)}) collective-permute-start(bf16[64,1024]{1,0:T(8,128)(2,1)S(1)} %encode.1.refs_3_.refs_1_.refs_10_), channel_id=1, source_target_pairs={{0,2},{2,0},{1,3},{3,1},{4,6},{6,4},{5,7},{7,5},{8,10},{10,8},{9,1... | collective-permute-start | bytes 393224 | tf_op jit(solution)/shard_map/ppermute | solution.py:51
  20.3 1.4 %collective-permute-start.6 = (bf16[64,1024]{1,0:T(8,128)(2,1)S(1)}, bf16[64,1024]{1,0:T(8,128)(2,1)S(1)}, u32[]{:S(2)}, u32[]{:S(2)}) collective-permute-start(bf16[64,1024]{1,0:T(8,128)(2,1)S(1)} %encode.1.refs_3_.refs_1_.refs_10_), channel_id=1, source_target_pairs={{0,1},{1,0},{2,3},{3,2},{4,5},{5,4},{6,7},{7,6},{8,9},{9,8},{10,11... | collective-permute-start | bytes 393224 | tf_op jit(solution)/shard_map/ppermute | solution.py:51
  24.6 3.3 %collective-permute-start.10 = (bf16[64,1024]{1,0:T(8,128)(2,1)S(1)}, bf16[64,1024]{1,0:T(8,128)(2,1)S(1)}, u32[]{:S(2)}, u32[]{:S(2)}) collective-permute-start(bf16[64,1024]{1,0:T(8,128)(2,1)S(1)} %collective-permute-done.8.refs_5_.refs_1_), channel_id=1, source_target_pairs={{0,2},{2,0},{1,3},{3,1},{4,6},{6,4},{5,7},{7,5},{8,10},{10,8},{9,1... | collective-permute-start | bytes 393224 | tf_op jit(solution)/shard_map/ppermute | solution.py:51
  28.1 1.4 %hidden0.1 = (bf16[96,1536]{1,0:T(8,128)(2,1)S(1)}, bf16[96,1024]{1,0:T(8,128)(2,1)S(1)}) custom-call(bf16[512,512]{1,0:T(8,128)(2,1)S(1)} %get-tuple-element.55.refs_0_, bf16[64,1024]{1,0:T(8,128)(2,1)S(1)} %encode.1.refs_3_.refs_1_.refs_10_, bf16[64,1024]{1,0:T(8,128)(2,1)S(1)} %collective-permute-done.5.refs_2_, ...), custom_call_target="tpu_custom_call" | custom-call | flops 2000000000 | tf_op jit(solution)/shard_map/hidden0/pallas_call | solution.py:57
  29.6 2.1 %collective-permute-start.21 = (bf16[96,1536]{1,0:T(8,128)(2,1)S(1)}, bf16[96,1536]{1,0:T(8,128)(2,1)S(1)}, u32[]{:S(2)}, u32[]{:S(2)}) collective-permute-start(bf16[96,1536]{1,0:T(8,128)(2,1)S(1)} %get-tuple-element.63.refs_0_), channel_id=1, source_target_pairs={{0,8},{1,9},{2,10},{3,11},{16,24},{17,25},{18,26},{19,27}} | collective-permute-start | bytes 884744 | tf_op jit(solution)/shard_map/ppermute | solution.py:567
  32.1 1.8 %collective-permute-start.9 = (bf16[64,1024]{1,0:T(8,128)(2,1)S(1)}, bf16[64,1024]{1,0:T(8,128)(2,1)S(1)}, u32[]{:S(2)}, u32[]{:S(2)}) collective-permute-start(bf16[64,1024]{1,0:T(8,128)(2,1)S(1)} %collective-permute-done.4.refs_5_.refs_1_), channel_id=1, source_target_pairs={{0,2},{2,0},{1,3},{3,1},{4,6},{6,4},{5,7},{7,5},{8,10},{10,8},{9,1... | collective-permute-start | bytes 393224 | tf_op jit(solution)/shard_map/ppermute | solution.py:51
  33.9 2.2 %collective-permute-start.16 = (bf16[64,1024]{1,0:T(8,128)(2,1)S(1)}, bf16[64,1024]{1,0:T(8,128)(2,1)S(1)}, u32[]{:S(2)}, u32[]{:S(2)}) collective-permute-start(bf16[64,1024]{1,0:T(8,128)(2,1)S(1)} %collective-permute-done.13.refs_9_.refs_5_), channel_id=1, source_target_pairs={{0,2},{2,0},{1,3},{3,1},{4,6},{6,4},{5,7},{7,5},{8,10},{10,8},{9,1... | collective-permute-start | bytes 393224 | tf_op jit(solution)/shard_map/ppermute | solution.py:51
  36.6 1.4 %hidden1.1 = (bf16[128,1536]{1,0:T(8,128)(2,1)S(1)}, bf16[128,1024]{1,0:T(8,128)(2,1)S(1)}) custom-call(bf16[512,512]{1,0:T(8,128)(2,1)S(1)} %get-tuple-element.55.refs_0_, bf16[64,1024]{1,0:T(8,128)(2,1)S(1)} %encode.1.refs_3_.refs_1_.refs_10_, bf16[64,1024]{1,0:T(8,128)(2,1)S(1)} %collective-permute-done.5.refs_2_, ...), custom_call_target="tpu_custom_call" | custom-call | tf_op jit(solution)/shard_map/hidden1/pallas_call | solution.py:57
  38.4 2.4 %collective-permute-done.16.refs_10_.refs_6_ = bf16[64,1024]{1,0:T(8,128)(2,1)S(1)} collective-permute-done((bf16[64,1024]{1,0:T(8,128)(2,1)S(1)}, bf16[64,1024]{1,0:T(8,128)(2,1)S(1)}, u32[]{:S(2)}, u32[]{:S(2)}) %collective-permute-start.16) | collective-permute-done | bytes 131104 | tf_op jit(solution)/shard_map/ppermute | solution.py:51
  41.3 2.9 %collective-permute-start.20 = (bf16[128,1536]{1,0:T(8,128)(2,1)S(1)}, bf16[128,1536]{1,0:T(8,128)(2,1)S(1)}, u32[]{:S(2)}, u32[]{:S(2)}) collective-permute-start(bf16[128,1536]{1,0:T(8,128)(2,1)S(1)} %get-tuple-element.73.refs_18_.refs_0_), channel_id=1, source_target_pairs={{0,8},{1,9},{2,10},{3,11},{16,24},{17,25},{18,26},{19,27}} | collective-permute-start | bytes 1179656 | tf_op jit(solution)/shard_map/ppermute | solution.py:567
  44.2 1.7 %hidden2.1 = (bf16[160,1536]{1,0:T(8,128)(2,1)S(1)}, bf16[160,1024]{1,0:T(8,128)(2,1)S(1)}) custom-call(bf16[512,512]{1,0:T(8,128)(2,1)S(1)} %get-tuple-element.55.refs_0_, bf16[64,1024]{1,0:T(8,128)(2,1)S(1)} %collective-permute-done.8.refs_5_.refs_1_, bf16[64,1024]{1,0:T(8,128)(2,1)S(1)} %collective-permute-done.10.refs_6_.refs_2_, ...), custom_call_target="tpu_custom_call" | custom-call | tf_op jit(solution)/shard_map/hidden2/pallas_call | solution.py:57
  46.0 1.4 %hidden3.1 = (bf16[128,1536]{1,0:T(8,128)(2,1)S(1)}, bf16[128,1024]{1,0:T(8,128)(2,1)S(1)}) custom-call(bf16[512,512]{1,0:T(8,128)(2,1)S(1)} %get-tuple-element.55.refs_0_, bf16[64,1024]{1,0:T(8,128)(2,1)S(1)} %collective-permute-done.4.refs_5_.refs_1_, bf16[64,1024]{1,0:T(8,128)(2,1)S(1)} %collective-permute-done.9.refs_6_.refs_2_, ...), custom_call_target="tpu_custom_call" | custom-call | tf_op jit(solution)/shard_map/hidden3/pallas_call | solution.py:57
  48.8 2.8 %collective-permute-start.24 = (bf16[160,1536]{1,0:T(8,128)(2,1)S(1)}, bf16[160,1536]{1,0:T(8,128)(2,1)S(1)}, u32[]{:S(2)}, u32[]{:S(2)}) collective-permute-start(bf16[160,1536]{1,0:T(8,128)(2,1)S(1)} %get-tuple-element.74.refs_14_.refs_0_), channel_id=1, source_target_pairs={{0,8},{1,9},{2,10},{3,11},{16,24},{17,25},{18,26},{19,27}} | collective-permute-start | bytes 1474568 | tf_op jit(solution)/shard_map/ppermute | solution.py:567
  51.6 1.3 %collective-permute-start.19 = (bf16[128,1536]{1,0:T(8,128)(2,1)S(1)}, bf16[128,1536]{1,0:T(8,128)(2,1)S(1)}, u32[]{:S(2)}, u32[]{:S(2)}) collective-permute-start(bf16[128,1536]{1,0:T(8,128)(2,1)S(1)} %get-tuple-element.76.refs_0_), channel_id=1, source_target_pairs={{0,8},{1,9},{2,10},{3,11},{16,24},{17,25},{18,26},{19,27}} | collective-permute-start | bytes 1179656 | tf_op jit(solution)/shard_map/ppermute | solution.py:567
  56.7 7.4 %collective-permute-done.24.refs_8_.refs_2_ = bf16[160,1536]{1,0:T(8,128)(2,1)S(1)} collective-permute-done((bf16[160,1536]{1,0:T(8,128)(2,1)S(1)}, bf16[160,1536]{1,0:T(8,128)(2,1)S(1)}, u32[]{:S(2)}, u32[]{:S(2)}) %collective-permute-start.24) | collective-permute-done | bytes 491552 | tf_op jit(solution)/shard_map/ppermute | solution.py:567
  65.5 2.7 %collective-permute-start.31 = (bf16[32,1024]{1,0:T(8,128)(2,1)S(1)}, bf16[32,1024]{1,0:T(8,128)(2,1)S(1)}, u32[]{:S(2)}, u32[]{:S(2)}) collective-permute-start(bf16[32,1024]{1,0:T(8,128)(2,1)S(1)} %get-tuple-element.90), channel_id=1, source_target_pairs={{0,4},{4,8},{8,12},{1,5},{5,9},{9,13},{2,6},{6,10},{10,14},{3,7},{... | collective-permute-start | bytes 196616 | tf_op jit(solution)/shard_map/ppermute | solution.py:626
  70.7 1.7 %collective-permute-done.19.refs_8_.refs_2_ = bf16[128,1536]{1,0:T(8,128)(2,1)S(1)} collective-permute-done((bf16[128,1536]{1,0:T(8,128)(2,1)S(1)}, bf16[128,1536]{1,0:T(8,128)(2,1)S(1)}, u32[]{:S(2)}, u32[]{:S(2)}) %collective-permute-start.19) | collective-permute-done | bytes 393248 | tf_op jit(solution)/shard_map/ppermute | solution.py:567
  74.9 1.8 %collective-permute-done.32.refs_2_ = bf16[32,1024]{1,0:T(8,128)(2,1)S(1)} collective-permute-done((bf16[32,1024]{1,0:T(8,128)(2,1)S(1)}, bf16[32,1024]{1,0:T(8,128)(2,1)S(1)}, u32[]{:S(2)}, u32[]{:S(2)}) %collective-permute-start.32) | collective-permute-done | bytes 65568 | tf_op jit(solution)/shard_map/ppermute | solution.py:626
  79.8 1.5 %collective-permute-start.39 = (bf16[128,1024]{1,0:T(8,128)(2,1)S(1)}, bf16[128,1024]{1,0:T(8,128)(2,1)S(1)}, u32[]{:S(2)}, u32[]{:S(2)}) collective-permute-start(bf16[128,1024]{1,0:T(8,128)(2,1)S(1)} %get-tuple-element.96.refs_7_), channel_id=1, source_target_pairs={{0,2},{2,0},{1,3},{3,1},{4,6},{6,4},{5,7},{7,5},{8,10},{10,8},{9,1... | collective-permute-start | bytes 786440 | tf_op jit(solution)/shard_map/ppermute | solution.py:51
  82.6 1.3 %collective-permute-done.37.refs_1_ = bf16[64,1024]{1,0:T(8,128)(2,1)S(1)} collective-permute-done((bf16[64,1024]{1,0:T(8,128)(2,1)S(1)}, bf16[64,1024]{1,0:T(8,128)(2,1)S(1)}, u32[]{:S(2)}, u32[]{:S(2)}) %collective-permute-start.37) | collective-permute-done | bytes 131104 | tf_op jit(solution)/shard_map/ppermute | solution.py:51
  84.7 4.3 %collective-permute-done.39.refs_1_ = bf16[128,1024]{1,0:T(8,128)(2,1)S(1)} collective-permute-done((bf16[128,1024]{1,0:T(8,128)(2,1)S(1)}, bf16[128,1024]{1,0:T(8,128)(2,1)S(1)}, u32[]{:S(2)}, u32[]{:S(2)}) %collective-permute-start.39) | collective-permute-done | bytes 262176 | tf_op jit(solution)/shard_map/ppermute | solution.py:51
  89.7 6.3 %collective-permute-start.40 = (bf16[32,1024]{1,0:T(8,128)(2,1)S(1)}, bf16[32,1024]{1,0:T(8,128)(2,1)S(1)}, u32[]{:S(2)}, u32[]{:S(2)}) collective-permute-start(bf16[32,1024]{1,0:T(8,128)(2,1)S(1)} %get-tuple-element.104), channel_id=1, source_target_pairs={{0,4},{4,8},{8,12},{12,0},{1,5},{5,9},{9,13},{13,1},{2,6},{6,10},{... | collective-permute-start | bytes 196616 | tf_op jit(solution)/shard_map/ppermute | solution.py:646
  96.1 2.7 %collective-permute-start.41 = (bf16[32,1024]{1,0:T(8,128)(2,1)S(1)}, bf16[32,1024]{1,0:T(8,128)(2,1)S(1)}, u32[]{:S(2)}, u32[]{:S(2)}) collective-permute-start(bf16[32,1024]{1,0:T(8,128)(2,1)S(1)} %get-tuple-element.105), channel_id=1, source_target_pairs={{0,8},{4,12},{8,0},{12,4},{1,9},{5,13},{9,1},{13,5},{2,10},{6,14},... | collective-permute-start | bytes 196616 | tf_op jit(solution)/shard_map/ppermute | solution.py:646
  99.2 1.8 %collective-permute-done.40.refs_1_ = bf16[32,1024]{1,0:T(8,128)(2,1)S(1)} collective-permute-done((bf16[32,1024]{1,0:T(8,128)(2,1)S(1)}, bf16[32,1024]{1,0:T(8,128)(2,1)S(1)}, u32[]{:S(2)}, u32[]{:S(2)}) %collective-permute-start.40) | collective-permute-done | bytes 65568 | tf_op jit(solution)/shard_map/ppermute | solution.py:646
  100.9 1.9 %collective-permute-done.41.refs_2_ = bf16[32,1024]{1,0:T(8,128)(2,1)S(1)} collective-permute-done((bf16[32,1024]{1,0:T(8,128)(2,1)S(1)}, bf16[32,1024]{1,0:T(8,128)(2,1)S(1)}, u32[]{:S(2)}, u32[]{:S(2)}) %collective-permute-start.41) | collective-permute-done | bytes 65568 | tf_op jit(solution)/shard_map/ppermute | solution.py:646
  (106 shorter events, 28.6 us)
Async XLA Ops:
  0.6 12.5 %collective-permute-start = (bf16[128,1024]{1,0:T(8,128)(2,1)}, bf16[128,1024]{1,0:T(8,128)(2,1)S(1)}, u32[]{:S(2)}, u32[]{:S(2)}) collective-permute-start(bf16[128,1024]{1,0:T(8,128)(2,1)} %refs_0_.3), channel_id=1, source_target_pairs={{0,1},{1,2},{2,3},{3,4},{4,5},{5,6},{6,7},{7,8},{8,9},{9,10},{10,1... | collective-permute-start | bytes 786440 | tf_op jit(solution)/shard_map/ppermute | solution.py:433
  7.8 8.6 %collective-permute-start.1 = (f32[2,1536]{1,0:T(2,128)S(1)}, f32[2,1536]{1,0:T(2,128)S(1)}, u32[]{:S(2)}, u32[]{:S(2)}) collective-permute-start(f32[2,1536]{1,0:T(2,128)S(1)} %pad_terms.1.refs_4_.refs_9_), channel_id=1, source_target_pairs={{12,0},{13,1},{14,2},{15,3},{28,16},{29,17},{30,18},{31,19}} | collective-permute-start | bytes 36872 | tf_op jit(solution)/shard_map/ppermute | solution.py:519
  9.1 7.3 %collective-permute-start.2 = (f32[2,1536]{1,0:T(2,128)S(1)}, f32[2,1536]{1,0:T(2,128)S(1)}, u32[]{:S(2)}, u32[]{:S(2)}) collective-permute-start(f32[2,1536]{1,0:T(2,128)S(1)} %pad_terms.1.refs_4_.refs_9_), channel_id=1, source_target_pairs={{8,0},{9,1},{10,2},{11,3},{24,16},{25,17},{26,18},{27,19}} | collective-permute-start | bytes 36872 | tf_op jit(solution)/shard_map/ppermute | solution.py:519
  10.4 6.0 %collective-permute-start.3 = (f32[2,1536]{1,0:T(2,128)S(1)}, f32[2,1536]{1,0:T(2,128)S(1)}, u32[]{:S(2)}, u32[]{:S(2)}) collective-permute-start(f32[2,1536]{1,0:T(2,128)S(1)} %pad_terms.1.refs_4_.refs_9_), channel_id=1, source_target_pairs={{4,0},{5,1},{6,2},{7,3},{20,16},{21,17},{22,18},{23,19}} | collective-permute-start | bytes 36872 | tf_op jit(solution)/shard_map/ppermute | solution.py:519
  16.5 6.9 %collective-permute-start.8 = (bf16[64,1024]{1,0:T(8,128)(2,1)S(1)}, bf16[64,1024]{1,0:T(8,128)(2,1)S(1)}, u32[]{:S(2)}, u32[]{:S(2)}) collective-permute-start(bf16[64,1024]{1,0:T(8,128)(2,1)S(1)} %encode.1.refs_3_.refs_1_.refs_10_), channel_id=1, source_target_pairs={{4,0},{5,1},{6,2},{7,3},{20,16},{21,17},{22,18},{23,19}} | collective-permute-start | bytes 393224 | tf_op jit(solution)/shard_map/ppermute | solution.py:526
  17.8 6.9 %collective-permute-start.5 = (bf16[64,1024]{1,0:T(8,128)(2,1)S(1)}, bf16[64,1024]{1,0:T(8,128)(2,1)S(1)}, u32[]{:S(2)}, u32[]{:S(2)}) collective-permute-start(bf16[64,1024]{1,0:T(8,128)(2,1)S(1)} %encode.1.refs_3_.refs_1_.refs_10_), channel_id=1, source_target_pairs={{0,2},{2,0},{1,3},{3,1},{4,6},{6,4},{5,7},{7,5},{8,10},{10,8},{9,1... | collective-permute-start | bytes 393224 | tf_op jit(solution)/shard_map/ppermute | solution.py:51
  20.3 7.6 %collective-permute-start.6 = (bf16[64,1024]{1,0:T(8,128)(2,1)S(1)}, bf16[64,1024]{1,0:T(8,128)(2,1)S(1)}, u32[]{:S(2)}, u32[]{:S(2)}) collective-permute-start(bf16[64,1024]{1,0:T(8,128)(2,1)S(1)} %encode.1.refs_3_.refs_1_.refs_10_), channel_id=1, source_target_pairs={{0,1},{1,0},{2,3},{3,2},{4,5},{5,4},{6,7},{7,6},{8,9},{9,8},{10,11... | collective-permute-start | bytes 393224 | tf_op jit(solution)/shard_map/ppermute | solution.py:51
  21.7 6.4 %collective-permute-start.7 = (bf16[64,1024]{1,0:T(8,128)(2,1)S(1)}, bf16[64,1024]{1,0:T(8,128)(2,1)S(1)}, u32[]{:S(2)}, u32[]{:S(2)}) collective-permute-start(bf16[64,1024]{1,0:T(8,128)(2,1)S(1)} %encode.1.refs_3_.refs_1_.refs_10_), channel_id=1, source_target_pairs={{0,3},{1,2},{2,1},{3,0},{4,7},{5,6},{6,5},{7,4},{8,11},{9,10},{10,... | collective-permute-start | bytes 393224 | tf_op jit(solution)/shard_map/ppermute | solution.py:527
  21.8 9.9 %collective-permute-start.4 = (bf16[64,1024]{1,0:T(8,128)(2,1)S(1)}, bf16[64,1024]{1,0:T(8,128)(2,1)S(1)}, u32[]{:S(2)}, u32[]{:S(2)}) collective-permute-start(bf16[64,1024]{1,0:T(8,128)(2,1)S(1)} %encode.1.refs_3_.refs_1_.refs_10_), channel_id=1, source_target_pairs={{8,0},{9,1},{10,2},{11,3},{24,16},{25,17},{26,18},{27,19}} | collective-permute-start | bytes 393224 | tf_op jit(solution)/shard_map/ppermute | solution.py:526
  23.3 10.6 %collective-permute-start.13 = (bf16[64,1024]{1,0:T(8,128)(2,1)S(1)}, bf16[64,1024]{1,0:T(8,128)(2,1)S(1)}, u32[]{:S(2)}, u32[]{:S(2)}) collective-permute-start(bf16[64,1024]{1,0:T(8,128)(2,1)S(1)} %encode.1.refs_3_.refs_1_.refs_10_), channel_id=1, source_target_pairs={{12,0},{13,1},{14,2},{15,3},{28,16},{29,17},{30,18},{31,19}} | collective-permute-start | bytes 393224 | tf_op jit(solution)/shard_map/ppermute | solution.py:526
  24.6 7.4 %collective-permute-start.10 = (bf16[64,1024]{1,0:T(8,128)(2,1)S(1)}, bf16[64,1024]{1,0:T(8,128)(2,1)S(1)}, u32[]{:S(2)}, u32[]{:S(2)}) collective-permute-start(bf16[64,1024]{1,0:T(8,128)(2,1)S(1)} %collective-permute-done.8.refs_5_.refs_1_), channel_id=1, source_target_pairs={{0,2},{2,0},{1,3},{3,1},{4,6},{6,4},{5,7},{7,5},{8,10},{10,8},{9,1... | collective-permute-start | bytes 393224 | tf_op jit(solution)/shard_map/ppermute | solution.py:51
  27.9 8.2 %collective-permute-start.11 = (bf16[64,1024]{1,0:T(8,128)(2,1)S(1)}, bf16[64,1024]{1,0:T(8,128)(2,1)S(1)}, u32[]{:S(2)}, u32[]{:S(2)}) collective-permute-start(bf16[64,1024]{1,0:T(8,128)(2,1)S(1)} %collective-permute-done.8.refs_5_.refs_1_), channel_id=1, source_target_pairs={{0,1},{1,0},{2,3},{3,2},{4,5},{5,4},{6,7},{7,6},{8,9},{9,8},{10,11... | collective-permute-start | bytes 393224 | tf_op jit(solution)/shard_map/ppermute | solution.py:51
  29.6 17.8 %collective-permute-start.21 = (bf16[96,1536]{1,0:T(8,128)(2,1)S(1)}, bf16[96,1536]{1,0:T(8,128)(2,1)S(1)}, u32[]{:S(2)}, u32[]{:S(2)}) collective-permute-start(bf16[96,1536]{1,0:T(8,128)(2,1)S(1)} %get-tuple-element.63.refs_0_), channel_id=1, source_target_pairs={{0,8},{1,9},{2,10},{3,11},{16,24},{17,25},{18,26},{19,27}} | collective-permute-start | bytes 884744 | tf_op jit(solution)/shard_map/ppermute | solution.py:567
  32.1 6.3 %collective-permute-start.9 = (bf16[64,1024]{1,0:T(8,128)(2,1)S(1)}, bf16[64,1024]{1,0:T(8,128)(2,1)S(1)}, u32[]{:S(2)}, u32[]{:S(2)}) collective-permute-start(bf16[64,1024]{1,0:T(8,128)(2,1)S(1)} %collective-permute-done.4.refs_5_.refs_1_), channel_id=1, source_target_pairs={{0,2},{2,0},{1,3},{3,1},{4,6},{6,4},{5,7},{7,5},{8,10},{10,8},{9,1... | collective-permute-start | bytes 393224 | tf_op jit(solution)/shard_map/ppermute | solution.py:51
  33.9 6.9 %collective-permute-start.16 = (bf16[64,1024]{1,0:T(8,128)(2,1)S(1)}, bf16[64,1024]{1,0:T(8,128)(2,1)S(1)}, u32[]{:S(2)}, u32[]{:S(2)}) collective-permute-start(bf16[64,1024]{1,0:T(8,128)(2,1)S(1)} %collective-permute-done.13.refs_9_.refs_5_), channel_id=1, source_target_pairs={{0,2},{2,0},{1,3},{3,1},{4,6},{6,4},{5,7},{7,5},{8,10},{10,8},{9,1... | collective-permute-start | bytes 393224 | tf_op jit(solution)/shard_map/ppermute | solution.py:51
  36.1 8.0 %collective-permute-start.14 = (bf16[64,1024]{1,0:T(8,128)(2,1)S(1)}, bf16[64,1024]{1,0:T(8,128)(2,1)S(1)}, u32[]{:S(2)}, u32[]{:S(2)}) collective-permute-start(bf16[64,1024]{1,0:T(8,128)(2,1)S(1)} %collective-permute-done.4.refs_5_.refs_1_), channel_id=1, source_target_pairs={{0,1},{1,0},{2,3},{3,2},{4,5},{5,4},{6,7},{7,6},{8,9},{9,8},{10,11... | collective-permute-start | bytes 393224 | tf_op jit(solution)/shard_map/ppermute | solution.py:51
  41.3 12.2 %collective-permute-start.20 = (bf16[128,1536]{1,0:T(8,128)(2,1)S(1)}, bf16[128,1536]{1,0:T(8,128)(2,1)S(1)}, u32[]{:S(2)}, u32[]{:S(2)}) collective-permute-start(bf16[128,1536]{1,0:T(8,128)(2,1)S(1)} %get-tuple-element.73.refs_18_.refs_0_), channel_id=1, source_target_pairs={{0,8},{1,9},{2,10},{3,11},{16,24},{17,25},{18,26},{19,27}} | collective-permute-start | bytes 1179656 | tf_op jit(solution)/shard_map/ppermute | solution.py:567
  47.4 7.0 %collective-permute-start.25 = (bf16[96,1536]{1,0:T(8,128)(2,1)S(1)}, bf16[96,1536]{1,0:T(8,128)(2,1)S(1)}, u32[]{:S(2)}, u32[]{:S(2)}) collective-permute-start(bf16[96,1536]{1,0:T(8,128)(2,1)S(1)} %collective-permute-done.21.refs_2_), channel_id=1, source_target_pairs={{8,4},{9,5},{10,6},{11,7},{24,20},{25,21},{26,22},{27,23}} | collective-permute-start | bytes 884744 | tf_op jit(solution)/shard_map/ppermute | solution.py:147
  48.1 7.2 %collective-permute-start.26 = (bf16[96,1536]{1,0:T(8,128)(2,1)S(1)}, bf16[96,1536]{1,0:T(8,128)(2,1)S(1)}, u32[]{:S(2)}, u32[]{:S(2)}) collective-permute-start(bf16[96,1536]{1,0:T(8,128)(2,1)S(1)} %collective-permute-done.21.refs_2_), channel_id=1, source_target_pairs={{8,12},{9,13},{10,14},{11,15},{24,28},{25,29},{26,30},{27,31}} | collective-permute-start | bytes 884744 | tf_op jit(solution)/shard_map/ppermute | solution.py:147
  48.8 15.3 %collective-permute-start.24 = (bf16[160,1536]{1,0:T(8,128)(2,1)S(1)}, bf16[160,1536]{1,0:T(8,128)(2,1)S(1)}, u32[]{:S(2)}, u32[]{:S(2)}) collective-permute-start(bf16[160,1536]{1,0:T(8,128)(2,1)S(1)} %get-tuple-element.74.refs_14_.refs_0_), channel_id=1, source_target_pairs={{0,8},{1,9},{2,10},{3,11},{16,24},{17,25},{18,26},{19,27}} | collective-permute-start | bytes 1474568 | tf_op jit(solution)/shard_map/ppermute | solution.py:567
  51.6 20.7 %collective-permute-start.19 = (bf16[128,1536]{1,0:T(8,128)(2,1)S(1)}, bf16[128,1536]{1,0:T(8,128)(2,1)S(1)}, u32[]{:S(2)}, u32[]{:S(2)}) collective-permute-start(bf16[128,1536]{1,0:T(8,128)(2,1)S(1)} %get-tuple-element.76.refs_0_), channel_id=1, source_target_pairs={{0,8},{1,9},{2,10},{3,11},{16,24},{17,25},{18,26},{19,27}} | collective-permute-start | bytes 1179656 | tf_op jit(solution)/shard_map/ppermute | solution.py:567
  53.6 11.9 %collective-permute-start.22 = (bf16[128,1536]{1,0:T(8,128)(2,1)S(1)}, bf16[128,1536]{1,0:T(8,128)(2,1)S(1)}, u32[]{:S(2)}, u32[]{:S(2)}) collective-permute-start(bf16[128,1536]{1,0:T(8,128)(2,1)S(1)} %collective-permute-done.20.refs_8_.refs_2_), channel_id=1, source_target_pairs={{8,4},{9,5},{10,6},{11,7},{24,20},{25,21},{26,22},{27,23}} | collective-permute-start | bytes 1179656 | tf_op jit(solution)/shard_map/ppermute | solution.py:147
  54.4 13.8 %collective-permute-start.23 = (bf16[128,1536]{1,0:T(8,128)(2,1)S(1)}, bf16[128,1536]{1,0:T(8,128)(2,1)S(1)}, u32[]{:S(2)}, u32[]{:S(2)}) collective-permute-start(bf16[128,1536]{1,0:T(8,128)(2,1)S(1)} %collective-permute-done.20.refs_8_.refs_2_), channel_id=1, source_target_pairs={{8,12},{9,13},{10,14},{11,15},{24,28},{25,29},{26,30},{27,31}} | collective-permute-start | bytes 1179656 | tf_op jit(solution)/shard_map/ppermute | solution.py:147
  64.1 8.9 %collective-permute-start.29 = (bf16[160,1536]{1,0:T(8,128)(2,1)S(1)}, bf16[160,1536]{1,0:T(8,128)(2,1)S(1)}, u32[]{:S(2)}, u32[]{:S(2)}) collective-permute-start(bf16[160,1536]{1,0:T(8,128)(2,1)S(1)} %collective-permute-done.24.refs_8_.refs_2_), channel_id=1, source_target_pairs={{8,4},{9,5},{10,6},{11,7},{24,20},{25,21},{26,22},{27,23}} | collective-permute-start | bytes 1474568 | tf_op jit(solution)/shard_map/ppermute | solution.py:147
  64.8 8.9 %collective-permute-start.30 = (bf16[160,1536]{1,0:T(8,128)(2,1)S(1)}, bf16[160,1536]{1,0:T(8,128)(2,1)S(1)}, u32[]{:S(2)}, u32[]{:S(2)}) collective-permute-start(bf16[160,1536]{1,0:T(8,128)(2,1)S(1)} %collective-permute-done.24.refs_8_.refs_2_), channel_id=1, source_target_pairs={{8,12},{9,13},{10,14},{11,15},{24,28},{25,29},{26,30},{27,31}} | collective-permute-start | bytes 1474568 | tf_op jit(solution)/shard_map/ppermute | solution.py:147
  65.5 9.4 %collective-permute-start.31 = (bf16[32,1024]{1,0:T(8,128)(2,1)S(1)}, bf16[32,1024]{1,0:T(8,128)(2,1)S(1)}, u32[]{:S(2)}, u32[]{:S(2)}) collective-permute-start(bf16[32,1024]{1,0:T(8,128)(2,1)S(1)} %get-tuple-element.90), channel_id=1, source_target_pairs={{0,4},{4,8},{8,12},{1,5},{5,9},{9,13},{2,6},{6,10},{10,14},{3,7},{... | collective-permute-start | bytes 196616 | tf_op jit(solution)/shard_map/ppermute | solution.py:626
  68.2 8.5 %collective-permute-start.32 = (bf16[32,1024]{1,0:T(8,128)(2,1)S(1)}, bf16[32,1024]{1,0:T(8,128)(2,1)S(1)}, u32[]{:S(2)}, u32[]{:S(2)}) collective-permute-start(bf16[32,1024]{1,0:T(8,128)(2,1)S(1)} %get-tuple-element.91), channel_id=1, source_target_pairs={{4,0},{8,4},{12,8},{5,1},{9,5},{13,9},{6,2},{10,6},{14,10},{7,3},{... | collective-permute-start | bytes 196616 | tf_op jit(solution)/shard_map/ppermute | solution.py:626
  72.3 9.0 %collective-permute-start.27 = (bf16[128,1536]{1,0:T(8,128)(2,1)S(1)}, bf16[128,1536]{1,0:T(8,128)(2,1)S(1)}, u32[]{:S(2)}, u32[]{:S(2)}) collective-permute-start(bf16[128,1536]{1,0:T(8,128)(2,1)S(1)} %collective-permute-done.19.refs_8_.refs_2_), channel_id=1, source_target_pairs={{8,4},{9,5},{10,6},{11,7},{24,20},{25,21},{26,22},{27,23}} | collective-permute-start | bytes 1179656 | tf_op jit(solution)/shard_map/ppermute | solution.py:147
  73.0 8.3 %collective-permute-start.28 = (bf16[128,1536]{1,0:T(8,128)(2,1)S(1)}, bf16[128,1536]{1,0:T(8,128)(2,1)S(1)}, u32[]{:S(2)}, u32[]{:S(2)}) collective-permute-start(bf16[128,1536]{1,0:T(8,128)(2,1)S(1)} %collective-permute-done.19.refs_8_.refs_2_), channel_id=1, source_target_pairs={{8,12},{9,13},{10,14},{11,15},{24,28},{25,29},{26,30},{27,31}} | collective-permute-start | bytes 1179656 | tf_op jit(solution)/shard_map/ppermute | solution.py:147
  79.8 9.1 %collective-permute-start.39 = (bf16[128,1024]{1,0:T(8,128)(2,1)S(1)}, bf16[128,1024]{1,0:T(8,128)(2,1)S(1)}, u32[]{:S(2)}, u32[]{:S(2)}) collective-permute-start(bf16[128,1024]{1,0:T(8,128)(2,1)S(1)} %get-tuple-element.96.refs_7_), channel_id=1, source_target_pairs={{0,2},{2,0},{1,3},{3,1},{4,6},{6,4},{5,7},{7,5},{8,10},{10,8},{9,1... | collective-permute-start | bytes 786440 | tf_op jit(solution)/shard_map/ppermute | solution.py:51
  89.7 11.2 %collective-permute-start.40 = (bf16[32,1024]{1,0:T(8,128)(2,1)S(1)}, bf16[32,1024]{1,0:T(8,128)(2,1)S(1)}, u32[]{:S(2)}, u32[]{:S(2)}) collective-permute-start(bf16[32,1024]{1,0:T(8,128)(2,1)S(1)} %get-tuple-element.104), channel_id=1, source_target_pairs={{0,4},{4,8},{8,12},{12,0},{1,5},{5,9},{9,13},{13,1},{2,6},{6,10},{... | collective-permute-start | bytes 196616 | tf_op jit(solution)/shard_map/ppermute | solution.py:646
  96.1 6.8 %collective-permute-start.41 = (bf16[32,1024]{1,0:T(8,128)(2,1)S(1)}, bf16[32,1024]{1,0:T(8,128)(2,1)S(1)}, u32[]{:S(2)}, u32[]{:S(2)}) collective-permute-start(bf16[32,1024]{1,0:T(8,128)(2,1)S(1)} %get-tuple-element.105), channel_id=1, source_target_pairs={{0,8},{4,12},{8,0},{12,4},{1,9},{5,13},{9,1},{13,5},{2,10},{6,14},... | collective-permute-start | bytes 196616 | tf_op jit(solution)/shard_map/ppermute | solution.py:646
  (23 other events, 76.6 us)

commit v5 on v4

--- a/solution.py
+++ b/solution.py
@@ -15,7 +15,6 @@
 GROUP = 32
 VMEM = pl.BlockSpec(memory_space=pltpu.VMEM)
 ANY = pl.BlockSpec(memory_space=pl.ANY)
-HBM = pl.BlockSpec(memory_space=pltpu.HBM)
 COST = {
     "plan": 20_000_000_000,
     "tick0": 4_000_000_000,
@@ -51,15 +50,14 @@
     return lax.ppermute(value, axis, [(0, 1), (1, 0)])
 
 
-def kernel_call(kernel, out_shape, *operands, name, after=(), streamed=0, scratch=()):
+def kernel_call(kernel, out_shape, *operands, name, after=()):
     count = len(operands)
     body = lambda *refs: kernel(*refs[:count], *refs[count + len(after) :])
     return pl.pallas_call(
         body,
         out_shape=out_shape,
-        in_specs=[VMEM] * (count - streamed) + [HBM] * streamed + [ANY] * len(after),
+        in_specs=[VMEM] * count + [ANY] * len(after),
         out_specs=jax.tree.map(lambda _: VMEM, out_shape),
-        scratch_shapes=scratch,
         compiler_params=pltpu.CompilerParams(vmem_limit_bytes=24 << 20),
         cost_estimate=pl.CostEstimate(flops=COST.get(name, 0), bytes_accessed=0, transcendentals=0),
         name=name,

time: 105 us -> 105 us (level)
  no operation moved by 1% of the time
where the time goes in v5:
time: 105 us; the launch traced here: 104 us
  starting transfers between devices  54 us (51%)
  waiting for transfers between devices  26.7 us (25%)
  Pallas kernels  18.9 us (18%)
  local copies, waits for them, and re-layouts  3.08 us (3%)
  between operations  1.24 us (1%)
    pallas_call x27, Pallas kernels, kernel_call(): pl.pallas_call(body, out_shape=out_shape, in_specs=[VMEM] * count + [ANY]...  18.9 us
    ppermute x18, starting transfers between devices, swap(): return lax.ppermute(value, axis, [(0, 1), (1, 0)])  15.5 us
    ppermute x18, waiting for transfers between devices, swap(): return lax.ppermute(value, axis, [(0, 1), (1, 0)])  10.8 us
    ppermute x4, waiting for transfers between devices, make_hidden(): relayed.append(lax.ppermute(hidden, 'seq', [(0, 2)]))  9.69 us
    ppermute x3, starting transfers between devices, local(): arrived.append(lax.ppermute(turned[turn], 'seq', pairs))  9.45 us
    ppermute x4, starting transfers between devices, make_hidden(): relayed.append(lax.ppermute(hidden, 'seq', [(0, 2)]))  9.13 us
    ppermute x3, waiting for transfers between devices, local(): arrived.append(lax.ppermute(turned[turn], 'seq', pairs))  4.1 us
    ppermute x3, starting transfers between devices, local(): lax.ppermute(pad_terms, 'seq', [(j, 0)])  3.88 us
  transfers between devices with their start and end apart: 43, of which 16 were waited for; matrix products, arithmetic and copies ran while one was open for 0% of the time, Pallas kernels for 17%

profile of v5, /device:TPU:0, one launch (start us, length us, event | category | flops | bytes accessed | tf_op | source)
XLA Modules:
  0.0 104.0 jit_solution(16301014992683786230)
XLA Ops:
  0.6 2.4 %collective-permute-start = (bf16[128,1024]{1,0:T(8,128)(2,1)}, bf16[128,1024]{1,0:T(8,128)(2,1)S(1)}, u32[]{:S(2)}, u32[]{:S(2)}) collective-permute-start(bf16[128,1024]{1,0:T(8,128)(2,1)} %refs_0_.3), channel_id=1, source_target_pairs={{0,1},{1,2},{2,3},{3,4},{4,5},{5,6},{6,7},{7,8},{8,9},{9,10},{10,1... | collective-permute-start | bytes 786440 | tf_op jit(solution)/shard_map/ppermute | solution.py:431
  7.8 1.3 %collective-permute-start.1 = (f32[2,1536]{1,0:T(2,128)S(1)}, f32[2,1536]{1,0:T(2,128)S(1)}, u32[]{:S(2)}, u32[]{:S(2)}) collective-permute-start(f32[2,1536]{1,0:T(2,128)S(1)} %pad_terms.1.refs_4_.refs_9_), channel_id=1, source_target_pairs={{12,0},{13,1},{14,2},{15,3},{28,16},{29,17},{30,18},{31,19}} | collective-permute-start | bytes 36872 | tf_op jit(solution)/shard_map/ppermute | solution.py:517
  9.1 1.3 %collective-permute-start.2 = (f32[2,1536]{1,0:T(2,128)S(1)}, f32[2,1536]{1,0:T(2,128)S(1)}, u32[]{:S(2)}, u32[]{:S(2)}) collective-permute-start(f32[2,1536]{1,0:T(2,128)S(1)} %pad_terms.1.refs_4_.refs_9_), channel_id=1, source_target_pairs={{8,0},{9,1},{10,2},{11,3},{24,16},{25,17},{26,18},{27,19}} | collective-permute-start | bytes 36872 | tf_op jit(solution)/shard_map/ppermute | solution.py:517
  10.4 1.3 %collective-permute-start.3 = (f32[2,1536]{1,0:T(2,128)S(1)}, f32[2,1536]{1,0:T(2,128)S(1)}, u32[]{:S(2)}, u32[]{:S(2)}) collective-permute-start(f32[2,1536]{1,0:T(2,128)S(1)} %pad_terms.1.refs_4_.refs_9_), channel_id=1, source_target_pairs={{4,0},{5,1},{6,2},{7,3},{20,16},{21,17},{22,18},{23,19}} | collective-permute-start | bytes 36872 | tf_op jit(solution)/shard_map/ppermute | solution.py:517
  11.8 1.3 %own.1 = (bf16[64,1024]{1,0:T(8,128)(2,1)S(1)}, bf16[128,2048]{1,0:T(8,128)(2,1)S(1)}) custom-call(bf16[128,1024]{1,0:T(8,128)(2,1)S(1)} %copy-done.5, bf16[64,128]{1,0:T(8,128)(2,1)S(1)} %get-tuple-element.56.refs_4_.refs_1_.refs_2_, f32[1,1024]{1,0:T(1,128)S(1)} %bitcast.20, bf16[1024,3072]{1,0:T(8,128)(2,1)S(1)} %bitcast.5, ...), custom_call_target="tpu_custom_call" | custom-call | tf_op jit(solution)/shard_map/own/pallas_call | solution.py:56
  13.4 3.1 %encode.1.refs_3_.refs_1_.refs_10_ = bf16[64,1024]{1,0:T(8,128)(2,1)S(1)} custom-call(bf16[128,1024]{1,0:T(8,128)(2,1)S(1)} %copy-done.5, bf16[128,1024]{1,0:T(8,128)(2,1)S(1)} %collective-permute-done.refs_1_, bf16[64,128]{1,0:T(8,128)(2,1)S(1)} %get-tuple-element.56.refs_4_.refs_1_.refs_2_, f32[64,256]{1,0:T(8,128)S(1)} %get-tuple-element.57.refs_3_, ...), custom_call_target="tpu_custom_call" | custom-call | flops 20000000000 | tf_op jit(solution)/shard_map/encode/pallas_call | solution.py:56
  16.5 1.3 %collective-permute-start.8 = (bf16[64,1024]{1,0:T(8,128)(2,1)S(1)}, bf16[64,1024]{1,0:T(8,128)(2,1)S(1)}, u32[]{:S(2)}, u32[]{:S(2)}) collective-permute-start(bf16[64,1024]{1,0:T(8,128)(2,1)S(1)} %encode.1.refs_3_.refs_1_.refs_10_), channel_id=1, source_target_pairs={{4,0},{5,1},{6,2},{7,3},{20,16},{21,17},{22,18},{23,19}} | collective-permute-start | bytes 393224 | tf_op jit(solution)/shard_map/ppermute | solution.py:524
  17.8 2.5 %collective-permute-start.5 = (bf16[64,1024]{1,0:T(8,128)(2,1)S(1)}, bf16[64,1024]{1,0:T(8,128)(2,1)S(1)}, u32[]{:S(2)}, u32[]{:S(2)}) collective-permute-start(bf16[64,1024]{1,0:T(8,128)(2,1)S(1)} %encode.1.refs_3_.refs_1_.refs_10_), channel_id=1, source_target_pairs={{0,2},{2,0},{1,3},{3,1},{4,6},{6,4},{5,7},{7,5},{8,10},{10,8},{9,1... | collective-permute-start | bytes 393224 | tf_op jit(solution)/shard_map/ppermute | solution.py:50
  20.3 1.4 %collective-permute-start.6 = (bf16[64,1024]{1,0:T(8,128)(2,1)S(1)}, bf16[64,1024]{1,0:T(8,128)(2,1)S(1)}, u32[]{:S(2)}, u32[]{:S(2)}) collective-permute-start(bf16[64,1024]{1,0:T(8,128)(2,1)S(1)} %encode.1.refs_3_.refs_1_.refs_10_), channel_id=1, source_target_pairs={{0,1},{1,0},{2,3},{3,2},{4,5},{5,4},{6,7},{7,6},{8,9},{9,8},{10,11... | collective-permute-start | bytes 393224 | tf_op jit(solution)/shard_map/ppermute | solution.py:50
  24.6 3.3 %collective-permute-start.10 = (bf16[64,1024]{1,0:T(8,128)(2,1)S(1)}, bf16[64,1024]{1,0:T(8,128)(2,1)S(1)}, u32[]{:S(2)}, u32[]{:S(2)}) collective-permute-start(bf16[64,1024]{1,0:T(8,128)(2,1)S(1)} %collective-permute-done.8.refs_5_.refs_1_), channel_id=1, source_target_pairs={{0,2},{2,0},{1,3},{3,1},{4,6},{6,4},{5,7},{7,5},{8,10},{10,8},{9,1... | collective-permute-start | bytes 393224 | tf_op jit(solution)/shard_map/ppermute | solution.py:50
  28.1 1.4 %hidden0.1 = (bf16[96,1536]{1,0:T(8,128)(2,1)S(1)}, bf16[96,1024]{1,0:T(8,128)(2,1)S(1)}) custom-call(bf16[512,512]{1,0:T(8,128)(2,1)S(1)} %get-tuple-element.55.refs_0_, bf16[64,1024]{1,0:T(8,128)(2,1)S(1)} %encode.1.refs_3_.refs_1_.refs_10_, bf16[64,1024]{1,0:T(8,128)(2,1)S(1)} %collective-permute-done.5.refs_2_, ...), custom_call_target="tpu_custom_call" | custom-call | flops 2000000000 | tf_op jit(solution)/shard_map/hidden0/pallas_call | solution.py:56
  29.6 2.1 %collective-permute-start.21 = (bf16[96,1536]{1,0:T(8,128)(2,1)S(1)}, bf16[96,1536]{1,0:T(8,128)(2,1)S(1)}, u32[]{:S(2)}, u32[]{:S(2)}) collective-permute-start(bf16[96,1536]{1,0:T(8,128)(2,1)S(1)} %get-tuple-element.63.refs_0_), channel_id=1, source_target_pairs={{0,8},{1,9},{2,10},{3,11},{16,24},{17,25},{18,26},{19,27}} | collective-permute-start | bytes 884744 | tf_op jit(solution)/shard_map/ppermute | solution.py:565
  32.1 1.8 %collective-permute-start.9 = (bf16[64,1024]{1,0:T(8,128)(2,1)S(1)}, bf16[64,1024]{1,0:T(8,128)(2,1)S(1)}, u32[]{:S(2)}, u32[]{:S(2)}) collective-permute-start(bf16[64,1024]{1,0:T(8,128)(2,1)S(1)} %collective-permute-done.4.refs_5_.refs_1_), channel_id=1, source_target_pairs={{0,2},{2,0},{1,3},{3,1},{4,6},{6,4},{5,7},{7,5},{8,10},{10,8},{9,1... | collective-permute-start | bytes 393224 | tf_op jit(solution)/shard_map/ppermute | solution.py:50
  33.9 2.2 %collective-permute-start.16 = (bf16[64,1024]{1,0:T(8,128)(2,1)S(1)}, bf16[64,1024]{1,0:T(8,128)(2,1)S(1)}, u32[]{:S(2)}, u32[]{:S(2)}) collective-permute-start(bf16[64,1024]{1,0:T(8,128)(2,1)S(1)} %collective-permute-done.13.refs_9_.refs_5_), channel_id=1, source_target_pairs={{0,2},{2,0},{1,3},{3,1},{4,6},{6,4},{5,7},{7,5},{8,10},{10,8},{9,1... | collective-permute-start | bytes 393224 | tf_op jit(solution)/shard_map/ppermute | solution.py:50
  36.6 1.4 %hidden1.1 = (bf16[128,1536]{1,0:T(8,128)(2,1)S(1)}, bf16[128,1024]{1,0:T(8,128)(2,1)S(1)}) custom-call(bf16[512,512]{1,0:T(8,128)(2,1)S(1)} %get-tuple-element.55.refs_0_, bf16[64,1024]{1,0:T(8,128)(2,1)S(1)} %encode.1.refs_3_.refs_1_.refs_10_, bf16[64,1024]{1,0:T(8,128)(2,1)S(1)} %collective-permute-done.5.refs_2_, ...), custom_call_target="tpu_custom_call" | custom-call | tf_op jit(solution)/shard_map/hidden1/pallas_call | solution.py:56
  38.4 2.4 %collective-permute-done.16.refs_10_.refs_6_ = bf16[64,1024]{1,0:T(8,128)(2,1)S(1)} collective-permute-done((bf16[64,1024]{1,0:T(8,128)(2,1)S(1)}, bf16[64,1024]{1,0:T(8,128)(2,1)S(1)}, u32[]{:S(2)}, u32[]{:S(2)}) %collective-permute-start.16) | collective-permute-done | bytes 131104 | tf_op jit(solution)/shard_map/ppermute | solution.py:50
  41.3 2.9 %collective-permute-start.20 = (bf16[128,1536]{1,0:T(8,128)(2,1)S(1)}, bf16[128,1536]{1,0:T(8,128)(2,1)S(1)}, u32[]{:S(2)}, u32[]{:S(2)}) collective-permute-start(bf16[128,1536]{1,0:T(8,128)(2,1)S(1)} %get-tuple-element.73.refs_18_.refs_0_), channel_id=1, source_target_pairs={{0,8},{1,9},{2,10},{3,11},{16,24},{17,25},{18,26},{19,27}} | collective-permute-start | bytes 1179656 | tf_op jit(solution)/shard_map/ppermute | solution.py:565
  44.2 1.7 %hidden2.1 = (bf16[160,1536]{1,0:T(8,128)(2,1)S(1)}, bf16[160,1024]{1,0:T(8,128)(2,1)S(1)}) custom-call(bf16[512,512]{1,0:T(8,128)(2,1)S(1)} %get-tuple-element.55.refs_0_, bf16[64,1024]{1,0:T(8,128)(2,1)S(1)} %collective-permute-done.8.refs_5_.refs_1_, bf16[64,1024]{1,0:T(8,128)(2,1)S(1)} %collective-permute-done.10.refs_6_.refs_2_, ...), custom_call_target="tpu_custom_call" | custom-call | tf_op jit(solution)/shard_map/hidden2/pallas_call | solution.py:56
  46.0 1.4 %hidden3.1 = (bf16[128,1536]{1,0:T(8,128)(2,1)S(1)}, bf16[128,1024]{1,0:T(8,128)(2,1)S(1)}) custom-call(bf16[512,512]{1,0:T(8,128)(2,1)S(1)} %get-tuple-element.55.refs_0_, bf16[64,1024]{1,0:T(8,128)(2,1)S(1)} %collective-permute-done.4.refs_5_.refs_1_, bf16[64,1024]{1,0:T(8,128)(2,1)S(1)} %collective-permute-done.9.refs_6_.refs_2_, ...), custom_call_target="tpu_custom_call" | custom-call | tf_op jit(solution)/shard_map/hidden3/pallas_call | solution.py:56
  48.8 2.8 %collective-permute-start.24 = (bf16[160,1536]{1,0:T(8,128)(2,1)S(1)}, bf16[160,1536]{1,0:T(8,128)(2,1)S(1)}, u32[]{:S(2)}, u32[]{:S(2)}) collective-permute-start(bf16[160,1536]{1,0:T(8,128)(2,1)S(1)} %get-tuple-element.74.refs_14_.refs_0_), channel_id=1, source_target_pairs={{0,8},{1,9},{2,10},{3,11},{16,24},{17,25},{18,26},{19,27}} | collective-permute-start | bytes 1474568 | tf_op jit(solution)/shard_map/ppermute | solution.py:565
  51.6 1.3 %collective-permute-start.19 = (bf16[128,1536]{1,0:T(8,128)(2,1)S(1)}, bf16[128,1536]{1,0:T(8,128)(2,1)S(1)}, u32[]{:S(2)}, u32[]{:S(2)}) collective-permute-start(bf16[128,1536]{1,0:T(8,128)(2,1)S(1)} %get-tuple-element.76.refs_0_), channel_id=1, source_target_pairs={{0,8},{1,9},{2,10},{3,11},{16,24},{17,25},{18,26},{19,27}} | collective-permute-start | bytes 1179656 | tf_op jit(solution)/shard_map/ppermute | solution.py:565
  56.7 7.4 %collective-permute-done.24.refs_8_.refs_2_ = bf16[160,1536]{1,0:T(8,128)(2,1)S(1)} collective-permute-done((bf16[160,1536]{1,0:T(8,128)(2,1)S(1)}, bf16[160,1536]{1,0:T(8,128)(2,1)S(1)}, u32[]{:S(2)}, u32[]{:S(2)}) %collective-permute-start.24) | collective-permute-done | bytes 491552 | tf_op jit(solution)/shard_map/ppermute | solution.py:565
  65.5 2.7 %collective-permute-start.31 = (bf16[32,1024]{1,0:T(8,128)(2,1)S(1)}, bf16[32,1024]{1,0:T(8,128)(2,1)S(1)}, u32[]{:S(2)}, u32[]{:S(2)}) collective-permute-start(bf16[32,1024]{1,0:T(8,128)(2,1)S(1)} %get-tuple-element.90), channel_id=1, source_target_pairs={{0,4},{4,8},{8,12},{1,5},{5,9},{9,13},{2,6},{6,10},{10,14},{3,7},{... | collective-permute-start | bytes 196616 | tf_op jit(solution)/shard_map/ppermute | solution.py:624
  70.7 1.7 %collective-permute-done.19.refs_8_.refs_2_ = bf16[128,1536]{1,0:T(8,128)(2,1)S(1)} collective-permute-done((bf16[128,1536]{1,0:T(8,128)(2,1)S(1)}, bf16[128,1536]{1,0:T(8,128)(2,1)S(1)}, u32[]{:S(2)}, u32[]{:S(2)}) %collective-permute-start.19) | collective-permute-done | bytes 393248 | tf_op jit(solution)/shard_map/ppermute | solution.py:565
  74.9 1.8 %collective-permute-done.32.refs_2_ = bf16[32,1024]{1,0:T(8,128)(2,1)S(1)} collective-permute-done((bf16[32,1024]{1,0:T(8,128)(2,1)S(1)}, bf16[32,1024]{1,0:T(8,128)(2,1)S(1)}, u32[]{:S(2)}, u32[]{:S(2)}) %collective-permute-start.32) | collective-permute-done | bytes 65568 | tf_op jit(solution)/shard_map/ppermute | solution.py:624
  79.8 1.5 %collective-permute-start.39 = (bf16[128,1024]{1,0:T(8,128)(2,1)S(1)}, bf16[128,1024]{1,0:T(8,128)(2,1)S(1)}, u32[]{:S(2)}, u32[]{:S(2)}) collective-permute-start(bf16[128,1024]{1,0:T(8,128)(2,1)S(1)} %get-tuple-element.96.refs_7_), channel_id=1, source_target_pairs={{0,2},{2,0},{1,3},{3,1},{4,6},{6,4},{5,7},{7,5},{8,10},{10,8},{9,1... | collective-permute-start | bytes 786440 | tf_op jit(solution)/shard_map/ppermute | solution.py:50
  82.6 1.3 %collective-permute-done.37.refs_1_ = bf16[64,1024]{1,0:T(8,128)(2,1)S(1)} collective-permute-done((bf16[64,1024]{1,0:T(8,128)(2,1)S(1)}, bf16[64,1024]{1,0:T(8,128)(2,1)S(1)}, u32[]{:S(2)}, u32[]{:S(2)}) %collective-permute-start.37) | collective-permute-done | bytes 131104 | tf_op jit(solution)/shard_map/ppermute | solution.py:50
  84.7 4.3 %collective-permute-done.39.refs_1_ = bf16[128,1024]{1,0:T(8,128)(2,1)S(1)} collective-permute-done((bf16[128,1024]{1,0:T(8,128)(2,1)S(1)}, bf16[128,1024]{1,0:T(8,128)(2,1)S(1)}, u32[]{:S(2)}, u32[]{:S(2)}) %collective-permute-start.39) | collective-permute-done | bytes 262176 | tf_op jit(solution)/shard_map/ppermute | solution.py:50
  89.7 6.3 %collective-permute-start.40 = (bf16[32,1024]{1,0:T(8,128)(2,1)S(1)}, bf16[32,1024]{1,0:T(8,128)(2,1)S(1)}, u32[]{:S(2)}, u32[]{:S(2)}) collective-permute-start(bf16[32,1024]{1,0:T(8,128)(2,1)S(1)} %get-tuple-element.104), channel_id=1, source_target_pairs={{0,4},{4,8},{8,12},{12,0},{1,5},{5,9},{9,13},{13,1},{2,6},{6,10},{... | collective-permute-start | bytes 196616 | tf_op jit(solution)/shard_map/ppermute | solution.py:644
  96.1 2.7 %collective-permute-start.41 = (bf16[32,1024]{1,0:T(8,128)(2,1)S(1)}, bf16[32,1024]{1,0:T(8,128)(2,1)S(1)}, u32[]{:S(2)}, u32[]{:S(2)}) collective-permute-start(bf16[32,1024]{1,0:T(8,128)(2,1)S(1)} %get-tuple-element.105), channel_id=1, source_target_pairs={{0,8},{4,12},{8,0},{12,4},{1,9},{5,13},{9,1},{13,5},{2,10},{6,14},... | collective-permute-start | bytes 196616 | tf_op jit(solution)/shard_map/ppermute | solution.py:644
  99.2 1.8 %collective-permute-done.40.refs_1_ = bf16[32,1024]{1,0:T(8,128)(2,1)S(1)} collective-permute-done((bf16[32,1024]{1,0:T(8,128)(2,1)S(1)}, bf16[32,1024]{1,0:T(8,128)(2,1)S(1)}, u32[]{:S(2)}, u32[]{:S(2)}) %collective-permute-start.40) | collective-permute-done | bytes 65568 | tf_op jit(solution)/shard_map/ppermute | solution.py:644
  100.9 1.9 %collective-permute-done.41.refs_2_ = bf16[32,1024]{1,0:T(8,128)(2,1)S(1)} collective-permute-done((bf16[32,1024]{1,0:T(8,128)(2,1)S(1)}, bf16[32,1024]{1,0:T(8,128)(2,1)S(1)}, u32[]{:S(2)}, u32[]{:S(2)}) %collective-permute-start.41) | collective-permute-done | bytes 65568 | tf_op jit(solution)/shard_map/ppermute | solution.py:644
  (106 shorter events, 28.6 us)
Async XLA Ops:
  0.6 12.5 %collective-permute-start = (bf16[128,1024]{1,0:T(8,128)(2,1)}, bf16[128,1024]{1,0:T(8,128)(2,1)S(1)}, u32[]{:S(2)}, u32[]{:S(2)}) collective-permute-start(bf16[128,1024]{1,0:T(8,128)(2,1)} %refs_0_.3), channel_id=1, source_target_pairs={{0,1},{1,2},{2,3},{3,4},{4,5},{5,6},{6,7},{7,8},{8,9},{9,10},{10,1... | collective-permute-start | bytes 786440 | tf_op jit(solution)/shard_map/ppermute | solution.py:431
  7.8 8.6 %collective-permute-start.1 = (f32[2,1536]{1,0:T(2,128)S(1)}, f32[2,1536]{1,0:T(2,128)S(1)}, u32[]{:S(2)}, u32[]{:S(2)}) collective-permute-start(f32[2,1536]{1,0:T(2,128)S(1)} %pad_terms.1.refs_4_.refs_9_), channel_id=1, source_target_pairs={{12,0},{13,1},{14,2},{15,3},{28,16},{29,17},{30,18},{31,19}} | collective-permute-start | bytes 36872 | tf_op jit(solution)/shard_map/ppermute | solution.py:517
  9.1 7.3 %collective-permute-start.2 = (f32[2,1536]{1,0:T(2,128)S(1)}, f32[2,1536]{1,0:T(2,128)S(1)}, u32[]{:S(2)}, u32[]{:S(2)}) collective-permute-start(f32[2,1536]{1,0:T(2,128)S(1)} %pad_terms.1.refs_4_.refs_9_), channel_id=1, source_target_pairs={{8,0},{9,1},{10,2},{11,3},{24,16},{25,17},{26,18},{27,19}} | collective-permute-start | bytes 36872 | tf_op jit(solution)/shard_map/ppermute | solution.py:517
  10.4 6.0 %collective-permute-start.3 = (f32[2,1536]{1,0:T(2,128)S(1)}, f32[2,1536]{1,0:T(2,128)S(1)}, u32[]{:S(2)}, u32[]{:S(2)}) collective-permute-start(f32[2,1536]{1,0:T(2,128)S(1)} %pad_terms.1.refs_4_.refs_9_), channel_id=1, source_target_pairs={{4,0},{5,1},{6,2},{7,3},{20,16},{21,17},{22,18},{23,19}} | collective-permute-start | bytes 36872 | tf_op jit(solution)/shard_map/ppermute | solution.py:517
  16.5 6.9 %collective-permute-start.8 = (bf16[64,1024]{1,0:T(8,128)(2,1)S(1)}, bf16[64,1024]{1,0:T(8,128)(2,1)S(1)}, u32[]{:S(2)}, u32[]{:S(2)}) collective-permute-start(bf16[64,1024]{1,0:T(8,128)(2,1)S(1)} %encode.1.refs_3_.refs_1_.refs_10_), channel_id=1, source_target_pairs={{4,0},{5,1},{6,2},{7,3},{20,16},{21,17},{22,18},{23,19}} | collective-permute-start | bytes 393224 | tf_op jit(solution)/shard_map/ppermute | solution.py:524
  17.8 6.9 %collective-permute-start.5 = (bf16[64,1024]{1,0:T(8,128)(2,1)S(1)}, bf16[64,1024]{1,0:T(8,128)(2,1)S(1)}, u32[]{:S(2)}, u32[]{:S(2)}) collective-permute-start(bf16[64,1024]{1,0:T(8,128)(2,1)S(1)} %encode.1.refs_3_.refs_1_.refs_10_), channel_id=1, source_target_pairs={{0,2},{2,0},{1,3},{3,1},{4,6},{6,4},{5,7},{7,5},{8,10},{10,8},{9,1... | collective-permute-start | bytes 393224 | tf_op jit(solution)/shard_map/ppermute | solution.py:50
  20.3 7.6 %collective-permute-start.6 = (bf16[64,1024]{1,0:T(8,128)(2,1)S(1)}, bf16[64,1024]{1,0:T(8,128)(2,1)S(1)}, u32[]{:S(2)}, u32[]{:S(2)}) collective-permute-start(bf16[64,1024]{1,0:T(8,128)(2,1)S(1)} %encode.1.refs_3_.refs_1_.refs_10_), channel_id=1, source_target_pairs={{0,1},{1,0},{2,3},{3,2},{4,5},{5,4},{6,7},{7,6},{8,9},{9,8},{10,11... | collective-permute-start | bytes 393224 | tf_op jit(solution)/shard_map/ppermute | solution.py:50
  21.7 6.4 %collective-permute-start.7 = (bf16[64,1024]{1,0:T(8,128)(2,1)S(1)}, bf16[64,1024]{1,0:T(8,128)(2,1)S(1)}, u32[]{:S(2)}, u32[]{:S(2)}) collective-permute-start(bf16[64,1024]{1,0:T(8,128)(2,1)S(1)} %encode.1.refs_3_.refs_1_.refs_10_), channel_id=1, source_target_pairs={{0,3},{1,2},{2,1},{3,0},{4,7},{5,6},{6,5},{7,4},{8,11},{9,10},{10,... | collective-permute-start | bytes 393224 | tf_op jit(solution)/shard_map/ppermute | solution.py:525
  21.8 9.9 %collective-permute-start.4 = (bf16[64,1024]{1,0:T(8,128)(2,1)S(1)}, bf16[64,1024]{1,0:T(8,128)(2,1)S(1)}, u32[]{:S(2)}, u32[]{:S(2)}) collective-permute-start(bf16[64,1024]{1,0:T(8,128)(2,1)S(1)} %encode.1.refs_3_.refs_1_.refs_10_), channel_id=1, source_target_pairs={{8,0},{9,1},{10,2},{11,3},{24,16},{25,17},{26,18},{27,19}} | collective-permute-start | bytes 393224 | tf_op jit(solution)/shard_map/ppermute | solution.py:524
  23.3 10.6 %collective-permute-start.13 = (bf16[64,1024]{1,0:T(8,128)(2,1)S(1)}, bf16[64,1024]{1,0:T(8,128)(2,1)S(1)}, u32[]{:S(2)}, u32[]{:S(2)}) collective-permute-start(bf16[64,1024]{1,0:T(8,128)(2,1)S(1)} %encode.1.refs_3_.refs_1_.refs_10_), channel_id=1, source_target_pairs={{12,0},{13,1},{14,2},{15,3},{28,16},{29,17},{30,18},{31,19}} | collective-permute-start | bytes 393224 | tf_op jit(solution)/shard_map/ppermute | solution.py:524
  24.6 7.4 %collective-permute-start.10 = (bf16[64,1024]{1,0:T(8,128)(2,1)S(1)}, bf16[64,1024]{1,0:T(8,128)(2,1)S(1)}, u32[]{:S(2)}, u32[]{:S(2)}) collective-permute-start(bf16[64,1024]{1,0:T(8,128)(2,1)S(1)} %collective-permute-done.8.refs_5_.refs_1_), channel_id=1, source_target_pairs={{0,2},{2,0},{1,3},{3,1},{4,6},{6,4},{5,7},{7,5},{8,10},{10,8},{9,1... | collective-permute-start | bytes 393224 | tf_op jit(solution)/shard_map/ppermute | solution.py:50
  27.9 8.2 %collective-permute-start.11 = (bf16[64,1024]{1,0:T(8,128)(2,1)S(1)}, bf16[64,1024]{1,0:T(8,128)(2,1)S(1)}, u32[]{:S(2)}, u32[]{:S(2)}) collective-permute-start(bf16[64,1024]{1,0:T(8,128)(2,1)S(1)} %collective-permute-done.8.refs_5_.refs_1_), channel_id=1, source_target_pairs={{0,1},{1,0},{2,3},{3,2},{4,5},{5,4},{6,7},{7,6},{8,9},{9,8},{10,11... | collective-permute-start | bytes 393224 | tf_op jit(solution)/shard_map/ppermute | solution.py:50
  29.6 17.8 %collective-permute-start.21 = (bf16[96,1536]{1,0:T(8,128)(2,1)S(1)}, bf16[96,1536]{1,0:T(8,128)(2,1)S(1)}, u32[]{:S(2)}, u32[]{:S(2)}) collective-permute-start(bf16[96,1536]{1,0:T(8,128)(2,1)S(1)} %get-tuple-element.63.refs_0_), channel_id=1, source_target_pairs={{0,8},{1,9},{2,10},{3,11},{16,24},{17,25},{18,26},{19,27}} | collective-permute-start | bytes 884744 | tf_op jit(solution)/shard_map/ppermute | solution.py:565
  32.1 6.3 %collective-permute-start.9 = (bf16[64,1024]{1,0:T(8,128)(2,1)S(1)}, bf16[64,1024]{1,0:T(8,128)(2,1)S(1)}, u32[]{:S(2)}, u32[]{:S(2)}) collective-permute-start(bf16[64,1024]{1,0:T(8,128)(2,1)S(1)} %collective-permute-done.4.refs_5_.refs_1_), channel_id=1, source_target_pairs={{0,2},{2,0},{1,3},{3,1},{4,6},{6,4},{5,7},{7,5},{8,10},{10,8},{9,1... | collective-permute-start | bytes 393224 | tf_op jit(solution)/shard_map/ppermute | solution.py:50
  33.9 6.9 %collective-permute-start.16 = (bf16[64,1024]{1,0:T(8,128)(2,1)S(1)}, bf16[64,1024]{1,0:T(8,128)(2,1)S(1)}, u32[]{:S(2)}, u32[]{:S(2)}) collective-permute-start(bf16[64,1024]{1,0:T(8,128)(2,1)S(1)} %collective-permute-done.13.refs_9_.refs_5_), channel_id=1, source_target_pairs={{0,2},{2,0},{1,3},{3,1},{4,6},{6,4},{5,7},{7,5},{8,10},{10,8},{9,1... | collective-permute-start | bytes 393224 | tf_op jit(solution)/shard_map/ppermute | solution.py:50
  36.1 8.0 %collective-permute-start.14 = (bf16[64,1024]{1,0:T(8,128)(2,1)S(1)}, bf16[64,1024]{1,0:T(8,128)(2,1)S(1)}, u32[]{:S(2)}, u32[]{:S(2)}) collective-permute-start(bf16[64,1024]{1,0:T(8,128)(2,1)S(1)} %collective-permute-done.4.refs_5_.refs_1_), channel_id=1, source_target_pairs={{0,1},{1,0},{2,3},{3,2},{4,5},{5,4},{6,7},{7,6},{8,9},{9,8},{10,11... | collective-permute-start | bytes 393224 | tf_op jit(solution)/shard_map/ppermute | solution.py:50
  41.3 12.2 %collective-permute-start.20 = (bf16[128,1536]{1,0:T(8,128)(2,1)S(1)}, bf16[128,1536]{1,0:T(8,128)(2,1)S(1)}, u32[]{:S(2)}, u32[]{:S(2)}) collective-permute-start(bf16[128,1536]{1,0:T(8,128)(2,1)S(1)} %get-tuple-element.73.refs_18_.refs_0_), channel_id=1, source_target_pairs={{0,8},{1,9},{2,10},{3,11},{16,24},{17,25},{18,26},{19,27}} | collective-permute-start | bytes 1179656 | tf_op jit(solution)/shard_map/ppermute | solution.py:565
  47.4 7.0 %collective-permute-start.25 = (bf16[96,1536]{1,0:T(8,128)(2,1)S(1)}, bf16[96,1536]{1,0:T(8,128)(2,1)S(1)}, u32[]{:S(2)}, u32[]{:S(2)}) collective-permute-start(bf16[96,1536]{1,0:T(8,128)(2,1)S(1)} %collective-permute-done.21.refs_2_), channel_id=1, source_target_pairs={{8,4},{9,5},{10,6},{11,7},{24,20},{25,21},{26,22},{27,23}} | collective-permute-start | bytes 884744 | tf_op jit(solution)/shard_map/ppermute | solution.py:145
  48.1 7.2 %collective-permute-start.26 = (bf16[96,1536]{1,0:T(8,128)(2,1)S(1)}, bf16[96,1536]{1,0:T(8,128)(2,1)S(1)}, u32[]{:S(2)}, u32[]{:S(2)}) collective-permute-start(bf16[96,1536]{1,0:T(8,128)(2,1)S(1)} %collective-permute-done.21.refs_2_), channel_id=1, source_target_pairs={{8,12},{9,13},{10,14},{11,15},{24,28},{25,29},{26,30},{27,31}} | collective-permute-start | bytes 884744 | tf_op jit(solution)/shard_map/ppermute | solution.py:145
  48.8 15.3 %collective-permute-start.24 = (bf16[160,1536]{1,0:T(8,128)(2,1)S(1)}, bf16[160,1536]{1,0:T(8,128)(2,1)S(1)}, u32[]{:S(2)}, u32[]{:S(2)}) collective-permute-start(bf16[160,1536]{1,0:T(8,128)(2,1)S(1)} %get-tuple-element.74.refs_14_.refs_0_), channel_id=1, source_target_pairs={{0,8},{1,9},{2,10},{3,11},{16,24},{17,25},{18,26},{19,27}} | collective-permute-start | bytes 1474568 | tf_op jit(solution)/shard_map/ppermute | solution.py:565
  51.6 20.7 %collective-permute-start.19 = (bf16[128,1536]{1,0:T(8,128)(2,1)S(1)}, bf16[128,1536]{1,0:T(8,128)(2,1)S(1)}, u32[]{:S(2)}, u32[]{:S(2)}) collective-permute-start(bf16[128,1536]{1,0:T(8,128)(2,1)S(1)} %get-tuple-element.76.refs_0_), channel_id=1, source_target_pairs={{0,8},{1,9},{2,10},{3,11},{16,24},{17,25},{18,26},{19,27}} | collective-permute-start | bytes 1179656 | tf_op jit(solution)/shard_map/ppermute | solution.py:565
  53.6 11.9 %collective-permute-start.22 = (bf16[128,1536]{1,0:T(8,128)(2,1)S(1)}, bf16[128,1536]{1,0:T(8,128)(2,1)S(1)}, u32[]{:S(2)}, u32[]{:S(2)}) collective-permute-start(bf16[128,1536]{1,0:T(8,128)(2,1)S(1)} %collective-permute-done.20.refs_8_.refs_2_), channel_id=1, source_target_pairs={{8,4},{9,5},{10,6},{11,7},{24,20},{25,21},{26,22},{27,23}} | collective-permute-start | bytes 1179656 | tf_op jit(solution)/shard_map/ppermute | solution.py:145
  54.4 13.8 %collective-permute-start.23 = (bf16[128,1536]{1,0:T(8,128)(2,1)S(1)}, bf16[128,1536]{1,0:T(8,128)(2,1)S(1)}, u32[]{:S(2)}, u32[]{:S(2)}) collective-permute-start(bf16[128,1536]{1,0:T(8,128)(2,1)S(1)} %collective-permute-done.20.refs_8_.refs_2_), channel_id=1, source_target_pairs={{8,12},{9,13},{10,14},{11,15},{24,28},{25,29},{26,30},{27,31}} | collective-permute-start | bytes 1179656 | tf_op jit(solution)/shard_map/ppermute | solution.py:145
  64.1 8.9 %collective-permute-start.29 = (bf16[160,1536]{1,0:T(8,128)(2,1)S(1)}, bf16[160,1536]{1,0:T(8,128)(2,1)S(1)}, u32[]{:S(2)}, u32[]{:S(2)}) collective-permute-start(bf16[160,1536]{1,0:T(8,128)(2,1)S(1)} %collective-permute-done.24.refs_8_.refs_2_), channel_id=1, source_target_pairs={{8,4},{9,5},{10,6},{11,7},{24,20},{25,21},{26,22},{27,23}} | collective-permute-start | bytes 1474568 | tf_op jit(solution)/shard_map/ppermute | solution.py:145
  64.8 8.9 %collective-permute-start.30 = (bf16[160,1536]{1,0:T(8,128)(2,1)S(1)}, bf16[160,1536]{1,0:T(8,128)(2,1)S(1)}, u32[]{:S(2)}, u32[]{:S(2)}) collective-permute-start(bf16[160,1536]{1,0:T(8,128)(2,1)S(1)} %collective-permute-done.24.refs_8_.refs_2_), channel_id=1, source_target_pairs={{8,12},{9,13},{10,14},{11,15},{24,28},{25,29},{26,30},{27,31}} | collective-permute-start | bytes 1474568 | tf_op jit(solution)/shard_map/ppermute | solution.py:145
  65.5 9.4 %collective-permute-start.31 = (bf16[32,1024]{1,0:T(8,128)(2,1)S(1)}, bf16[32,1024]{1,0:T(8,128)(2,1)S(1)}, u32[]{:S(2)}, u32[]{:S(2)}) collective-permute-start(bf16[32,1024]{1,0:T(8,128)(2,1)S(1)} %get-tuple-element.90), channel_id=1, source_target_pairs={{0,4},{4,8},{8,12},{1,5},{5,9},{9,13},{2,6},{6,10},{10,14},{3,7},{... | collective-permute-start | bytes 196616 | tf_op jit(solution)/shard_map/ppermute | solution.py:624
  68.2 8.5 %collective-permute-start.32 = (bf16[32,1024]{1,0:T(8,128)(2,1)S(1)}, bf16[32,1024]{1,0:T(8,128)(2,1)S(1)}, u32[]{:S(2)}, u32[]{:S(2)}) collective-permute-start(bf16[32,1024]{1,0:T(8,128)(2,1)S(1)} %get-tuple-element.91), channel_id=1, source_target_pairs={{4,0},{8,4},{12,8},{5,1},{9,5},{13,9},{6,2},{10,6},{14,10},{7,3},{... | collective-permute-start | bytes 196616 | tf_op jit(solution)/shard_map/ppermute | solution.py:624
  72.3 9.0 %collective-permute-start.27 = (bf16[128,1536]{1,0:T(8,128)(2,1)S(1)}, bf16[128,1536]{1,0:T(8,128)(2,1)S(1)}, u32[]{:S(2)}, u32[]{:S(2)}) collective-permute-start(bf16[128,1536]{1,0:T(8,128)(2,1)S(1)} %collective-permute-done.19.refs_8_.refs_2_), channel_id=1, source_target_pairs={{8,4},{9,5},{10,6},{11,7},{24,20},{25,21},{26,22},{27,23}} | collective-permute-start | bytes 1179656 | tf_op jit(solution)/shard_map/ppermute | solution.py:145
  73.0 8.3 %collective-permute-start.28 = (bf16[128,1536]{1,0:T(8,128)(2,1)S(1)}, bf16[128,1536]{1,0:T(8,128)(2,1)S(1)}, u32[]{:S(2)}, u32[]{:S(2)}) collective-permute-start(bf16[128,1536]{1,0:T(8,128)(2,1)S(1)} %collective-permute-done.19.refs_8_.refs_2_), channel_id=1, source_target_pairs={{8,12},{9,13},{10,14},{11,15},{24,28},{25,29},{26,30},{27,31}} | collective-permute-start | bytes 1179656 | tf_op jit(solution)/shard_map/ppermute | solution.py:145
  79.8 9.1 %collective-permute-start.39 = (bf16[128,1024]{1,0:T(8,128)(2,1)S(1)}, bf16[128,1024]{1,0:T(8,128)(2,1)S(1)}, u32[]{:S(2)}, u32[]{:S(2)}) collective-permute-start(bf16[128,1024]{1,0:T(8,128)(2,1)S(1)} %get-tuple-element.96.refs_7_), channel_id=1, source_target_pairs={{0,2},{2,0},{1,3},{3,1},{4,6},{6,4},{5,7},{7,5},{8,10},{10,8},{9,1... | collective-permute-start | bytes 786440 | tf_op jit(solution)/shard_map/ppermute | solution.py:50
  89.7 11.2 %collective-permute-start.40 = (bf16[32,1024]{1,0:T(8,128)(2,1)S(1)}, bf16[32,1024]{1,0:T(8,128)(2,1)S(1)}, u32[]{:S(2)}, u32[]{:S(2)}) collective-permute-start(bf16[32,1024]{1,0:T(8,128)(2,1)S(1)} %get-tuple-element.104), channel_id=1, source_target_pairs={{0,4},{4,8},{8,12},{12,0},{1,5},{5,9},{9,13},{13,1},{2,6},{6,10},{... | collective-permute-start | bytes 196616 | tf_op jit(solution)/shard_map/ppermute | solution.py:644
  96.1 6.8 %collective-permute-start.41 = (bf16[32,1024]{1,0:T(8,128)(2,1)S(1)}, bf16[32,1024]{1,0:T(8,128)(2,1)S(1)}, u32[]{:S(2)}, u32[]{:S(2)}) collective-permute-start(bf16[32,1024]{1,0:T(8,128)(2,1)S(1)} %get-tuple-element.105), channel_id=1, source_target_pairs={{0,8},{4,12},{8,0},{12,4},{1,9},{5,13},{9,1},{13,5},{2,10},{6,14},... | collective-permute-start | bytes 196616 | tf_op jit(solution)/shard_map/ppermute | solution.py:644
  (23 other events, 76.6 us)

commit v6 on v5

--- a/solution.py
+++ b/solution.py
@@ -602,10 +602,12 @@
         from_chip, token = tie(from_chip, token)
         planes.append((value, from_chip, from_core, swap(from_chip, "rep")))
     make_hidden(2, token)
-    make_hidden(3, hiddens[2])
-    token = hiddens[3]
+    token = hiddens[2]
     for index in range(len(CHUNKS)):
         arrived, token = pass_on(index, token)
+        if index == 0:
+            make_hidden(3, arrived, token)
+            token = hiddens[3]
         token = tick(f"tick{index}", token)
         if index:
             make_part(index - 1, token, arrived)

time: 105 us -> 104 us (level)
  starting transfers between devices: 54 us -> 55.6 us
  waiting for transfers between devices: 26.7 us -> 25.2 us
    ppermute x4, starting transfers between devices: 9.13 us -> 10.8 us  [make_hidden(): relayed.append(lax.ppermute(hidden, 'seq', [(0, 2)]))]
    ppermute x4, waiting for transfers between devices: 9.69 us -> 8.14 us  [make_hidden(): relayed.append(lax.ppermute(hidden, 'seq', [(0, 2)]))]
  transfers between devices with their start and end apart: 43 -> 43, of which waited for: 16 -> 15; matrix products, arithmetic and copies ran while one was open for 0% -> 0% of each run, Pallas kernels for 17% -> 17%
where the time goes in v6:
time: 104 us
  starting transfers between devices  55.6 us (53%)
  waiting for transfers between devices  25.2 us (24%)
  Pallas kernels  18.9 us (18%)
  local copies, waits for them, and re-layouts  3.08 us (3%)
  between operations  1.25 us (1%)
    pallas_call x27, Pallas kernels, kernel_call(): pl.pallas_call(body, out_shape=out_shape, in_specs=[VMEM] * count + [ANY]...  18.9 us
    ppermute x18, starting transfers between devices, swap(): return lax.ppermute(value, axis, [(0, 1), (1, 0)])  15.5 us
    ppermute x4, starting transfers between devices, make_hidden(): relayed.append(lax.ppermute(hidden, 'seq', [(0, 2)]))  10.8 us
    ppermute x18, waiting for transfers between devices, swap(): return lax.ppermute(value, axis, [(0, 1), (1, 0)])  10.8 us
    ppermute x3, starting transfers between devices, local(): arrived.append(lax.ppermute(turned[turn], 'seq', pairs))  9.45 us
    ppermute x4, waiting for transfers between devices, make_hidden(): relayed.append(lax.ppermute(hidden, 'seq', [(0, 2)]))  8.14 us
    ppermute x3, waiting for transfers between devices, local(): arrived.append(lax.ppermute(turned[turn], 'seq', pairs))  4.1 us
    ppermute x3, starting transfers between devices, local(): lax.ppermute(pad_terms, 'seq', [(j, 0)])  3.88 us
  transfers between devices with their start and end apart: 43, of which 15 were waited for; matrix products, arithmetic and copies ran while one was open for 0% of the time, Pallas kernels for 17%

profile of v6, /device:TPU:0, one launch (start us, length us, event | category | flops | bytes accessed | tf_op | source)
XLA Modules:
  0.0 104.0 jit_solution(15483871859795120010)
XLA Ops:
  0.6 2.4 %collective-permute-start = (bf16[128,1024]{1,0:T(8,128)(2,1)}, bf16[128,1024]{1,0:T(8,128)(2,1)S(1)}, u32[]{:S(2)}, u32[]{:S(2)}) collective-permute-start(bf16[128,1024]{1,0:T(8,128)(2,1)} %refs_0_.3), channel_id=1, source_target_pairs={{0,1},{1,2},{2,3},{3,4},{4,5},{5,6},{6,7},{7,8},{8,9},{9,10},{10,1... | collective-permute-start | bytes 786440 | tf_op jit(solution)/shard_map/ppermute | solution.py:431
  7.8 1.3 %collective-permute-start.1 = (f32[2,1536]{1,0:T(2,128)S(1)}, f32[2,1536]{1,0:T(2,128)S(1)}, u32[]{:S(2)}, u32[]{:S(2)}) collective-permute-start(f32[2,1536]{1,0:T(2,128)S(1)} %pad_terms.1.refs_4_.refs_9_), channel_id=1, source_target_pairs={{12,0},{13,1},{14,2},{15,3},{28,16},{29,17},{30,18},{31,19}} | collective-permute-start | bytes 36872 | tf_op jit(solution)/shard_map/ppermute | solution.py:517
  9.1 1.3 %collective-permute-start.2 = (f32[2,1536]{1,0:T(2,128)S(1)}, f32[2,1536]{1,0:T(2,128)S(1)}, u32[]{:S(2)}, u32[]{:S(2)}) collective-permute-start(f32[2,1536]{1,0:T(2,128)S(1)} %pad_terms.1.refs_4_.refs_9_), channel_id=1, source_target_pairs={{8,0},{9,1},{10,2},{11,3},{24,16},{25,17},{26,18},{27,19}} | collective-permute-start | bytes 36872 | tf_op jit(solution)/shard_map/ppermute | solution.py:517
  10.4 1.3 %collective-permute-start.3 = (f32[2,1536]{1,0:T(2,128)S(1)}, f32[2,1536]{1,0:T(2,128)S(1)}, u32[]{:S(2)}, u32[]{:S(2)}) collective-permute-start(f32[2,1536]{1,0:T(2,128)S(1)} %pad_terms.1.refs_4_.refs_9_), channel_id=1, source_target_pairs={{4,0},{5,1},{6,2},{7,3},{20,16},{21,17},{22,18},{23,19}} | collective-permute-start | bytes 36872 | tf_op jit(solution)/shard_map/ppermute | solution.py:517
  11.8 1.3 %own.1 = (bf16[64,1024]{1,0:T(8,128)(2,1)S(1)}, bf16[128,2048]{1,0:T(8,128)(2,1)S(1)}) custom-call(bf16[128,1024]{1,0:T(8,128)(2,1)S(1)} %copy-done.5, bf16[64,128]{1,0:T(8,128)(2,1)S(1)} %get-tuple-element.56.refs_4_.refs_1_.refs_2_, f32[1,1024]{1,0:T(1,128)S(1)} %bitcast.20, bf16[1024,3072]{1,0:T(8,128)(2,1)S(1)} %bitcast.5, ...), custom_call_target="tpu_custom_call" | custom-call | tf_op jit(solution)/shard_map/own/pallas_call | solution.py:56
  13.4 3.1 %encode.1.refs_3_.refs_1_.refs_10_ = bf16[64,1024]{1,0:T(8,128)(2,1)S(1)} custom-call(bf16[128,1024]{1,0:T(8,128)(2,1)S(1)} %copy-done.5, bf16[128,1024]{1,0:T(8,128)(2,1)S(1)} %collective-permute-done.refs_1_, bf16[64,128]{1,0:T(8,128)(2,1)S(1)} %get-tuple-element.56.refs_4_.refs_1_.refs_2_, f32[64,256]{1,0:T(8,128)S(1)} %get-tuple-element.57.refs_3_, ...), custom_call_target="tpu_custom_call" | custom-call | flops 20000000000 | tf_op jit(solution)/shard_map/encode/pallas_call | solution.py:56
  16.5 1.3 %collective-permute-start.8 = (bf16[64,1024]{1,0:T(8,128)(2,1)S(1)}, bf16[64,1024]{1,0:T(8,128)(2,1)S(1)}, u32[]{:S(2)}, u32[]{:S(2)}) collective-permute-start(bf16[64,1024]{1,0:T(8,128)(2,1)S(1)} %encode.1.refs_3_.refs_1_.refs_10_), channel_id=1, source_target_pairs={{4,0},{5,1},{6,2},{7,3},{20,16},{21,17},{22,18},{23,19}} | collective-permute-start | bytes 393224 | tf_op jit(solution)/shard_map/ppermute | solution.py:524
  17.8 2.5 %collective-permute-start.5 = (bf16[64,1024]{1,0:T(8,128)(2,1)S(1)}, bf16[64,1024]{1,0:T(8,128)(2,1)S(1)}, u32[]{:S(2)}, u32[]{:S(2)}) collective-permute-start(bf16[64,1024]{1,0:T(8,128)(2,1)S(1)} %encode.1.refs_3_.refs_1_.refs_10_), channel_id=1, source_target_pairs={{0,2},{2,0},{1,3},{3,1},{4,6},{6,4},{5,7},{7,5},{8,10},{10,8},{9,1... | collective-permute-start | bytes 393224 | tf_op jit(solution)/shard_map/ppermute | solution.py:50
  20.3 1.4 %collective-permute-start.6 = (bf16[64,1024]{1,0:T(8,128)(2,1)S(1)}, bf16[64,1024]{1,0:T(8,128)(2,1)S(1)}, u32[]{:S(2)}, u32[]{:S(2)}) collective-permute-start(bf16[64,1024]{1,0:T(8,128)(2,1)S(1)} %encode.1.refs_3_.refs_1_.refs_10_), channel_id=1, source_target_pairs={{0,1},{1,0},{2,3},{3,2},{4,5},{5,4},{6,7},{7,6},{8,9},{9,8},{10,11... | collective-permute-start | bytes 393224 | tf_op jit(solution)/shard_map/ppermute | solution.py:50
  24.6 3.3 %collective-permute-start.10 = (bf16[64,1024]{1,0:T(8,128)(2,1)S(1)}, bf16[64,1024]{1,0:T(8,128)(2,1)S(1)}, u32[]{:S(2)}, u32[]{:S(2)}) collective-permute-start(bf16[64,1024]{1,0:T(8,128)(2,1)S(1)} %collective-permute-done.8.refs_5_.refs_1_), channel_id=1, source_target_pairs={{0,2},{2,0},{1,3},{3,1},{4,6},{6,4},{5,7},{7,5},{8,10},{10,8},{9,1... | collective-permute-start | bytes 393224 | tf_op jit(solution)/shard_map/ppermute | solution.py:50
  28.1 1.4 %hidden0.1 = (bf16[96,1536]{1,0:T(8,128)(2,1)S(1)}, bf16[96,1024]{1,0:T(8,128)(2,1)S(1)}) custom-call(bf16[512,512]{1,0:T(8,128)(2,1)S(1)} %get-tuple-element.55.refs_0_, bf16[64,1024]{1,0:T(8,128)(2,1)S(1)} %encode.1.refs_3_.refs_1_.refs_10_, bf16[64,1024]{1,0:T(8,128)(2,1)S(1)} %collective-permute-done.5.refs_2_, ...), custom_call_target="tpu_custom_call" | custom-call | flops 2000000000 | tf_op jit(solution)/shard_map/hidden0/pallas_call | solution.py:56
  29.6 2.1 %collective-permute-start.19 = (bf16[96,1536]{1,0:T(8,128)(2,1)S(1)}, bf16[96,1536]{1,0:T(8,128)(2,1)S(1)}, u32[]{:S(2)}, u32[]{:S(2)}) collective-permute-start(bf16[96,1536]{1,0:T(8,128)(2,1)S(1)} %get-tuple-element.63.refs_0_), channel_id=1, source_target_pairs={{0,8},{1,9},{2,10},{3,11},{16,24},{17,25},{18,26},{19,27}} | collective-permute-start | bytes 884744 | tf_op jit(solution)/shard_map/ppermute | solution.py:565
  32.1 1.8 %collective-permute-start.9 = (bf16[64,1024]{1,0:T(8,128)(2,1)S(1)}, bf16[64,1024]{1,0:T(8,128)(2,1)S(1)}, u32[]{:S(2)}, u32[]{:S(2)}) collective-permute-start(bf16[64,1024]{1,0:T(8,128)(2,1)S(1)} %collective-permute-done.4.refs_5_.refs_1_), channel_id=1, source_target_pairs={{0,2},{2,0},{1,3},{3,1},{4,6},{6,4},{5,7},{7,5},{8,10},{10,8},{9,1... | collective-permute-start | bytes 393224 | tf_op jit(solution)/shard_map/ppermute | solution.py:50
  33.9 2.2 %collective-permute-start.16 = (bf16[64,1024]{1,0:T(8,128)(2,1)S(1)}, bf16[64,1024]{1,0:T(8,128)(2,1)S(1)}, u32[]{:S(2)}, u32[]{:S(2)}) collective-permute-start(bf16[64,1024]{1,0:T(8,128)(2,1)S(1)} %collective-permute-done.13.refs_9_.refs_5_), channel_id=1, source_target_pairs={{0,2},{2,0},{1,3},{3,1},{4,6},{6,4},{5,7},{7,5},{8,10},{10,8},{9,1... | collective-permute-start | bytes 393224 | tf_op jit(solution)/shard_map/ppermute | solution.py:50
  36.6 1.4 %hidden1.1 = (bf16[128,1536]{1,0:T(8,128)(2,1)S(1)}, bf16[128,1024]{1,0:T(8,128)(2,1)S(1)}) custom-call(bf16[512,512]{1,0:T(8,128)(2,1)S(1)} %get-tuple-element.55.refs_0_, bf16[64,1024]{1,0:T(8,128)(2,1)S(1)} %encode.1.refs_3_.refs_1_.refs_10_, bf16[64,1024]{1,0:T(8,128)(2,1)S(1)} %collective-permute-done.5.refs_2_, ...), custom_call_target="tpu_custom_call" | custom-call | tf_op jit(solution)/shard_map/hidden1/pallas_call | solution.py:56
  38.4 2.4 %collective-permute-done.16.refs_10_.refs_6_ = bf16[64,1024]{1,0:T(8,128)(2,1)S(1)} collective-permute-done((bf16[64,1024]{1,0:T(8,128)(2,1)S(1)}, bf16[64,1024]{1,0:T(8,128)(2,1)S(1)}, u32[]{:S(2)}, u32[]{:S(2)}) %collective-permute-start.16) | collective-permute-done | bytes 131104 | tf_op jit(solution)/shard_map/ppermute | solution.py:50
  41.3 2.9 %collective-permute-start.21 = (bf16[128,1536]{1,0:T(8,128)(2,1)S(1)}, bf16[128,1536]{1,0:T(8,128)(2,1)S(1)}, u32[]{:S(2)}, u32[]{:S(2)}) collective-permute-start(bf16[128,1536]{1,0:T(8,128)(2,1)S(1)} %get-tuple-element.73.refs_18_.refs_0_), channel_id=1, source_target_pairs={{0,8},{1,9},{2,10},{3,11},{16,24},{17,25},{18,26},{19,27}} | collective-permute-start | bytes 1179656 | tf_op jit(solution)/shard_map/ppermute | solution.py:565
  44.2 1.8 %hidden2.1 = (bf16[160,1536]{1,0:T(8,128)(2,1)S(1)}, bf16[160,1024]{1,0:T(8,128)(2,1)S(1)}) custom-call(bf16[512,512]{1,0:T(8,128)(2,1)S(1)} %get-tuple-element.55.refs_0_, bf16[64,1024]{1,0:T(8,128)(2,1)S(1)} %collective-permute-done.8.refs_5_.refs_1_, bf16[64,1024]{1,0:T(8,128)(2,1)S(1)} %collective-permute-done.10.refs_6_.refs_2_, ...), custom_call_target="tpu_custom_call" | custom-call | tf_op jit(solution)/shard_map/hidden2/pallas_call | solution.py:56
  47.4 4.2 %collective-permute-start.24 = (bf16[160,1536]{1,0:T(8,128)(2,1)S(1)}, bf16[160,1536]{1,0:T(8,128)(2,1)S(1)}, u32[]{:S(2)}, u32[]{:S(2)}) collective-permute-start(bf16[160,1536]{1,0:T(8,128)(2,1)S(1)} %get-tuple-element.76.refs_15_.refs_0_), channel_id=1, source_target_pairs={{0,8},{1,9},{2,10},{3,11},{16,24},{17,25},{18,26},{19,27}} | collective-permute-start | bytes 1474568 | tf_op jit(solution)/shard_map/ppermute | solution.py:565
  51.6 1.4 %hidden3.1 = (bf16[128,1536]{1,0:T(8,128)(2,1)S(1)}, bf16[128,1024]{1,0:T(8,128)(2,1)S(1)}) custom-call(bf16[512,512]{1,0:T(8,128)(2,1)S(1)} %get-tuple-element.55.refs_0_, bf16[64,1024]{1,0:T(8,128)(2,1)S(1)} %collective-permute-done.4.refs_5_.refs_1_, bf16[64,1024]{1,0:T(8,128)(2,1)S(1)} %collective-permute-done.9.refs_6_.refs_2_, ...), custom_call_target="tpu_custom_call" | custom-call | tf_op jit(solution)/shard_map/hidden3/pallas_call | solution.py:56
  53.0 1.6 %collective-permute-start.20 = (bf16[128,1536]{1,0:T(8,128)(2,1)S(1)}, bf16[128,1536]{1,0:T(8,128)(2,1)S(1)}, u32[]{:S(2)}, u32[]{:S(2)}) collective-permute-start(bf16[128,1536]{1,0:T(8,128)(2,1)S(1)} %get-tuple-element.77.refs_0_), channel_id=1, source_target_pairs={{0,8},{1,9},{2,10},{3,11},{16,24},{17,25},{18,26},{19,27}} | collective-permute-start | bytes 1179656 | tf_op jit(solution)/shard_map/ppermute | solution.py:565
  57.6 6.5 %collective-permute-done.24.refs_8_.refs_2_ = bf16[160,1536]{1,0:T(8,128)(2,1)S(1)} collective-permute-done((bf16[160,1536]{1,0:T(8,128)(2,1)S(1)}, bf16[160,1536]{1,0:T(8,128)(2,1)S(1)}, u32[]{:S(2)}, u32[]{:S(2)}) %collective-permute-start.24) | collective-permute-done | bytes 491552 | tf_op jit(solution)/shard_map/ppermute | solution.py:565
  65.5 2.7 %collective-permute-start.31 = (bf16[32,1024]{1,0:T(8,128)(2,1)S(1)}, bf16[32,1024]{1,0:T(8,128)(2,1)S(1)}, u32[]{:S(2)}, u32[]{:S(2)}) collective-permute-start(bf16[32,1024]{1,0:T(8,128)(2,1)S(1)} %get-tuple-element.90), channel_id=1, source_target_pairs={{0,4},{4,8},{8,12},{1,5},{5,9},{9,13},{2,6},{6,10},{10,14},{3,7},{... | collective-permute-start | bytes 196616 | tf_op jit(solution)/shard_map/ppermute | solution.py:626
  70.7 1.7 %collective-permute-done.20.refs_8_.refs_2_ = bf16[128,1536]{1,0:T(8,128)(2,1)S(1)} collective-permute-done((bf16[128,1536]{1,0:T(8,128)(2,1)S(1)}, bf16[128,1536]{1,0:T(8,128)(2,1)S(1)}, u32[]{:S(2)}, u32[]{:S(2)}) %collective-permute-start.20) | collective-permute-done | bytes 393248 | tf_op jit(solution)/shard_map/ppermute | solution.py:565
  74.9 1.8 %collective-permute-done.32.refs_2_ = bf16[32,1024]{1,0:T(8,128)(2,1)S(1)} collective-permute-done((bf16[32,1024]{1,0:T(8,128)(2,1)S(1)}, bf16[32,1024]{1,0:T(8,128)(2,1)S(1)}, u32[]{:S(2)}, u32[]{:S(2)}) %collective-permute-start.32) | collective-permute-done | bytes 65568 | tf_op jit(solution)/shard_map/ppermute | solution.py:626
  79.8 1.5 %collective-permute-start.39 = (bf16[128,1024]{1,0:T(8,128)(2,1)S(1)}, bf16[128,1024]{1,0:T(8,128)(2,1)S(1)}, u32[]{:S(2)}, u32[]{:S(2)}) collective-permute-start(bf16[128,1024]{1,0:T(8,128)(2,1)S(1)} %get-tuple-element.96.refs_7_), channel_id=1, source_target_pairs={{0,2},{2,0},{1,3},{3,1},{4,6},{6,4},{5,7},{7,5},{8,10},{10,8},{9,1... | collective-permute-start | bytes 786440 | tf_op jit(solution)/shard_map/ppermute | solution.py:50
  82.6 1.3 %collective-permute-done.37.refs_1_ = bf16[64,1024]{1,0:T(8,128)(2,1)S(1)} collective-permute-done((bf16[64,1024]{1,0:T(8,128)(2,1)S(1)}, bf16[64,1024]{1,0:T(8,128)(2,1)S(1)}, u32[]{:S(2)}, u32[]{:S(2)}) %collective-permute-start.37) | collective-permute-done | bytes 131104 | tf_op jit(solution)/shard_map/ppermute | solution.py:50
  84.7 4.3 %collective-permute-done.39.refs_1_ = bf16[128,1024]{1,0:T(8,128)(2,1)S(1)} collective-permute-done((bf16[128,1024]{1,0:T(8,128)(2,1)S(1)}, bf16[128,1024]{1,0:T(8,128)(2,1)S(1)}, u32[]{:S(2)}, u32[]{:S(2)}) %collective-permute-start.39) | collective-permute-done | bytes 262176 | tf_op jit(solution)/shard_map/ppermute | solution.py:50
  89.7 6.3 %collective-permute-start.40 = (bf16[32,1024]{1,0:T(8,128)(2,1)S(1)}, bf16[32,1024]{1,0:T(8,128)(2,1)S(1)}, u32[]{:S(2)}, u32[]{:S(2)}) collective-permute-start(bf16[32,1024]{1,0:T(8,128)(2,1)S(1)} %get-tuple-element.104), channel_id=1, source_target_pairs={{0,4},{4,8},{8,12},{12,0},{1,5},{5,9},{9,13},{13,1},{2,6},{6,10},{... | collective-permute-start | bytes 196616 | tf_op jit(solution)/shard_map/ppermute | solution.py:646
  96.1 2.7 %collective-permute-start.41 = (bf16[32,1024]{1,0:T(8,128)(2,1)S(1)}, bf16[32,1024]{1,0:T(8,128)(2,1)S(1)}, u32[]{:S(2)}, u32[]{:S(2)}) collective-permute-start(bf16[32,1024]{1,0:T(8,128)(2,1)S(1)} %get-tuple-element.105), channel_id=1, source_target_pairs={{0,8},{4,12},{8,0},{12,4},{1,9},{5,13},{9,1},{13,5},{2,10},{6,14},... | collective-permute-start | bytes 196616 | tf_op jit(solution)/shard_map/ppermute | solution.py:646
  99.2 1.8 %collective-permute-done.40.refs_1_ = bf16[32,1024]{1,0:T(8,128)(2,1)S(1)} collective-permute-done((bf16[32,1024]{1,0:T(8,128)(2,1)S(1)}, bf16[32,1024]{1,0:T(8,128)(2,1)S(1)}, u32[]{:S(2)}, u32[]{:S(2)}) %collective-permute-start.40) | collective-permute-done | bytes 65568 | tf_op jit(solution)/shard_map/ppermute | solution.py:646
  100.9 1.9 %collective-permute-done.41.refs_2_ = bf16[32,1024]{1,0:T(8,128)(2,1)S(1)} collective-permute-done((bf16[32,1024]{1,0:T(8,128)(2,1)S(1)}, bf16[32,1024]{1,0:T(8,128)(2,1)S(1)}, u32[]{:S(2)}, u32[]{:S(2)}) %collective-permute-start.41) | collective-permute-done | bytes 65568 | tf_op jit(solution)/shard_map/ppermute | solution.py:646
  (106 shorter events, 27.9 us)
Async XLA Ops:
  0.6 12.5 %collective-permute-start = (bf16[128,1024]{1,0:T(8,128)(2,1)}, bf16[128,1024]{1,0:T(8,128)(2,1)S(1)}, u32[]{:S(2)}, u32[]{:S(2)}) collective-permute-start(bf16[128,1024]{1,0:T(8,128)(2,1)} %refs_0_.3), channel_id=1, source_target_pairs={{0,1},{1,2},{2,3},{3,4},{4,5},{5,6},{6,7},{7,8},{8,9},{9,10},{10,1... | collective-permute-start | bytes 786440 | tf_op jit(solution)/shard_map/ppermute | solution.py:431
  7.8 8.6 %collective-permute-start.1 = (f32[2,1536]{1,0:T(2,128)S(1)}, f32[2,1536]{1,0:T(2,128)S(1)}, u32[]{:S(2)}, u32[]{:S(2)}) collective-permute-start(f32[2,1536]{1,0:T(2,128)S(1)} %pad_terms.1.refs_4_.refs_9_), channel_id=1, source_target_pairs={{12,0},{13,1},{14,2},{15,3},{28,16},{29,17},{30,18},{31,19}} | collective-permute-start | bytes 36872 | tf_op jit(solution)/shard_map/ppermute | solution.py:517
  9.1 7.3 %collective-permute-start.2 = (f32[2,1536]{1,0:T(2,128)S(1)}, f32[2,1536]{1,0:T(2,128)S(1)}, u32[]{:S(2)}, u32[]{:S(2)}) collective-permute-start(f32[2,1536]{1,0:T(2,128)S(1)} %pad_terms.1.refs_4_.refs_9_), channel_id=1, source_target_pairs={{8,0},{9,1},{10,2},{11,3},{24,16},{25,17},{26,18},{27,19}} | collective-permute-start | bytes 36872 | tf_op jit(solution)/shard_map/ppermute | solution.py:517
  10.4 6.0 %collective-permute-start.3 = (f32[2,1536]{1,0:T(2,128)S(1)}, f32[2,1536]{1,0:T(2,128)S(1)}, u32[]{:S(2)}, u32[]{:S(2)}) collective-permute-start(f32[2,1536]{1,0:T(2,128)S(1)} %pad_terms.1.refs_4_.refs_9_), channel_id=1, source_target_pairs={{4,0},{5,1},{6,2},{7,3},{20,16},{21,17},{22,18},{23,19}} | collective-permute-start | bytes 36872 | tf_op jit(solution)/shard_map/ppermute | solution.py:517
  16.5 6.9 %collective-permute-start.8 = (bf16[64,1024]{1,0:T(8,128)(2,1)S(1)}, bf16[64,1024]{1,0:T(8,128)(2,1)S(1)}, u32[]{:S(2)}, u32[]{:S(2)}) collective-permute-start(bf16[64,1024]{1,0:T(8,128)(2,1)S(1)} %encode.1.refs_3_.refs_1_.refs_10_), channel_id=1, source_target_pairs={{4,0},{5,1},{6,2},{7,3},{20,16},{21,17},{22,18},{23,19}} | collective-permute-start | bytes 393224 | tf_op jit(solution)/shard_map/ppermute | solution.py:524
  17.8 6.9 %collective-permute-start.5 = (bf16[64,1024]{1,0:T(8,128)(2,1)S(1)}, bf16[64,1024]{1,0:T(8,128)(2,1)S(1)}, u32[]{:S(2)}, u32[]{:S(2)}) collective-permute-start(bf16[64,1024]{1,0:T(8,128)(2,1)S(1)} %encode.1.refs_3_.refs_1_.refs_10_), channel_id=1, source_target_pairs={{0,2},{2,0},{1,3},{3,1},{4,6},{6,4},{5,7},{7,5},{8,10},{10,8},{9,1... | collective-permute-start | bytes 393224 | tf_op jit(solution)/shard_map/ppermute | solution.py:50
  20.3 7.6 %collective-permute-start.6 = (bf16[64,1024]{1,0:T(8,128)(2,1)S(1)}, bf16[64,1024]{1,0:T(8,128)(2,1)S(1)}, u32[]{:S(2)}, u32[]{:S(2)}) collective-permute-start(bf16[64,1024]{1,0:T(8,128)(2,1)S(1)} %encode.1.refs_3_.refs_1_.refs_10_), channel_id=1, source_target_pairs={{0,1},{1,0},{2,3},{3,2},{4,5},{5,4},{6,7},{7,6},{8,9},{9,8},{10,11... | collective-permute-start | bytes 393224 | tf_op jit(solution)/shard_map/ppermute | solution.py:50
  21.7 6.4 %collective-permute-start.7 = (bf16[64,1024]{1,0:T(8,128)(2,1)S(1)}, bf16[64,1024]{1,0:T(8,128)(2,1)S(1)}, u32[]{:S(2)}, u32[]{:S(2)}) collective-permute-start(bf16[64,1024]{1,0:T(8,128)(2,1)S(1)} %encode.1.refs_3_.refs_1_.refs_10_), channel_id=1, source_target_pairs={{0,3},{1,2},{2,1},{3,0},{4,7},{5,6},{6,5},{7,4},{8,11},{9,10},{10,... | collective-permute-start | bytes 393224 | tf_op jit(solution)/shard_map/ppermute | solution.py:525
  21.8 9.9 %collective-permute-start.4 = (bf16[64,1024]{1,0:T(8,128)(2,1)S(1)}, bf16[64,1024]{1,0:T(8,128)(2,1)S(1)}, u32[]{:S(2)}, u32[]{:S(2)}) collective-permute-start(bf16[64,1024]{1,0:T(8,128)(2,1)S(1)} %encode.1.refs_3_.refs_1_.refs_10_), channel_id=1, source_target_pairs={{8,0},{9,1},{10,2},{11,3},{24,16},{25,17},{26,18},{27,19}} | collective-permute-start | bytes 393224 | tf_op jit(solution)/shard_map/ppermute | solution.py:524
  23.3 10.6 %collective-permute-start.13 = (bf16[64,1024]{1,0:T(8,128)(2,1)S(1)}, bf16[64,1024]{1,0:T(8,128)(2,1)S(1)}, u32[]{:S(2)}, u32[]{:S(2)}) collective-permute-start(bf16[64,1024]{1,0:T(8,128)(2,1)S(1)} %encode.1.refs_3_.refs_1_.refs_10_), channel_id=1, source_target_pairs={{12,0},{13,1},{14,2},{15,3},{28,16},{29,17},{30,18},{31,19}} | collective-permute-start | bytes 393224 | tf_op jit(solution)/shard_map/ppermute | solution.py:524
  24.6 7.4 %collective-permute-start.10 = (bf16[64,1024]{1,0:T(8,128)(2,1)S(1)}, bf16[64,1024]{1,0:T(8,128)(2,1)S(1)}, u32[]{:S(2)}, u32[]{:S(2)}) collective-permute-start(bf16[64,1024]{1,0:T(8,128)(2,1)S(1)} %collective-permute-done.8.refs_5_.refs_1_), channel_id=1, source_target_pairs={{0,2},{2,0},{1,3},{3,1},{4,6},{6,4},{5,7},{7,5},{8,10},{10,8},{9,1... | collective-permute-start | bytes 393224 | tf_op jit(solution)/shard_map/ppermute | solution.py:50
  27.9 8.2 %collective-permute-start.11 = (bf16[64,1024]{1,0:T(8,128)(2,1)S(1)}, bf16[64,1024]{1,0:T(8,128)(2,1)S(1)}, u32[]{:S(2)}, u32[]{:S(2)}) collective-permute-start(bf16[64,1024]{1,0:T(8,128)(2,1)S(1)} %collective-permute-done.8.refs_5_.refs_1_), channel_id=1, source_target_pairs={{0,1},{1,0},{2,3},{3,2},{4,5},{5,4},{6,7},{7,6},{8,9},{9,8},{10,11... | collective-permute-start | bytes 393224 | tf_op jit(solution)/shard_map/ppermute | solution.py:50
  29.6 16.4 %collective-permute-start.19 = (bf16[96,1536]{1,0:T(8,128)(2,1)S(1)}, bf16[96,1536]{1,0:T(8,128)(2,1)S(1)}, u32[]{:S(2)}, u32[]{:S(2)}) collective-permute-start(bf16[96,1536]{1,0:T(8,128)(2,1)S(1)} %get-tuple-element.63.refs_0_), channel_id=1, source_target_pairs={{0,8},{1,9},{2,10},{3,11},{16,24},{17,25},{18,26},{19,27}} | collective-permute-start | bytes 884744 | tf_op jit(solution)/shard_map/ppermute | solution.py:565
  32.1 6.3 %collective-permute-start.9 = (bf16[64,1024]{1,0:T(8,128)(2,1)S(1)}, bf16[64,1024]{1,0:T(8,128)(2,1)S(1)}, u32[]{:S(2)}, u32[]{:S(2)}) collective-permute-start(bf16[64,1024]{1,0:T(8,128)(2,1)S(1)} %collective-permute-done.4.refs_5_.refs_1_), channel_id=1, source_target_pairs={{0,2},{2,0},{1,3},{3,1},{4,6},{6,4},{5,7},{7,5},{8,10},{10,8},{9,1... | collective-permute-start | bytes 393224 | tf_op jit(solution)/shard_map/ppermute | solution.py:50
  33.9 6.9 %collective-permute-start.16 = (bf16[64,1024]{1,0:T(8,128)(2,1)S(1)}, bf16[64,1024]{1,0:T(8,128)(2,1)S(1)}, u32[]{:S(2)}, u32[]{:S(2)}) collective-permute-start(bf16[64,1024]{1,0:T(8,128)(2,1)S(1)} %collective-permute-done.13.refs_9_.refs_5_), channel_id=1, source_target_pairs={{0,2},{2,0},{1,3},{3,1},{4,6},{6,4},{5,7},{7,5},{8,10},{10,8},{9,1... | collective-permute-start | bytes 393224 | tf_op jit(solution)/shard_map/ppermute | solution.py:50
  36.1 8.0 %collective-permute-start.14 = (bf16[64,1024]{1,0:T(8,128)(2,1)S(1)}, bf16[64,1024]{1,0:T(8,128)(2,1)S(1)}, u32[]{:S(2)}, u32[]{:S(2)}) collective-permute-start(bf16[64,1024]{1,0:T(8,128)(2,1)S(1)} %collective-permute-done.4.refs_5_.refs_1_), channel_id=1, source_target_pairs={{0,1},{1,0},{2,3},{3,2},{4,5},{5,4},{6,7},{7,6},{8,9},{9,8},{10,11... | collective-permute-start | bytes 393224 | tf_op jit(solution)/shard_map/ppermute | solution.py:50
  41.3 13.3 %collective-permute-start.21 = (bf16[128,1536]{1,0:T(8,128)(2,1)S(1)}, bf16[128,1536]{1,0:T(8,128)(2,1)S(1)}, u32[]{:S(2)}, u32[]{:S(2)}) collective-permute-start(bf16[128,1536]{1,0:T(8,128)(2,1)S(1)} %get-tuple-element.73.refs_18_.refs_0_), channel_id=1, source_target_pairs={{0,8},{1,9},{2,10},{3,11},{16,24},{17,25},{18,26},{19,27}} | collective-permute-start | bytes 1179656 | tf_op jit(solution)/shard_map/ppermute | solution.py:565
  46.0 9.4 %collective-permute-start.25 = (bf16[96,1536]{1,0:T(8,128)(2,1)S(1)}, bf16[96,1536]{1,0:T(8,128)(2,1)S(1)}, u32[]{:S(2)}, u32[]{:S(2)}) collective-permute-start(bf16[96,1536]{1,0:T(8,128)(2,1)S(1)} %collective-permute-done.19.refs_14_.refs_2_), channel_id=1, source_target_pairs={{8,4},{9,5},{10,6},{11,7},{24,20},{25,21},{26,22},{27,23}} | collective-permute-start | bytes 884744 | tf_op jit(solution)/shard_map/ppermute | solution.py:145
  46.7 9.6 %collective-permute-start.26 = (bf16[96,1536]{1,0:T(8,128)(2,1)S(1)}, bf16[96,1536]{1,0:T(8,128)(2,1)S(1)}, u32[]{:S(2)}, u32[]{:S(2)}) collective-permute-start(bf16[96,1536]{1,0:T(8,128)(2,1)S(1)} %collective-permute-done.19.refs_14_.refs_2_), channel_id=1, source_target_pairs={{8,12},{9,13},{10,14},{11,15},{24,28},{25,29},{26,30},{27,31}} | collective-permute-start | bytes 884744 | tf_op jit(solution)/shard_map/ppermute | solution.py:145
  47.4 16.7 %collective-permute-start.24 = (bf16[160,1536]{1,0:T(8,128)(2,1)S(1)}, bf16[160,1536]{1,0:T(8,128)(2,1)S(1)}, u32[]{:S(2)}, u32[]{:S(2)}) collective-permute-start(bf16[160,1536]{1,0:T(8,128)(2,1)S(1)} %get-tuple-element.76.refs_15_.refs_0_), channel_id=1, source_target_pairs={{0,8},{1,9},{2,10},{3,11},{16,24},{17,25},{18,26},{19,27}} | collective-permute-start | bytes 1474568 | tf_op jit(solution)/shard_map/ppermute | solution.py:565
  53.0 19.3 %collective-permute-start.20 = (bf16[128,1536]{1,0:T(8,128)(2,1)S(1)}, bf16[128,1536]{1,0:T(8,128)(2,1)S(1)}, u32[]{:S(2)}, u32[]{:S(2)}) collective-permute-start(bf16[128,1536]{1,0:T(8,128)(2,1)S(1)} %get-tuple-element.77.refs_0_), channel_id=1, source_target_pairs={{0,8},{1,9},{2,10},{3,11},{16,24},{17,25},{18,26},{19,27}} | collective-permute-start | bytes 1179656 | tf_op jit(solution)/shard_map/ppermute | solution.py:565
  54.6 10.9 %collective-permute-start.22 = (bf16[128,1536]{1,0:T(8,128)(2,1)S(1)}, bf16[128,1536]{1,0:T(8,128)(2,1)S(1)}, u32[]{:S(2)}, u32[]{:S(2)}) collective-permute-start(bf16[128,1536]{1,0:T(8,128)(2,1)S(1)} %collective-permute-done.21.refs_8_.refs_2_), channel_id=1, source_target_pairs={{8,4},{9,5},{10,6},{11,7},{24,20},{25,21},{26,22},{27,23}} | collective-permute-start | bytes 1179656 | tf_op jit(solution)/shard_map/ppermute | solution.py:145
  55.3 12.9 %collective-permute-start.23 = (bf16[128,1536]{1,0:T(8,128)(2,1)S(1)}, bf16[128,1536]{1,0:T(8,128)(2,1)S(1)}, u32[]{:S(2)}, u32[]{:S(2)}) collective-permute-start(bf16[128,1536]{1,0:T(8,128)(2,1)S(1)} %collective-permute-done.21.refs_8_.refs_2_), channel_id=1, source_target_pairs={{8,12},{9,13},{10,14},{11,15},{24,28},{25,29},{26,30},{27,31}} | collective-permute-start | bytes 1179656 | tf_op jit(solution)/shard_map/ppermute | solution.py:145
  64.1 8.9 %collective-permute-start.29 = (bf16[160,1536]{1,0:T(8,128)(2,1)S(1)}, bf16[160,1536]{1,0:T(8,128)(2,1)S(1)}, u32[]{:S(2)}, u32[]{:S(2)}) collective-permute-start(bf16[160,1536]{1,0:T(8,128)(2,1)S(1)} %collective-permute-done.24.refs_8_.refs_2_), channel_id=1, source_target_pairs={{8,4},{9,5},{10,6},{11,7},{24,20},{25,21},{26,22},{27,23}} | collective-permute-start | bytes 1474568 | tf_op jit(solution)/shard_map/ppermute | solution.py:145
  64.8 8.9 %collective-permute-start.30 = (bf16[160,1536]{1,0:T(8,128)(2,1)S(1)}, bf16[160,1536]{1,0:T(8,128)(2,1)S(1)}, u32[]{:S(2)}, u32[]{:S(2)}) collective-permute-start(bf16[160,1536]{1,0:T(8,128)(2,1)S(1)} %collective-permute-done.24.refs_8_.refs_2_), channel_id=1, source_target_pairs={{8,12},{9,13},{10,14},{11,15},{24,28},{25,29},{26,30},{27,31}} | collective-permute-start | bytes 1474568 | tf_op jit(solution)/shard_map/ppermute | solution.py:145
  65.5 9.4 %collective-permute-start.31 = (bf16[32,1024]{1,0:T(8,128)(2,1)S(1)}, bf16[32,1024]{1,0:T(8,128)(2,1)S(1)}, u32[]{:S(2)}, u32[]{:S(2)}) collective-permute-start(bf16[32,1024]{1,0:T(8,128)(2,1)S(1)} %get-tuple-element.90), channel_id=1, source_target_pairs={{0,4},{4,8},{8,12},{1,5},{5,9},{9,13},{2,6},{6,10},{10,14},{3,7},{... | collective-permute-start | bytes 196616 | tf_op jit(solution)/shard_map/ppermute | solution.py:626
  68.2 8.5 %collective-permute-start.32 = (bf16[32,1024]{1,0:T(8,128)(2,1)S(1)}, bf16[32,1024]{1,0:T(8,128)(2,1)S(1)}, u32[]{:S(2)}, u32[]{:S(2)}) collective-permute-start(bf16[32,1024]{1,0:T(8,128)(2,1)S(1)} %get-tuple-element.91), channel_id=1, source_target_pairs={{4,0},{8,4},{12,8},{5,1},{9,5},{13,9},{6,2},{10,6},{14,10},{7,3},{... | collective-permute-start | bytes 196616 | tf_op jit(solution)/shard_map/ppermute | solution.py:626
  72.3 9.0 %collective-permute-start.27 = (bf16[128,1536]{1,0:T(8,128)(2,1)S(1)}, bf16[128,1536]{1,0:T(8,128)(2,1)S(1)}, u32[]{:S(2)}, u32[]{:S(2)}) collective-permute-start(bf16[128,1536]{1,0:T(8,128)(2,1)S(1)} %collective-permute-done.20.refs_8_.refs_2_), channel_id=1, source_target_pairs={{8,4},{9,5},{10,6},{11,7},{24,20},{25,21},{26,22},{27,23}} | collective-permute-start | bytes 1179656 | tf_op jit(solution)/shard_map/ppermute | solution.py:145
  73.0 8.3 %collective-permute-start.28 = (bf16[128,1536]{1,0:T(8,128)(2,1)S(1)}, bf16[128,1536]{1,0:T(8,128)(2,1)S(1)}, u32[]{:S(2)}, u32[]{:S(2)}) collective-permute-start(bf16[128,1536]{1,0:T(8,128)(2,1)S(1)} %collective-permute-done.20.refs_8_.refs_2_), channel_id=1, source_target_pairs={{8,12},{9,13},{10,14},{11,15},{24,28},{25,29},{26,30},{27,31}} | collective-permute-start | bytes 1179656 | tf_op jit(solution)/shard_map/ppermute | solution.py:145
  79.8 9.1 %collective-permute-start.39 = (bf16[128,1024]{1,0:T(8,128)(2,1)S(1)}, bf16[128,1024]{1,0:T(8,128)(2,1)S(1)}, u32[]{:S(2)}, u32[]{:S(2)}) collective-permute-start(bf16[128,1024]{1,0:T(8,128)(2,1)S(1)} %get-tuple-element.96.refs_7_), channel_id=1, source_target_pairs={{0,2},{2,0},{1,3},{3,1},{4,6},{6,4},{5,7},{7,5},{8,10},{10,8},{9,1... | collective-permute-start | bytes 786440 | tf_op jit(solution)/shard_map/ppermute | solution.py:50
  89.7 11.2 %collective-permute-start.40 = (bf16[32,1024]{1,0:T(8,128)(2,1)S(1)}, bf16[32,1024]{1,0:T(8,128)(2,1)S(1)}, u32[]{:S(2)}, u32[]{:S(2)}) collective-permute-start(bf16[32,1024]{1,0:T(8,128)(2,1)S(1)} %get-tuple-element.104), channel_id=1, source_target_pairs={{0,4},{4,8},{8,12},{12,0},{1,5},{5,9},{9,13},{13,1},{2,6},{6,10},{... | collective-permute-start | bytes 196616 | tf_op jit(solution)/shard_map/ppermute | solution.py:646
  96.1 6.8 %collective-permute-start.41 = (bf16[32,1024]{1,0:T(8,128)(2,1)S(1)}, bf16[32,1024]{1,0:T(8,128)(2,1)S(1)}, u32[]{:S(2)}, u32[]{:S(2)}) collective-permute-start(bf16[32,1024]{1,0:T(8,128)(2,1)S(1)} %get-tuple-element.105), channel_id=1, source_target_pairs={{0,8},{4,12},{8,0},{12,4},{1,9},{5,13},{9,1},{13,5},{2,10},{6,14},... | collective-permute-start | bytes 196616 | tf_op jit(solution)/shard_map/ppermute | solution.py:646
  (23 other events, 77.5 us)
